TPU v7x, 32 devices: a whole 2x2x4 slice. The times are simulated.
32 devices in a mesh: grp: 8 (over z, y), tp: 4 (over x, core).
Axes of the slice: x: 2, y: 2, z: 4, core: 2. Of those that a mesh axis runs over, the one named last changes fastest.
Arguments:
- tokens: bfloat16 [512, 4, 8192], P('grp', None, 'tp'), may hold values from -6 to 6
- adapter_id: int32 [512], P('grp'), may hold values from 0 to 63, as said below
- pool_slot: int32 [64], replicated, may hold values from 0 to 63, as said below
- lengths: int32 [512], P('grp'), may hold values from 1 to 64, as said below
- w_query: bfloat16 [8192, 8192], P(None, 'tp'), may hold values from -0.0625 to 0.0625
- w_key: bfloat16 [8192, 1024], P(None, 'tp'), may hold values from -0.0625 to 0.0625
- w_value: bfloat16 [8192, 1024], P(None, 'tp'), may hold values from -0.0625 to 0.0625
- pooled_down_weights: bfloat16 [64, 8192, 64], P('grp', 'tp'), may hold values from -0.0625 to 0.0625
- pool_up: bfloat16 [64, 64, 8192], P('grp', None, 'tp'), may hold values from -0.75 to 0.75
- cache_key: bfloat16 [512, 64, 1024], P('grp', None, 'tp')
- cache_value: bfloat16 [512, 64, 1024], P('grp', None, 'tp'), may hold values from -6 to 6
Outputs:
- attended: bfloat16 [512, 4, 8192], P('grp', None, 'tp')
Inputs may be any that keep to these rules, and one draw needn't show every extreme that they name: `adapter_id`: each aligned block of 64 rows (one group) uses adapters of exactly 8 owners (owner = pool_slot // 8), 8 rows each, and at most 2 distinct adapters of one owner, reached in every block; a single owner, the same for all blocks, serves 8 rows of every block. `pool_slot`: A permutation. `lengths`: each aligned block of 64 rows has a row of length 64.
All inputs are finite; a program needn't handle non-finite values.
Results may differ from a plain program's by a relative error of at most 0.012.
The roundings to bfloat16 on the way count: a program that leaves them out, or rounds other values in their place, can miss the bound.
Values may be sent and summed in bfloat16 or wider, within the bound.
No kernel may reach another device: no remote copies, remote signals or barrier semaphores. Data moves between devices by JAX's collectives and lax.ppermute only.
A program may use at most 128 MiB of HBM per device.

v0:
```python
import math

import jax
import jax.numpy as jnp
from jax import lax
from jax.sharding import PartitionSpec as P

HD = 128
CAP = 8


rope_base = 500000.0


def rotate(values, position):
    half_width = values.shape[-1] // 2
    inv_freq = jnp.exp(
        jnp.arange(half_width, dtype=jnp.float32) * (-2.0 * math.log(rope_base) / values.shape[-1])
    )
    angles = position.astype(jnp.float32)[:, :, None, None] * inv_freq
    cosine = jnp.cos(angles)
    sines = jnp.sin(angles)
    front_half = values[..., :half_width]
    back_half = values[..., half_width:]
    return jnp.concatenate(
        [front_half * cosine - back_half * sines, back_half * cosine + front_half * sines], axis=-1
    )


def attend(queries, key_new, value_new, cache_key, cache_value, lengths):
    score_scale = 1.0 / math.sqrt(queries.shape[-1])
    cached = (
        jnp.einsum("rskgd,rlkd->rskgl", queries, cache_key, preferred_element_type=jnp.float32)
        * score_scale
    )
    fresh_scores = (
        jnp.einsum("rskgd,rtkd->rskgt", queries, key_new, preferred_element_type=jnp.float32)
        * score_scale
    )
    live_mask = jnp.arange(cache_key.shape[1], dtype=jnp.int32)[None, :] < lengths[:, None]
    cached = jnp.where(live_mask[:, None, None, None, :], cached, -1e30)
    steps_here = key_new.shape[1]
    causal = (
        jnp.arange(steps_here, dtype=jnp.int32)[:, None]
        >= jnp.arange(steps_here, dtype=jnp.int32)[None, :]
    )
    fresh_scores = jnp.where(causal[None, :, None, None, :], fresh_scores, -1e30)
    row_max = jnp.maximum(jnp.max(cached, axis=-1), jnp.max(fresh_scores, axis=-1))
    cache_exp = jnp.exp(cached - row_max[..., None])
    fresh_exp = jnp.exp(fresh_scores - row_max[..., None])
    weight_sum = jnp.sum(cache_exp, axis=-1) + jnp.sum(fresh_exp, axis=-1)
    cache_weights = (cache_exp / weight_sum[..., None]).astype(jnp.bfloat16)
    fresh_weights = (fresh_exp / weight_sum[..., None]).astype(jnp.bfloat16)
    combined = jnp.einsum(
        "rskgl,rlkd->rskgd", cache_weights, cache_value, preferred_element_type=jnp.float32
    )
    combined = combined + jnp.einsum(
        "rskgt,rtkd->rskgd", fresh_weights, value_new, preferred_element_type=jnp.float32
    )
    return combined.astype(jnp.bfloat16)


def paired_adapter_term(
    tokens_per_block, second_selection, down_weight_pair, up_weight_pair, summing_axis
):
    count_of_blocks, block_length, unused_item = tokens_per_block.shape
    adapter_rank = down_weight_pair.shape[3]
    query_width = up_weight_pair.shape[3]
    selection_mask = jnp.stack([second_selection == 0, second_selection == 1], axis=2)
    partial_value_sum = jnp.einsum(
        "btd,bjdc->btjc", tokens_per_block, down_weight_pair, preferred_element_type=jnp.float32
    )
    partial_value_sum = jnp.sum(
        partial_value_sum * selection_mask[:, :, :, None].astype(jnp.float32), axis=2
    )
    adapter_middle = summing_axis(partial_value_sum).astype(jnp.bfloat16)
    spread_rows = (
        selection_mask[:, :, :, None].astype(jnp.bfloat16) * adapter_middle[:, :, None, :]
    ).reshape(count_of_blocks, block_length, 2 * adapter_rank)
    return jnp.einsum(
        "btk,bkq->btq",
        spread_rows,
        up_weight_pair.reshape(count_of_blocks, 2 * adapter_rank, query_width),
        preferred_element_type=jnp.float32,
    ).astype(jnp.bfloat16)


def body(
    tokens,
    adapter_id,
    pool_slot,
    lengths,
    w_query,
    w_key,
    w_value,
    pooled_down_weights,
    pool_up,
    cache_key,
    cache_value,
):
    group_count = lax.axis_size("grp")
    row_count, step_count, part_width = tokens.shape
    local_adapter_rows, unused_item, adapter_rank = pooled_down_weights.shape
    query_width = w_query.shape[1]
    kv_width = w_key.shape[1]
    kv_local = kv_width // HD
    q_local = query_width // HD
    group_size = q_local // kv_local
    count_of_tokens = row_count * step_count
    adapter_span = jnp.arange(pool_slot.shape[0], dtype=jnp.int32)
    pool_pos = jnp.sum(
        jnp.where(adapter_id[:, None] == adapter_span[None, :], pool_slot[None, :], 0), axis=1
    )
    owner_grp = pool_pos // local_adapter_rows
    local_slot = pool_pos % local_adapter_rows
    owner_span = jnp.arange(group_count, dtype=jnp.int32)
    member = owner_grp[:, None] == owner_span[None, :]
    first_slot = jnp.min(jnp.where(member, local_slot[:, None], local_adapter_rows), axis=0)
    first_slot = jnp.where(first_slot >= local_adapter_rows, 0, first_slot)
    second_slot = jnp.maximum(jnp.max(jnp.where(member, local_slot[:, None], -1), axis=0), 0)
    wanted = jnp.stack([first_slot, second_slot], axis=1)
    asked_slots = lax.all_to_all(wanted, "grp", split_axis=0, concat_axis=0, tiled=True)
    down_weight_panels = pooled_down_weights[asked_slots]
    up_weight_panels = pool_up[asked_slots]
    down_got = lax.all_to_all(down_weight_panels, "grp", split_axis=0, concat_axis=0, tiled=True)
    up_got = lax.all_to_all(up_weight_panels, "grp", split_axis=0, concat_axis=0, tiled=True)
    order = jnp.argsort(owner_grp, stable=True)
    sorted_owner = owner_grp[order]
    count_of_blocks = row_count // CAP
    block_owner = sorted_owner.reshape(count_of_blocks, CAP)[:, 0]
    second_row = (local_slot[order] != first_slot[sorted_owner]).astype(jnp.int32)
    second_tok = jnp.repeat(second_row, step_count).reshape(count_of_blocks, CAP * step_count)
    tokens_per_block = tokens[order].reshape(count_of_blocks, CAP * step_count, part_width)

    def mid_reduce(partial_value_sum):
        return lax.psum(partial_value_sum, "tp")

    sorted_output_rows = paired_adapter_term(
        tokens_per_block, second_tok, down_got[block_owner], up_got[block_owner], mid_reduce
    )
    adapter_output = (
        jnp.zeros((row_count, step_count * query_width), jnp.bfloat16)
        .at[order]
        .set(sorted_output_rows.reshape(row_count, step_count * query_width))
    )
    adapter_output = adapter_output.reshape(count_of_tokens, query_width)
    shard_piece = lax.all_gather(tokens, "tp", axis=2, tiled=True)
    piece_width = shard_piece.shape[2]
    piece_rows = shard_piece.reshape(count_of_tokens, piece_width)

    def add_term(matrix):
        return jnp.dot(piece_rows, matrix, preferred_element_type=jnp.float32)

    base_query_rows = add_term(w_query)
    key_base = add_term(w_key)
    value_base = add_term(w_value)
    base_query_rows = base_query_rows + adapter_output.astype(jnp.float32)
    position = lengths[:, None] + jnp.arange(step_count, dtype=jnp.int32)[None, :]
    queries = rotate(base_query_rows.reshape(row_count, step_count, q_local, HD), position)
    queries = queries.astype(jnp.bfloat16).reshape(row_count, step_count, kv_local, group_size, HD)
    key_new = rotate(key_base.reshape(row_count, step_count, kv_local, HD), position).astype(
        jnp.bfloat16
    )
    value_new = value_base.reshape(row_count, step_count, kv_local, HD).astype(jnp.bfloat16)
    cache_keys = cache_key.reshape(row_count, cache_key.shape[1], kv_local, HD)
    cache_values = cache_value.reshape(row_count, cache_value.shape[1], kv_local, HD)
    combined = attend(queries, key_new, value_new, cache_keys, cache_values, lengths)
    return combined.reshape(row_count, step_count, query_width)


def solution(mesh):
    in_specs = (
        P("grp", None, "tp"),
        P("grp"),
        P(),
        P("grp"),
        P(None, "tp"),
        P(None, "tp"),
        P(None, "tp"),
        P("grp", "tp", None),
        P("grp", None, "tp"),
        P("grp", None, "tp"),
        P("grp", None, "tp"),
    )
    out_specs = P("grp", None, "tp")
    return jax.shard_map(body, mesh=mesh, in_specs=in_specs, out_specs=out_specs, check_vma=False)
```

profile of v0, /device:TPU:9, one launch (start us, length us, event | category | flops | bytes accessed | tf_op | source)
XLA Modules:
  0.0 266.3 jit_solution(7008238251561353337)
XLA Ops:
  7.8 9.6 %all_to_all.22 = s32[8,1,2]{2,1,0:T(1,128)S(1)} all-to-all(s32[8,1,2]{2,1,0:T(1,128)S(1)} %copy.71), channel_id=1, replica_groups=mesh['grp'=8,'tp'=4] {'grp'}, dimensions={0} | all-to-all | bytes 128 | tf_op jit(solution)/shard_map/all_to_all | solution.py:122
  17.7 2.8 %gather_fusion.3 = bf16[16,2048,64]{1,2,0:T(8,128)(2,1)} fusion(bf16[8,2048,64]{1,2,0:T(8,128)(2,1)S(1)} %copy-done, s32[1024]{0:T(1024)S(1)} %pad_clamp_fusion.1), kind=kCustom, calls=%fused_computation.3 | custom fusion | bytes 8388672 | tf_op jit(solution)/shard_map/gather | solution.py:123
  20.5 5.8 %all-to-all-start.1 = ((bf16[8,2,2048,64]{2,3,1,0:T(8,128)(2,1)}), bf16[8,2,2048,64]{2,3,1,0:T(8,128)(2,1)}, u32[]{:S(2)}, u32[]{:S(2)}) async-start(bf16[8,2,2048,64]{2,3,1,0:T(8,128)(2,1)} %bitcast.106), calls=%async_computation.1 | async-start | bytes 8388608 | tf_op jit(solution)/shard_map/all_to_all | solution.py:125
  27.9 2.8 %gather_fusion.5 = bf16[16,64,2048]{2,1,0:T(8,128)(2,1)} fusion(bf16[8,64,2048]{2,1,0:T(8,128)(2,1)S(1)} %copy-done.3, s32[1024]{0:T(1024)S(1)} %pad_clamp_fusion.1), kind=kCustom, calls=%fused_computation.5 | custom fusion | bytes 8388672 | tf_op jit(solution)/shard_map/gather | solution.py:124
  30.7 87.0 %all-to-all-done.1 = bf16[8,2,2048,64]{2,3,1,0:T(8,128)(2,1)} async-done(((bf16[8,2,2048,64]{2,3,1,0:T(8,128)(2,1)}), bf16[8,2,2048,64]{2,3,1,0:T(8,128)(2,1)}, u32[]{:S(2)}, u32[]{:S(2)}) %all-to-all-start.1) | async-done | bytes 4194336 | tf_op jit(solution)/shard_map/all_to_all | solution.py:125
  117.8 5.6 %all-to-all-start.2 = ((bf16[8,2,64,2048]{3,2,1,0:T(8,128)(2,1)}), bf16[8,2,64,2048]{3,2,1,0:T(8,128)(2,1)}, u32[]{:S(2)}, u32[]{:S(2)}) async-start(bf16[8,2,64,2048]{3,2,1,0:T(8,128)(2,1)} %bitcast.109), calls=%async_computation.2 | async-start | bytes 8388608 | tf_op jit(solution)/shard_map/all_to_all | solution.py:126
  129.2 5.0 %broadcast_compare_fusion = (pred[64]{0:T(512)(128)(4,1)S(1)}, s32[64]{0:T(128)S(1)}) fusion(s32[64]{0:T(128)S(1)} %gather_fusion, s32[]{:T(128)} %bitcast.9, s32[]{:T(128)} %bitcast.8, s32[]{:T(128)} %bitcast.7, s32[]{:T(128)} %bitcast.6, s32[]{:T(128)} %bitcast.5, s32[]{:T(128)} %bitcast.4, s32[]{:T(128)} %bitcast.3, s32[]{:T(128)} %bitcast.2, ...), kind=kLoop, calls=%fused_computation.100 | loop fusion | flops 1280 | bytes 864 | tf_op jit(solution)/shard_map/eq | solution.py:69
  136.0 6.4 %copy.97 = bf16[256,8192]{1,0:T(8,128)(2,1)} copy(bf16[256,8192]{0,1:T(8,128)(2,1)} %bitcast.111) | data formatting | bytes 8388608 | tf_op jit(solution)/shard_map/dot_general | solution.py:152
  142.4 4.0 %reshape.292 = bf16[64,64,2,128]{3,2,1,0:T(2,128)(2,1)} reshape(bf16[64,64,256]{2,1,0:T(8,128)(2,1)} %param.20) | data formatting | bytes 4194304 | tf_op jit(solution)/shard_map/reshape | solution.py:165
  146.4 4.0 %reshape.293 = bf16[64,64,2,128]{3,2,1,0:T(2,128)(2,1)} reshape(bf16[64,64,256]{2,1,0:T(8,128)(2,1)} %param.21) | data formatting | bytes 4194304 | tf_op jit(solution)/shard_map/reshape | solution.py:166
  150.3 6.4 %copy.102 = bf16[256,8192]{1,0:T(8,128)(2,1)} copy(bf16[256,8192]{0,1:T(8,128)(2,1)} %bitcast.112) | data formatting | bytes 8388608 | tf_op jit(solution)/shard_map/dot_general | solution.py:152
  156.9 7.4 %copy.65 = bf16[64,4,8192]{2,1,0:T(4,128)(2,1)} copy(bf16[64,4,8192]{2,0,1:T(8,128)(2,1)} %all-gather.2.cloned.1.call-done) | data formatting | bytes 8388608 | tf_op jit(solution)/shard_map/all_gather | solution.py:147
  164.2 6.9 %reshape.286 = bf16[256,8192]{1,0:T(8,128)(2,1)} reshape(bf16[64,4,8192]{2,1,0:T(4,128)(2,1)} %copy.65) | data formatting | bytes 8388608 | tf_op jit(solution)/shard_map/reshape | solution.py:149
  171.1 4.9 %fusion.2 = f32[64,4,2,128]{3,0,2,1:T(8,128)S(1)} fusion(bf16[2,128,8192,1]{2,1,0,3:T(8,128)(2,1)} %bitcast.114, bf16[64,4,8192]{2,0,1:T(8,128)(2,1)} %all-gather.2.cloned.1.call-done), kind=kOutput, calls=%fused_computation.10 | convolution fusion | flops 1073741824 | bytes 8650752 | tf_op jit(solution)/shard_map/dot_general | solution.py:152
  178.3 5.0 %gather_fusion.4 = bf16[8,2,2048,64]{2,3,1,0:T(8,128)(2,1)} fusion(bf16[8,2,2048,64]{2,3,1,0:T(8,128)(2,1)} %all-to-all-done.1, s32[1024]{0:T(1024)S(1)} %pad_clamp_fusion), kind=kCustom, calls=%fused_computation.4 | custom fusion | bytes 8388640 | tf_op jit(solution)/shard_map/gather | solution.py:139
  183.3 4.3 %fusion.14 = f32[8,32,64]{2,1,0:T(8,128)S(1)} fusion(bf16[8,2,2048,64]{2,3,1,0:T(8,128)(2,1)} %gather_fusion.4, bf16[8,32,2048,1]{2,1,0,3:T(8,128)(2,1)S(1)} %reshape.410, f32[8,32,2]{1,2,0:T(2,128)S(1)} %copy.75), kind=kOutput, calls=%fused_computation.33 | convolution fusion | flops 134266880 | bytes 5310464 | tf_op jit(solution)/shard_map/btd,bjdc->btjc/dot_general | solution.py:70
  187.6 14.1 %psum.7 = bf16[8,32,64]{2,1,0:T(8,128)(2,1)S(1)} all-reduce(f32[8,32,64]{2,1,0:T(8,128)S(1)} %fusion.14), channel_id=1, replica_groups=mesh['grp'=8,'tp'=4] {'tp'}, use_global_device_ids=true, to_apply=%region_5.6 | all-reduce | flops 16384 | bytes 98304 | tf_op jit(solution)/shard_map/psum | solution.py:136
  202.1 12.7 %all-to-all-done.2 = bf16[8,2,64,2048]{3,2,1,0:T(8,128)(2,1)} async-done(((bf16[8,2,64,2048]{3,2,1,0:T(8,128)(2,1)}), bf16[8,2,64,2048]{3,2,1,0:T(8,128)(2,1)}, u32[]{:S(2)}, u32[]{:S(2)}) %all-to-all-start.2) | async-done | bytes 4194336 | tf_op jit(solution)/shard_map/all_to_all | solution.py:126
  214.8 4.9 %gather_fusion.6 = bf16[8,2,64,2048]{3,2,1,0:T(8,128)(2,1)} fusion(bf16[8,2,64,2048]{3,2,1,0:T(8,128)(2,1)} %all-to-all-done.2, s32[1024]{0:T(1024)S(1)} %pad_clamp_fusion), kind=kCustom, calls=%fused_computation.6 | custom fusion | bytes 8388640 | tf_op jit(solution)/shard_map/gather | solution.py:139
  219.8 2.9 %convolution_convert_fusion = bf16[8,32,2048]{2,1,0:T(8,128)(2,1)S(1)} fusion(bf16[8,32,128]{2,1,0:T(8,128)(2,1)S(1)} %mul.138, bf16[8,128,2048]{2,1,0:T(8,128)(2,1)} %bitcast.108), kind=kOutput, calls=%fused_computation.13 | convolution fusion | flops 134742016 | bytes 5308416 | tf_op jit(solution)/shard_map/btk,bkq->btq/dot_general | solution.py:80
  223.5 2.3 scatter_custom_fusion
  227.5 16.8 %fusion.10 = f32[32,8,16,128]{3,1,2,0:T(8,128)S(1)} fusion(f32[256,2048]{1,0:T(8,128)} %reshape.295, bf16[256,8192]{1,0:T(8,128)(2,1)} %reshape.286, bf16[8192,2048]{1,0:T(8,128)(2,1)} %param.15), kind=kOutput, calls=%fused_computation.27 | convolution fusion | flops 8590458880 | bytes 41943040 | tf_op jit(solution)/shard_map/dot_general | solution.py:152
  245.5 4.9 %fusion.45 = (f32[64,4,2,8]{3,1,2,0:T(4,128)S(1)}, f32[64,4,2,8,4]{3,4,1,2,0:T(4,128)S(1)}) fusion(bf16[64,4,2,128,1]{3,0,2,1,4:T(8,128)(2,1)S(1)} %maximum_bitcast_fusion, pred[4,4]{1,0:T(4,128)(4,1)S(1)} %iota_compare_fusion.3, bf16[64,4,2,8,64]{4,3,2,1,0:T(8,128)(2,1)S(1)} %get-tuple-element.12, bf16[64,4,2,8,64]{4,3,2,1,0:T(8,128)(2,1)S(1)} %get-tuple-element.11), kind=kOutput, calls=%fused_computation.105 | convolution fusion | flops 6336512 | bytes 1261584 | tf_op jit(solution)/shard_map/rskgd,rtkd->rskgt/dot_general | solution.py:37
  254.7 2.6 fusion.5
  (84 shorter events, 23.8 us)
Async XLA Ops:
  6.5 11.2 %copy-start = (bf16[8,2048,64]{1,2,0:T(8,128)(2,1)S(1)}, bf16[8,2048,64]{1,2,0:T(8,128)(2,1)}, u32[]{:S(2)}) copy-start(bf16[8,2048,64]{1,2,0:T(8,128)(2,1)} %param.18) | copy-start | bytes 6291460
  20.5 5.8 %copy-start.4 = (bf16[64,4,2048]{2,1,0:T(4,128)(2,1)S(1)}, bf16[64,4,2048]{2,1,0:T(4,128)(2,1)}, u32[]{:S(2)}) copy-start(bf16[64,4,2048]{2,1,0:T(4,128)(2,1)} %param.11) | copy-start | bytes 3145732
  20.5 97.2 %all-to-all-start.1 = ((bf16[8,2,2048,64]{2,3,1,0:T(8,128)(2,1)}), bf16[8,2,2048,64]{2,3,1,0:T(8,128)(2,1)}, u32[]{:S(2)}, u32[]{:S(2)}) async-start(bf16[8,2,2048,64]{2,3,1,0:T(8,128)(2,1)} %bitcast.106), calls=%async_computation.1 | async-start | bytes 8388608 | tf_op jit(solution)/shard_map/all_to_all | solution.py:125
  26.3 1.7 copy-start.3
  26.3 130.6 %all-gather.2.cloned.1.call-start = ((), (), s32[]{:S(2)}) async-start(), calls=%async_computation.3 | async-start | bytes 5242880 | tf_op jit(solution)/shard_map/all_gather | solution.py:147
  117.8 97.1 %all-to-all-start.2 = ((bf16[8,2,64,2048]{3,2,1,0:T(8,128)(2,1)}), bf16[8,2,64,2048]{3,2,1,0:T(8,128)(2,1)}, u32[]{:S(2)}, u32[]{:S(2)}) async-start(bf16[8,2,64,2048]{3,2,1,0:T(8,128)(2,1)} %bitcast.109), calls=%async_computation.2 | async-start | bytes 8388608 | tf_op jit(solution)/shard_map/all_to_all | solution.py:126
  127.0 8.3 %copy-start.8 = (s32[64]{0:T(128)S(1)}, s32[64]{0:T(128)}, u32[]{:S(2)}) copy-start(s32[64]{0:T(128)} %param.14) | copy-start | bytes 772
  171.1 5.2 %copy-start.5 = (bf16[64,4,8192]{2,0,1:T(8,128)(2,1)S(1)}, bf16[64,4,8192]{2,0,1:T(8,128)(2,1)}, u32[]{:S(2)}) copy-start(bf16[64,4,8192]{2,0,1:T(8,128)(2,1)} %all-gather.2.cloned.1.call-done) | copy-start | bytes 12582916
  171.1 5.9 %copy-start.6 = (bf16[256,8192]{1,0:T(8,128)(2,1)S(1)}, bf16[256,8192]{1,0:T(8,128)(2,1)}, u32[]{:S(2)}) copy-start(bf16[256,8192]{1,0:T(8,128)(2,1)} %copy.102) | copy-start | bytes 12582916
  245.5 4.9 %copy-start.2 = (bf16[64,64,2,128]{3,2,1,0:T(2,128)(2,1)S(1)}, bf16[64,64,2,128]{3,2,1,0:T(2,128)(2,1)}, u32[]{:S(2)}) copy-start(bf16[64,64,2,128]{3,2,1,0:T(2,128)(2,1)} %reshape.292) | copy-start | bytes 6291460
  253.1 1.6 copy-start.7
  257.3 2.2 copy-start.1
Sparse Core Ops, SparseCore 0:
  28.7 37.4 all-gather.1
where the time goes:
time: 271 us; the launch traced here: 266 us
  waiting for transfers between devices  99.8 us (37%)
  local copies, waits for them, and re-layouts  64.9 us (24%)
  matrix products  40 us (15%)
  blocking collectives  23.7 us (9%)
  between operations  13.7 us (5%)
  other arithmetic  12.8 us (5%)
  starting transfers between devices  11.4 us (4%)
    all_to_all x1, waiting for transfers between devices, body(): lax.all_to_all(down_weight_panels, 'grp', split_axis=0, concat_axis=0, ti...  87 us
    dot_general x3, matrix products, add_term(): return jnp.dot(piece_rows, matrix, preferred_element_type=jnp.float32)  22.9 us
    psum x1, blocking collectives, mid_reduce(): return lax.psum(partial_value_sum, 'tp')  14.1 us
    dot_general x2, local copies, waits for them, and re-layouts, add_term(): return jnp.dot(piece_rows, matrix, preferred_element_type=jnp.float32)  12.8 us
    all_to_all x1, waiting for transfers between devices, body(): lax.all_to_all(up_weight_panels, 'grp', split_axis=0, concat_axis=0, tile...  12.7 us
    all_to_all x1, blocking collectives, body(): lax.all_to_all(wanted, 'grp', split_axis=0, concat_axis=0, tiled=True)  9.62 us
    all_gather x1, local copies, waits for them, and re-layouts, body(): shard_piece = lax.all_gather(tokens, 'tp', axis=2, tiled=True)  7.37 us
    reshape x1, local copies, waits for them, and re-layouts, body(): piece_rows = shard_piece.reshape(count_of_tokens, piece_width)  6.91 us
  transfers between devices with their start and end apart: 3, of which 2 were waited for; matrix products, arithmetic and copies ran while one was open for 26% of the time, Pallas kernels for 0%

commit v1 on v0

v1 whole, which is shorter than its diff:
```python
import functools
import math

import jax
import jax.numpy as jnp
from jax import lax
from jax.experimental import pallas as pl
from jax.experimental.pallas import tpu as pltpu
from jax.sharding import PartitionSpec as P

HD = 128
CAP = 8
ROPE_BASE = 500000.0
NEG = -1e30
VMEM_LIMIT = 56 * 1024 * 1024
F32 = jnp.float32
BF16 = jnp.bfloat16


def params(**kw):
    return pltpu.CompilerParams(vmem_limit_bytes=VMEM_LIMIT, **kw)


VM = pl.BlockSpec(memory_space=pltpu.VMEM)
SM = pl.BlockSpec(memory_space=pltpu.SMEM)
ANY = pl.BlockSpec(memory_space=pl.ANY)


def dot(a, b):
    return jnp.dot(a, b, preferred_element_type=F32)


def dot_t(a, b):
    return lax.dot_general(a, b, (((1,), (1,)), ((), ())), preferred_element_type=F32)


def pack_kernel(adp_rows, n_grp, steps, ids_ref, lens_ref, slots_ref, tok_ref, *outs):
    sends = outs[:n_grp]
    sorted_ref, len_ref, row_ref = outs[n_grp : n_grp + 3]
    rows = ids_ref.shape[1]
    pool = slots_ref.shape[1]
    width = sorted_ref.shape[1]
    me = lax.axis_index("grp")
    sub = lax.broadcasted_iota(jnp.int32, (rows, rows), 0)
    lane = lax.broadcasted_iota(jnp.int32, (rows, rows), 1)
    eye = sub == lane

    def to_col(row):
        return jnp.sum(jnp.where(eye, row, 0.0), axis=1, keepdims=True)

    def to_row(col):
        return jnp.sum(jnp.where(eye, col, 0.0), axis=0, keepdims=True)

    ids_col = to_col(ids_ref[...].astype(F32))
    lens_col = to_col(lens_ref[...].astype(F32))
    span = lax.broadcasted_iota(jnp.int32, (rows, pool), 1).astype(F32)
    pos = jnp.sum(jnp.where(ids_col == span, slots_ref[...].astype(F32), 0.0), axis=1, keepdims=True)
    pos = pos.astype(jnp.int32)
    owner = lax.div(pos, adp_rows)
    slot = (pos - owner * adp_rows).astype(F32)
    key_col = lax.bitwise_xor(owner, me).astype(F32)
    key_row = to_row(key_col)
    same = key_row == key_col
    ahead = jnp.where((key_row < key_col) | (same & (lane < sub)), 1.0, 0.0)
    rank = jnp.sum(jnp.where(same & (lane < sub), 1.0, 0.0), axis=1, keepdims=True)
    dest_row = to_row(jnp.sum(ahead, axis=1, keepdims=True))
    perm = jnp.where(sub.astype(F32) == dest_row, 1.0, 0.0).astype(BF16)

    def wide(col):
        return jnp.broadcast_to(col, (rows, 128)).astype(BF16)

    len_ref[...] = dot(perm, wide(lens_col))
    row_ref[...] = dot(perm, wide(sub[:, :1].astype(F32))).astype(jnp.int32)
    dense = n_grp * CAP == rows
    if dense:
        perm_send = perm
    else:
        slot_row = to_row(key_col * CAP + rank)
        sub_s = lax.broadcasted_iota(jnp.int32, (n_grp * CAP, rows), 0).astype(F32)
        perm_send = jnp.where(sub_s == slot_row, 1.0, 0.0).astype(BF16)
    slot_s = dot(perm_send, wide(slot))
    for k in range(n_grp):
        tile = slot_s[k * CAP : (k + 1) * CAP]
        sends[k][steps * CAP * (width // 128) :, :] = jnp.concatenate([tile, tile], axis=0).astype(BF16)
    for j in range(0, width, 512):
        w = min(512, width - j)
        got = [dot(perm, tok_ref[s, :, j : j + w]) for s in range(steps)]
        for b in range(rows // CAP):
            blk = jnp.concatenate([t[b * CAP : (b + 1) * CAP] for t in got], axis=0).astype(BF16)
            sorted_ref[b * steps * CAP : (b + 1) * steps * CAP, j : j + w] = blk
        if not dense:
            got = [dot(perm_send, tok_ref[s, :, j : j + w]) for s in range(steps)]
        for k in range(n_grp):
            blk = jnp.concatenate([t[k * CAP : (k + 1) * CAP] for t in got], axis=0).astype(BF16)
            for c in range(w // 128):
                at = (j // 128 + c) * steps * CAP
                sends[k][at : at + steps * CAP, :] = blk[:, c * 128 : (c + 1) * 128]


def pack(n_grp, adp_rows, adapter_id, lengths, pool_slot, tok):
    steps, rows, width = tok.shape
    n_tok = steps * CAP
    out = (
        [jax.ShapeDtypeStruct((n_tok * (width // 128) + 16, 128), BF16)] * n_grp
        + [jax.ShapeDtypeStruct((rows * steps, width), BF16)]
        + [jax.ShapeDtypeStruct((rows, 128), F32), jax.ShapeDtypeStruct((rows, 128), jnp.int32)]
    )
    got = pl.pallas_call(
        functools.partial(pack_kernel, adp_rows, n_grp, steps),
        out_shape=out,
        in_specs=[VM] * 4,
        out_specs=[VM] * len(out),
        compiler_params=params(),
        name="pack",
    )(adapter_id[None, :], lengths[None, :], pool_slot[None, :], tok)
    return got[:n_grp], got[n_grp], got[n_grp + 1], got[n_grp + 2]


def qkv_kernel(n_x, has_acc, kblk, ids_ref, *refs):
    xs = refs[:n_x]
    w_refs = refs[n_x : n_x + 3]
    acc_refs = refs[n_x + 3 : n_x + 6] if has_acc else None
    outs = refs[-3:]
    p, kb = pl.program_id(0), pl.program_id(1)

    @pl.when((p == 0) & (kb == 0))
    def _():
        for i in range(3):
            outs[i][...] = acc_refs[i][...] if has_acc else jnp.zeros_like(outs[i])

    for j in range(n_x):

        @pl.when(p == j)
        def _():
            x = xs[j][:, pl.ds(pl.multiple_of(kb * kblk, kblk), kblk)]
            for w, o in zip(w_refs, outs):
                o[...] += dot(x, w[...])


def qkv(xs, shards, weights, acc):
    m, width = xs[0].shape
    kblk = min(512, width)
    nk = width // kblk
    n_x = len(xs)
    has_acc = acc is not None

    def whole(a):
        return pl.BlockSpec(a.shape, lambda p, kb, ids: (0,) * len(a.shape))

    def wspec(w):
        return pl.BlockSpec((kblk, w.shape[1]), lambda p, kb, ids: (ids[p] * nk + kb, 0))

    outs = [jax.ShapeDtypeStruct((m, w.shape[1]), F32) for w in weights]
    cols = sum(w.shape[1] for w in weights)
    extra = list(acc) if has_acc else []
    return pl.pallas_call(
        functools.partial(qkv_kernel, n_x, has_acc, kblk),
        out_shape=outs,
        grid_spec=pltpu.PrefetchScalarGridSpec(
            num_scalar_prefetch=1,
            grid=(n_x, nk),
            in_specs=[whole(x) for x in xs] + [wspec(w) for w in weights] + [whole(a) for a in extra],
            out_specs=[whole(o) for o in outs],
        ),
        compiler_params=params(),
        cost_estimate=pl.CostEstimate(
            flops=2 * n_x * m * width * cols, bytes_accessed=2 * n_x * width * cols, transcendentals=0
        ),
        name="qkv",
    )(shards, *xs, *weights, *extra)


def slot_mask(tile, n_tok, cols, rank):
    slots = jnp.concatenate([tile[:CAP].astype(F32)] * (n_tok // CAP), axis=0)
    slots = jnp.concatenate([slots] * (cols // 128), axis=1)
    col = lax.div(lax.broadcasted_iota(jnp.int32, (n_tok, cols), 1), rank).astype(F32)
    return slots == col


def mid_kernel(n_tok, rank, down_ref, *refs):
    ins, out_ref, x_ref = refs[:-2], refs[-2], refs[-1]
    width = x_ref.shape[1]
    cols = down_ref.shape[1]
    for k, r in enumerate(ins):
        for c in range(width // 128):
            x_ref[k * n_tok : (k + 1) * n_tok, c * 128 : (c + 1) * 128] = r[c * n_tok : (c + 1) * n_tok, :]
    half = len(ins) // 2
    prod = dot(x_ref[...], down_ref[...])
    lane = lax.broadcasted_iota(jnp.int32, (n_tok, 128), 1)
    folded = []
    for k, r in enumerate(ins):
        mask = slot_mask(r[n_tok * (width // 128) :, :], n_tok, cols, rank)
        part = jnp.where(mask, prod[k * n_tok : (k + 1) * n_tok], 0.0)
        tot = part[:, :128]
        for c in range(128, cols, 128):
            tot = tot + part[:, c : c + 128]
        folded.append(tot + pltpu.roll(tot, 64, 1))
    for k in range(half):
        out_ref[k * n_tok : (k + 1) * n_tok, :] = jnp.where(lane < 64, folded[k], folded[k + half])


def mid(recv, down, n_tok, rank):
    width = down.shape[0]
    n = len(recv)
    return pl.pallas_call(
        functools.partial(mid_kernel, n_tok, rank),
        out_shape=jax.ShapeDtypeStruct((n * n_tok // 2, 128), F32),
        in_specs=[VM] * (n + 1),
        out_specs=VM,
        scratch_shapes=[pltpu.VMEM((n * n_tok, width), BF16)],
        compiler_params=params(),
        name="mid",
    )(down, *recv)


def up_kernel(n_tok, rank, n_recv, up_ref, a_ref, b_ref, *refs):
    ins, outs = refs[:n_recv], refs[n_recv:]
    cols = up_ref.shape[0]
    half = n_recv // 2
    total = (a_ref[...] + b_ref[...]).astype(BF16).astype(F32)
    lane = lax.broadcasted_iota(jnp.int32, (n_tok, 128), 1)
    spread = []
    for k in range(n_recv):
        at = (k % half) * n_tok
        mine = total[at : at + n_tok]
        other = pltpu.roll(mine, 64, 1)
        both = jnp.where((lane < 64) == (k < half), mine, other)
        both = jnp.concatenate([both] * (cols // 128), axis=1)
        mask = slot_mask(ins[k][ins[k].shape[0] - 16 :, :], n_tok, cols, rank)
        spread.append(jnp.where(mask, both, 0.0).astype(BF16))
    rows = jnp.concatenate(spread, axis=0)
    for j in range(0, up_ref.shape[1], 512):
        got = dot(rows, up_ref[:, j : j + 512]).astype(BF16)
        for k in range(n_recv):
            outs[k][:, j : j + 512] = got[k * n_tok : (k + 1) * n_tok]


def up(a, b, recv, up_rows, n_tok, rank):
    n = len(recv)
    return pl.pallas_call(
        functools.partial(up_kernel, n_tok, rank, n),
        out_shape=[jax.ShapeDtypeStruct((n_tok, up_rows.shape[1]), BF16)] * n,
        in_specs=[VM] * (n + 3),
        out_specs=[VM] * n,
        compiler_params=params(),
        name="up",
    )(up_rows, a, b, *recv)


def make_attn_kernel(first, nb, steps, group, has_prev):
    def kernel(*refs):
        rows_ref, q_ref, k_ref, v_ref, cos_ref, sin_ref, len_ref, ck_ref, cv_ref = refs[:9]
        loras = refs[9 : 9 + nb]
        at = 9 + nb + (1 if has_prev else 0)
        out_ref, kbuf, vbuf, obuf, ksem, vsem, osem = refs[at:]
        n_tok = steps * CAP
        kv_local = k_ref.shape[1] // HD
        span = ck_ref.shape[1]
        scale = 1.0 / math.sqrt(HD)

        def copies(b, i):
            r = rows_ref[(first + b) * CAP + i, 0]
            return (
                pltpu.make_async_copy(ck_ref.at[r], kbuf.at[b, i], ksem.at[b]),
                pltpu.make_async_copy(cv_ref.at[r], vbuf.at[b, i], vsem.at[b]),
            )

        for b in range(nb):
            for i in range(CAP):
                for c in copies(b, i):
                    c.start()

        n_q = group * n_tok
        tok_q = lax.broadcasted_iota(jnp.int32, (n_tok, n_tok), 0)
        tok_k = lax.broadcasted_iota(jnp.int32, (n_tok, n_tok), 1)
        new_ok = (lax.rem(tok_q, CAP) == lax.rem(tok_k, CAP)) & (lax.div(tok_q, CAP) >= lax.div(tok_k, CAP))
        new_ok = jnp.concatenate([new_ok.astype(F32)] * group, axis=0) > 0.5
        col = lax.broadcasted_iota(jnp.int32, (CAP, CAP * span), 1)
        sub = lax.broadcasted_iota(jnp.int32, (CAP, CAP * span), 0)
        own = lax.div(col, span) == sub
        at_pos = lax.rem(col, span).astype(F32)
        turn = (
            (lax.rem(tok_q, steps) * CAP + lax.div(tok_q, steps)) == tok_k
        ).astype(F32).astype(BF16)

        for b in range(nb):
            for i in range(CAP):
                for c in copies(b, i):
                    c.wait()
            rows = slice(b * n_tok, (b + 1) * n_tok)
            cos, sin = cos_ref[rows], sin_ref[rows]
            lens = len_ref[b * CAP : (b + 1) * CAP][:, :1]
            ok = own & (at_pos < lens)
            bias = jnp.where(ok, 0.0, NEG)
            bias = jnp.concatenate([bias] * (n_q // CAP), axis=0)

            def rope(v):
                return v * cos + pltpu.roll(v, HD // 2, 1) * sin

            for h in range(kv_local):
                hs = slice(h * HD, (h + 1) * HD)
                heads = []
                for g in range(group):
                    cs = slice((h * group + g) * HD, (h * group + g + 1) * HD)
                    heads.append(rope(q_ref[rows, cs] + loras[b][:, cs].astype(F32)))
                q = jnp.concatenate(heads, axis=0).astype(BF16)
                kn = rope(k_ref[rows, hs]).astype(BF16)
                vn = v_ref[rows, hs].astype(BF16)
                kc = kbuf[b, :, :, hs].reshape(CAP * span, HD)
                vc = vbuf[b, :, :, hs].reshape(CAP * span, HD)
                s1 = dot_t(q, kc) * scale + bias
                s2 = jnp.where(new_ok, dot_t(q, kn) * scale, NEG)
                top = jnp.maximum(jnp.max(s1, axis=1, keepdims=True), jnp.max(s2, axis=1, keepdims=True))
                e1 = jnp.exp(s1 - top)
                e2 = jnp.exp(s2 - top)
                den = jnp.sum(e1, axis=1, keepdims=True) + jnp.sum(e2, axis=1, keepdims=True)
                inv = 1.0 / den
                o = dot((e1 * inv).astype(BF16), vc) + dot((e2 * inv).astype(BF16), vn)
                o = o.astype(BF16)
                for g in range(group):
                    cs = slice((h * group + g) * HD, (h * group + g + 1) * HD)
                    mixed = dot(turn, o[g * n_tok : (g + 1) * n_tok])
                    for i in range(CAP):
                        obuf[b, i, :, cs] = mixed[i * steps : (i + 1) * steps].astype(BF16)
            for i in range(CAP):
                r = rows_ref[(first + b) * CAP + i, 0]
                pltpu.make_async_copy(obuf.at[b, i], out_ref.at[r], osem).start()
        for b in range(nb):
            for i in range(CAP):
                r = rows_ref[(first + b) * CAP + i, 0]
                pltpu.make_async_copy(obuf.at[b, i], out_ref.at[r], osem).wait()

    return kernel


def attention(first, nb, steps, rows, q, k, v, cos, sin, lens, ck, cv, loras, prev):
    n_tok = steps * CAP
    group = q.shape[1] // k.shape[1]
    n_rows = ck.shape[0]
    out = jax.ShapeDtypeStruct((n_rows, steps, q.shape[1]), BF16)
    at = first // nb

    def part(a, n):
        return pl.BlockSpec((n, a.shape[1]), lambda i: (at, 0))

    ins = [rows, q, k, v, cos, sin, lens, ck, cv, *loras]
    specs = [SM] + [part(a, nb * n_tok) for a in (q, k, v, cos, sin)] + [part(lens, nb * CAP), ANY, ANY]
    specs += [VM] * nb
    alias = {}
    if prev is not None:
        alias = {len(ins): 0}
        ins.append(prev)
        specs.append(ANY)
    buf = (nb, CAP) + ck.shape[1:]
    return pl.pallas_call(
        make_attn_kernel(first, nb, steps, group, prev is not None),
        out_shape=out,
        grid=(1,),
        in_specs=specs,
        out_specs=ANY,
        scratch_shapes=[
            pltpu.VMEM(buf, BF16),
            pltpu.VMEM(buf, BF16),
            pltpu.VMEM((nb, CAP, steps, q.shape[1]), BF16),
            pltpu.SemaphoreType.DMA((nb,)),
            pltpu.SemaphoreType.DMA((nb,)),
            pltpu.SemaphoreType.DMA,
        ],
        input_output_aliases=alias,
        compiler_params=params(),
        name="attn",
    )(*ins)


def swap(x, axis, n, bit):
    return lax.ppermute(x, axis, [(i, i ^ bit) for i in range(n)])


def body(
    tokens,
    adapter_id,
    pool_slot,
    lengths,
    w_query,
    w_key,
    w_value,
    pooled_down_weights,
    pool_up,
    cache_key,
    cache_value,
):
    n_grp = lax.axis_size("grp")
    n_tp = lax.axis_size("tp")
    row_count, steps, width = tokens.shape
    adp_rows, _, rank = pooled_down_weights.shape
    n_tok = steps * CAP
    n_blocks = row_count // CAP

    tok = jnp.transpose(tokens, (1, 0, 2))
    sends, mine, lens, rows = pack(n_grp, adp_rows, adapter_id, lengths, pool_slot, tok)

    recv = [sends[0]] + [swap(sends[k], "grp", n_grp, k) for k in range(1, n_grp)]

    pieces = {0: mine}
    bit = n_tp // 2
    while bit:
        pieces.update({off ^ bit: swap(p, "tp", n_tp, bit) for off, p in list(pieces.items())})
        bit //= 2
    me = lax.axis_index("tp")
    weights = (w_query, w_key, w_value)
    early = [o for o in pieces if o < 2]
    late = [o for o in pieces if o >= 2]

    def shards(offs):
        return jnp.stack([lax.bitwise_xor(me, o) for o in offs]).astype(jnp.int32)

    acc = qkv([pieces[o] for o in early], shards(early), weights, None)
    q, k, v = qkv([pieces[o] for o in late], shards(late), weights, acc)

    half = HD // 2
    inv_freq = jnp.exp(jnp.arange(half, dtype=F32) * (-2.0 * math.log(ROPE_BASE) / HD))
    inv_freq = jnp.concatenate([inv_freq, inv_freq])
    position = lens.reshape(n_blocks, 1, CAP, 128) + jnp.arange(steps, dtype=F32)[None, :, None, None]
    angles = (position * inv_freq).reshape(row_count * steps, HD)
    sign = jnp.where(jnp.arange(HD) < half, -1.0, 1.0).astype(F32)
    cos, sin = jnp.cos(angles), jnp.sin(angles) * sign

    down = jnp.transpose(pooled_down_weights, (1, 0, 2)).reshape(width, adp_rows * rank)
    part = mid(recv, down, n_tok, rank)
    bit = 1
    while bit < n_tp // 2:
        part = part + swap(part, "tp", n_tp, bit)
        bit *= 2
    other = swap(part, "tp", n_tp, bit)
    up_rows = pool_up.reshape(adp_rows * rank, pool_up.shape[2])
    back = up(part, other, recv, up_rows, n_tok, rank)
    loras = [back[0]] + [swap(back[k], "grp", n_grp, k) for k in range(1, n_grp)]
    rows = rows[:, :1]
    if n_grp != n_blocks:
        group = lax.axis_index("grp")
        span = jnp.arange(pool_slot.shape[0], dtype=jnp.int32)
        pos = jnp.sum(jnp.where(adapter_id[:, None] == span[None, :], pool_slot[None, :], 0), axis=1)
        keys = lax.bitwise_xor(lax.div(pos, adp_rows), group)
        used = jnp.any(keys[:, None] == jnp.arange(n_grp)[None, :], axis=0)
        at = jnp.cumsum(used.astype(jnp.int32)) - 1
        pick = (at[None, :] == jnp.arange(n_blocks)[:, None]) & used[None, :]
        chosen = jnp.sum(jnp.where(pick, jnp.arange(n_grp)[None, :], 0), axis=1)
        stacked = jnp.stack(loras)
        loras = [stacked[chosen[b]] for b in range(n_blocks)]
    out = None
    chunk = n_blocks // 2
    for first in range(0, n_blocks, chunk):
        out = attention(
            first, chunk, steps, rows, q, k, v, cos, sin, lens, cache_key, cache_value, loras[first : first + chunk], out
        )
    return out


def solution(mesh):
    in_specs = (
        P("grp", None, "tp"),
        P("grp"),
        P(),
        P("grp"),
        P(None, "tp"),
        P(None, "tp"),
        P(None, "tp"),
        P("grp", "tp", None),
        P("grp", None, "tp"),
        P("grp", None, "tp"),
        P("grp", None, "tp"),
    )
    out_specs = P("grp", None, "tp")
    return jax.shard_map(body, mesh=mesh, in_specs=in_specs, out_specs=out_specs, check_vma=False)
```

time: 271 us -> 133 us (0.49)
  the two profiles are of different devices: /device:TPU:9 before, /device:TPU:0 now
where the time goes in v1:
time: 133 us; the launch traced here: 132 us
  Pallas kernels  59.7 us (45%)
  starting transfers between devices  35.1 us (26%)
  waiting for transfers between devices  25.1 us (19%)
  local copies, waits for them, and re-layouts  8.18 us (6%)
  other arithmetic  4.2 us (3%)
    ppermute x19, starting transfers between devices, swap(): return lax.ppermute(x, axis, [(i, i ^ bit) for i in range(n)])  35.1 us
    pallas_call x2, Pallas kernels, qkv(): pl.pallas_call(functools.partial(qkv_kernel, n_x, has_acc, kblk), out_sha...  30.3 us
    ppermute x19, waiting for transfers between devices, swap(): return lax.ppermute(x, axis, [(i, i ^ bit) for i in range(n)])  25.1 us
    pallas_call x2, Pallas kernels, attention(): pl.pallas_call(make_attn_kernel(first, nb, steps, group, prev is not None...  19 us
    unnamed x35, local copies, waits for them, and re-layouts  5.58 us
    pallas_call x1, Pallas kernels, up(): pl.pallas_call(functools.partial(up_kernel, n_tok, rank, n), out_shape=[j...  3.67 us
    pallas_call x1, Pallas kernels, mid(): pl.pallas_call(functools.partial(mid_kernel, n_tok, rank), out_shape=jax....  3.37 us
    pallas_call x1, Pallas kernels, pack(): pl.pallas_call(functools.partial(pack_kernel, adp_rows, n_grp, steps), ou...  3.35 us
  transfers between devices with their start and end apart: 19, of which 5 were waited for; matrix products, arithmetic and copies ran while one was open for 5% of the time, Pallas kernels for 35%

profile of v1, /device:TPU:0, one launch (start us, length us, event | category | flops | bytes accessed | tf_op | source)
XLA Modules:
  0.0 132.5 jit_solution(10394899765862265605)
XLA Ops:
  0.0 2.9 %copy.18 = bf16[64,4,2048]{2,0,1:T(8,128)(2,1)} copy(bf16[64,4,2048]{2,1,0:T(4,128)(2,1)} %param.11) | data formatting | bytes 2097152 | tf_op args[0]
  2.9 3.4 %pack.1 = (bf16[528,128]{1,0:T(8,128)(2,1)}, bf16[528,128]{1,0:T(8,128)(2,1)}, bf16[528,128]{1,0:T(8,128)(2,1)}, bf16[528,128]{1,0:T(8,128)(2,1)}, bf16[528,128]...) custom-call(s32[1,64]{1,0:T(1,128)} %bitcast.32, ...), custom_call_target="tpu_custom_call" | custom-call | tf_op jit(solution)/shard_map/pack/pallas_call | solution.py:108
  6.3 2.9 %collective-permute-start = (bf16[256,2048]{1,0:T(8,128)(2,1)}, bf16[256,2048]{1,0:T(8,128)(2,1)S(1)}, u32[]{:S(2)}, u32[]{:S(2)}) collective-permute-start(bf16[256,2048]{1,0:T(8,128)(2,1)} %get-tuple-element.31.refs_0_), channel_id=1, source_target_pairs={{0,2},{1,3},{2,0},{3,1},{4,6},{5,7},{6,4},{7,5},{8,10},{9,11},{10,... | collective-permute-start | bytes 3145736 | tf_op jit(solution)/shard_map/ppermute | solution.py:376
  10.7 1.6 %collective-permute-start.4 = (bf16[528,128]{1,0:T(8,128)(2,1)}, bf16[528,128]{1,0:T(8,128)(2,1)S(1)}, u32[]{:S(2)}, u32[]{:S(2)}) collective-permute-start(bf16[528,128]{1,0:T(8,128)(2,1)} %get-tuple-element.41), channel_id=1, source_target_pairs={{0,8},{4,12},{8,0},{12,4},{16,24},{20,28},{24,16},{28,20},{1,9},{5... | collective-permute-start | bytes 405512 | tf_op jit(solution)/shard_map/ppermute | solution.py:376
  12.7 2.7 %collective-permute-done.3.refs_1_ = bf16[528,128]{1,0:T(8,128)(2,1)S(1)} collective-permute-done((bf16[528,128]{1,0:T(8,128)(2,1)}, bf16[528,128]{1,0:T(8,128)(2,1)S(1)}, u32[]{:S(2)}, u32[]{:S(2)}) %collective-permute-start.3) | collective-permute-done | bytes 135200 | tf_op jit(solution)/shard_map/ppermute | solution.py:376
  15.4 2.6 %collective-permute-start.6 = (bf16[528,128]{1,0:T(8,128)(2,1)}, bf16[528,128]{1,0:T(8,128)(2,1)}, u32[]{:S(2)}, u32[]{:S(2)}) collective-permute-start(bf16[528,128]{1,0:T(8,128)(2,1)} %get-tuple-element.43), channel_id=1, source_target_pairs={{0,16},{4,20},{8,24},{12,28},{16,0},{20,4},{24,8},{28,12},{1,17},{... | collective-permute-start | bytes 405512 | tf_op jit(solution)/shard_map/ppermute | solution.py:376
  18.0 14.6 %collective-permute-done.refs_0_ = bf16[256,2048]{1,0:T(8,128)(2,1)S(1)} collective-permute-done((bf16[256,2048]{1,0:T(8,128)(2,1)}, bf16[256,2048]{1,0:T(8,128)(2,1)S(1)}, u32[]{:S(2)}, u32[]{:S(2)}) %collective-permute-start) | collective-permute-done | bytes 1048608 | tf_op jit(solution)/shard_map/ppermute | solution.py:376
  32.6 3.9 %collective-permute-start.7 = (bf16[528,128]{1,0:T(8,128)(2,1)}, bf16[528,128]{1,0:T(8,128)(2,1)}, u32[]{:S(2)}, u32[]{:S(2)}) collective-permute-start(bf16[528,128]{1,0:T(8,128)(2,1)} %get-tuple-element.44), channel_id=1, source_target_pairs={{0,20},{4,16},{8,28},{12,24},{16,4},{20,0},{24,12},{28,8},{1,21},{... | collective-permute-start | bytes 405512 | tf_op jit(solution)/shard_map/ppermute | solution.py:376
  37.8 2.4 %collective-permute-start.9 = (bf16[528,128]{1,0:T(8,128)(2,1)}, bf16[528,128]{1,0:T(8,128)(2,1)}, u32[]{:S(2)}, u32[]{:S(2)}) collective-permute-start(bf16[528,128]{1,0:T(8,128)(2,1)} %get-tuple-element.46), channel_id=1, source_target_pairs={{0,28},{4,24},{8,20},{12,16},{16,12},{20,8},{24,4},{28,0},{1,29},{... | collective-permute-start | bytes 405512 | tf_op jit(solution)/shard_map/ppermute | solution.py:376
  40.3 2.5 %copy.16.down_ref = bf16[2048,512]{1,0:T(8,128)(2,1)} copy(bf16[2048,512]{0,1:T(8,128)(2,1)S(1)} %bitcast.27) | data formatting | bytes 4194304 | tf_op jit(solution)/shard_map/reshape | solution.py:428
  43.0 2.0 %fusion.3 = (f32[256,128]{1,0:T(8,128)}, f32[256,128]{1,0:T(8,128)}) fusion(f32[128]{0:T(128)S(1)} %get-tuple-element.57, f32[128]{0:T(128)S(1)} %get-tuple-element.58, f32[256]{0:T(256)S(1)} %add.29, f32[8,8,128]{2,1,0:T(8,128)} %bitcast.29), kind=kLoop, calls=%fused_computation.5 | loop fusion | flops 98304 | bytes 296960 | tf_op jit(solution)/shard_map/mul | solution.py:426
  45.0 5.0 %collective-permute-done.7.refs_5_ = bf16[528,128]{1,0:T(8,128)(2,1)} collective-permute-done((bf16[528,128]{1,0:T(8,128)(2,1)}, bf16[528,128]{1,0:T(8,128)(2,1)}, u32[]{:S(2)}, u32[]{:S(2)}) %collective-permute-start.7) | collective-permute-done | bytes 135200 | tf_op jit(solution)/shard_map/ppermute | solution.py:376
  49.9 3.4 %mid.1 = f32[128,128]{1,0:T(8,128)} custom-call(bf16[2048,512]{1,0:T(8,128)(2,1)} %copy.16.down_ref, bf16[528,128]{1,0:T(8,128)(2,1)} %get-tuple-element.39.refs_0_, bf16[528,128]{1,0:T(8,128)(2,1)} %copy-done.2, bf16[528,128]{1,0:T(8,128)(2,1)} %copy-done.3, bf16[528,128]{1,0:T(8,128)(2,1)} %copy-done.4, bf16[528,128]{1,0:T(8,128)(2,1)} %collective-permute-done.6.refs_4_, ...), custom_call_target="tpu_custom_call" | custom-call | tf_op jit(solution)/shard_map/mid/pallas_call | solution.py:205
  55.6 1.7 %collective-permute-start.11 = (f32[128,128]{1,0:T(8,128)S(1)}, f32[128,128]{1,0:T(8,128)S(1)}, u32[]{:S(2)}, u32[]{:S(2)}) collective-permute-start(f32[128,128]{1,0:T(8,128)S(1)} %add.32.a_ref), channel_id=1, source_target_pairs={{0,2},{1,3},{2,0},{3,1},{4,6},{5,7},{6,4},{7,5},{8,10},{9,11},{10,... | collective-permute-start | bytes 196616 | tf_op jit(solution)/shard_map/ppermute | solution.py:376
  58.0 1.9 %collective-permute-done.11.b_ref = f32[128,128]{1,0:T(8,128)S(1)} collective-permute-done((f32[128,128]{1,0:T(8,128)S(1)}, f32[128,128]{1,0:T(8,128)S(1)}, u32[]{:S(2)}, u32[]{:S(2)}) %collective-permute-start.11) | collective-permute-done | bytes 65568 | tf_op jit(solution)/shard_map/ppermute | solution.py:376
  60.6 3.7 %up.1 = (bf16[32,2048]{1,0:T(8,128)(2,1)}, bf16[32,2048]{1,0:T(8,128)(2,1)}, bf16[32,2048]{1,0:T(8,128)(2,1)}, bf16[32,2048]{1,0:T(8,128)(2,1)}, bf16[32,2048]{1...) custom-call(bf16[512,2048]{1,0:T(8,128)(2,1)} %bitcast.28, ...), custom_call_target="tpu_custom_call" | custom-call | tf_op jit(solution)/shard_map/up/pallas_call | solution.py:240
  64.2 1.7 %collective-permute-start.16 = (bf16[32,2048]{1,0:T(8,128)(2,1)}, bf16[32,2048]{1,0:T(8,128)(2,1)S(1)}, u32[]{:S(2)}, u32[]{:S(2)}) collective-permute-start(bf16[32,2048]{1,0:T(8,128)(2,1)} %get-tuple-element.52), channel_id=1, source_target_pairs={{0,4},{4,0},{8,12},{12,8},{16,20},{20,16},{24,28},{28,24},{1,5},{5... | collective-permute-start | bytes 393224 | tf_op jit(solution)/shard_map/ppermute | solution.py:376
  65.9 5.9 %collective-permute-start.17 = (bf16[32,2048]{1,0:T(8,128)(2,1)}, bf16[32,2048]{1,0:T(8,128)(2,1)S(1)}, u32[]{:S(2)}, u32[]{:S(2)}) collective-permute-start(bf16[32,2048]{1,0:T(8,128)(2,1)} %get-tuple-element.53), channel_id=1, source_target_pairs={{0,8},{4,12},{8,0},{12,4},{16,24},{20,28},{24,16},{28,20},{1,9},{5... | collective-permute-start | bytes 393224 | tf_op jit(solution)/shard_map/ppermute | solution.py:376
  72.0 4.0 %collective-permute-start.12 = (bf16[32,2048]{1,0:T(8,128)(2,1)}, bf16[32,2048]{1,0:T(8,128)(2,1)S(1)}, u32[]{:S(2)}, u32[]{:S(2)}) collective-permute-start(bf16[32,2048]{1,0:T(8,128)(2,1)} %get-tuple-element.47), channel_id=1, source_target_pairs={{0,16},{4,20},{8,24},{12,28},{16,0},{20,4},{24,8},{28,12},{1,17},{... | collective-permute-start | bytes 393224 | tf_op jit(solution)/shard_map/ppermute | solution.py:376
  75.9 14.8 %qkv.2 = (f32[256,2048]{1,0:T(8,128)}, f32[256,256]{1,0:T(8,128)}, f32[256,256]{1,0:T(8,128)}) custom-call(s32[2]{0:T(128)} %pad_add_fusion.1.ids_ref, bf16[256,2048]{1,0:T(8,128)(2,1)} %get-tuple-element.31.refs_0_, bf16[256,2048]{1,0:T(8,128)(2,1)} %collective-permute-done.2.refs_1_, bf16[8192,2048]{1,0:T(8,128)(2,1)} %refs_2_.3, ...), custom_call_target="tpu_custom_call" | custom-call | flops 5368709120 | bytes 20971520 | tf_op jit(solution)/shard_map/qkv/pallas_call | solution.py:156
  91.9 2.3 %collective-permute-start.14 = (bf16[32,2048]{1,0:T(8,128)(2,1)S(1)}, bf16[32,2048]{1,0:T(8,128)(2,1)S(1)}, u32[]{:S(2)}, u32[]{:S(2)}) collective-permute-start(bf16[32,2048]{1,0:T(8,128)(2,1)S(1)} %copy-done.15), channel_id=1, source_target_pairs={{0,24},{4,28},{8,16},{12,20},{16,8},{20,12},{24,0},{28,4},{1,25},{... | collective-permute-start | bytes 393224 | tf_op jit(solution)/shard_map/ppermute | solution.py:376
  95.7 15.5 %qkv.3 = (f32[256,2048]{1,0:T(8,128)}, f32[256,256]{1,0:T(8,128)}, f32[256,256]{1,0:T(8,128)}) custom-call(s32[2]{0:T(128)} %pad_add_fusion.ids_ref, bf16[256,2048]{1,0:T(8,128)(2,1)} %copy-done.1, bf16[256,2048]{1,0:T(8,128)(2,1)} %collective-permute-done.1.refs_1_, bf16[8192,2048]{1,0:T(8,128)(2,1)} %refs_2_.3, bf16[8192,256]{1,0:T(8,128)(2,1)} %refs_3_.3, ...), custom_call_target="tpu_custom_call" | custom-call | flops 5368709120 | bytes 20971520 | tf_op jit(solution)/shard_map/qkv/pallas_call | solution.py:156
  111.9 9.5 %attn.2.refs_13_ = bf16[64,4,2048]{2,1,0:T(4,128)(2,1)} custom-call(s32[64,1]{1,0:T(8,128)} %bitcast.30, f32[256,2048]{1,0:T(8,128)} %get-tuple-element.35.refs_1_, f32[256,256]{1,0:T(8,128)} %get-tuple-element.36.refs_2_, f32[256,256]{1,0:T(8,128)} %get-tuple-element.37.refs_3_, f32[256,128]{1,0:T(8,128)} %get-tuple-element.56.refs_4_, ...), custom_call_target="tpu_custom_call" | custom-call | tf_op jit(solution)/shard_map/attn/pallas_call | solution.py:355
  122.8 9.5 %attn.3 = bf16[64,4,2048]{2,1,0:T(4,128)(2,1)} custom-call(s32[64,1]{1,0:T(8,128)} %bitcast.31, f32[256,2048]{1,0:T(8,128)} %get-tuple-element.35.refs_1_, f32[256,256]{1,0:T(8,128)} %get-tuple-element.36.refs_2_, f32[256,256]{1,0:T(8,128)} %get-tuple-element.37.refs_3_, f32[256,128]{1,0:T(8,128)} %get-tuple-element.56.refs_4_, ...), custom_call_target="tpu_custom_call", output_to_operand_aliasing={{}: (13, {})} | custom-call | tf_op jit(solution)/shard_map/attn/pallas_call | solution.py:355
  (65 shorter events, 11.9 us)
Async XLA Ops:
  0.0 40.3 %copy-start = (bf16[8,2048,64]{1,2,0:T(8,128)(2,1)S(1)}, bf16[8,2048,64]{1,2,0:T(8,128)(2,1)}, u32[]{:S(2)}) copy-start(bf16[8,2048,64]{1,2,0:T(8,128)(2,1)} %param.18) | copy-start | bytes 6291460
  6.3 26.3 %collective-permute-start = (bf16[256,2048]{1,0:T(8,128)(2,1)}, bf16[256,2048]{1,0:T(8,128)(2,1)S(1)}, u32[]{:S(2)}, u32[]{:S(2)}) collective-permute-start(bf16[256,2048]{1,0:T(8,128)(2,1)} %get-tuple-element.31.refs_0_), channel_id=1, source_target_pairs={{0,2},{1,3},{2,0},{3,1},{4,6},{5,7},{6,4},{7,5},{8,10},{9,11},{10,... | collective-permute-start | bytes 3145736 | tf_op jit(solution)/shard_map/ppermute | solution.py:376
  9.2 62.7 %collective-permute-start.2 = (bf16[256,2048]{1,0:T(8,128)(2,1)}, bf16[256,2048]{1,0:T(8,128)(2,1)}, u32[]{:S(2)}, u32[]{:S(2)}) collective-permute-start(bf16[256,2048]{1,0:T(8,128)(2,1)} %get-tuple-element.31.refs_0_), channel_id=1, source_target_pairs={{0,1},{1,0},{2,3},{3,2},{4,5},{5,4},{6,7},{7,6},{8,9},{9,8},{10,11... | collective-permute-start | bytes 3145736 | tf_op jit(solution)/shard_map/ppermute | solution.py:376
  9.2 6.2 %collective-permute-start.3 = (bf16[528,128]{1,0:T(8,128)(2,1)}, bf16[528,128]{1,0:T(8,128)(2,1)S(1)}, u32[]{:S(2)}, u32[]{:S(2)}) collective-permute-start(bf16[528,128]{1,0:T(8,128)(2,1)} %get-tuple-element.40), channel_id=1, source_target_pairs={{0,4},{4,0},{8,12},{12,8},{16,20},{20,16},{24,28},{28,24},{1,5},{5... | collective-permute-start | bytes 405512 | tf_op jit(solution)/shard_map/ppermute | solution.py:376
  10.7 21.9 %collective-permute-start.4 = (bf16[528,128]{1,0:T(8,128)(2,1)}, bf16[528,128]{1,0:T(8,128)(2,1)S(1)}, u32[]{:S(2)}, u32[]{:S(2)}) collective-permute-start(bf16[528,128]{1,0:T(8,128)(2,1)} %get-tuple-element.41), channel_id=1, source_target_pairs={{0,8},{4,12},{8,0},{12,4},{16,24},{20,28},{24,16},{28,20},{1,9},{5... | collective-permute-start | bytes 405512 | tf_op jit(solution)/shard_map/ppermute | solution.py:376
  12.3 24.1 %collective-permute-start.5 = (bf16[528,128]{1,0:T(8,128)(2,1)}, bf16[528,128]{1,0:T(8,128)(2,1)S(1)}, u32[]{:S(2)}, u32[]{:S(2)}) collective-permute-start(bf16[528,128]{1,0:T(8,128)(2,1)} %get-tuple-element.42), channel_id=1, source_target_pairs={{0,12},{4,8},{8,4},{12,0},{16,28},{20,24},{24,20},{28,16},{1,13},{... | collective-permute-start | bytes 405512 | tf_op jit(solution)/shard_map/ppermute | solution.py:376
  15.4 27.3 %copy-start.2 = (bf16[528,128]{1,0:T(8,128)(2,1)}, bf16[528,128]{1,0:T(8,128)(2,1)S(1)}, u32[]{:S(2)}) copy-start(bf16[528,128]{1,0:T(8,128)(2,1)S(1)} %collective-permute-done.3.refs_1_) | copy-start | bytes 405508
  15.4 22.4 %collective-permute-start.6 = (bf16[528,128]{1,0:T(8,128)(2,1)}, bf16[528,128]{1,0:T(8,128)(2,1)}, u32[]{:S(2)}, u32[]{:S(2)}) collective-permute-start(bf16[528,128]{1,0:T(8,128)(2,1)} %get-tuple-element.43), channel_id=1, source_target_pairs={{0,16},{4,20},{8,24},{12,28},{16,0},{20,4},{24,8},{28,12},{1,17},{... | collective-permute-start | bytes 405512 | tf_op jit(solution)/shard_map/ppermute | solution.py:376
  32.6 61.6 %collective-permute-start.1 = (bf16[256,2048]{1,0:T(8,128)(2,1)S(1)}, bf16[256,2048]{1,0:T(8,128)(2,1)}, u32[]{:S(2)}, u32[]{:S(2)}) collective-permute-start(bf16[256,2048]{1,0:T(8,128)(2,1)S(1)} %collective-permute-done.refs_0_), channel_id=1, source_target_pairs={{0,1},{1,0},{2,3},{3,2},{4,5},{5,4},{6,7},{7,6},{8,9},{9,8},{10,11... | collective-permute-start | bytes 3145736 | tf_op jit(solution)/shard_map/ppermute | solution.py:376
  32.6 17.3 %collective-permute-start.7 = (bf16[528,128]{1,0:T(8,128)(2,1)}, bf16[528,128]{1,0:T(8,128)(2,1)}, u32[]{:S(2)}, u32[]{:S(2)}) collective-permute-start(bf16[528,128]{1,0:T(8,128)(2,1)} %get-tuple-element.44), channel_id=1, source_target_pairs={{0,20},{4,16},{8,28},{12,24},{16,4},{20,0},{24,12},{28,8},{1,21},{... | collective-permute-start | bytes 405512 | tf_op jit(solution)/shard_map/ppermute | solution.py:376
  36.5 13.5 %collective-permute-start.8 = (bf16[528,128]{1,0:T(8,128)(2,1)}, bf16[528,128]{1,0:T(8,128)(2,1)}, u32[]{:S(2)}, u32[]{:S(2)}) collective-permute-start(bf16[528,128]{1,0:T(8,128)(2,1)} %get-tuple-element.45), channel_id=1, source_target_pairs={{0,24},{4,28},{8,16},{12,20},{16,8},{20,12},{24,0},{28,4},{1,25},{... | collective-permute-start | bytes 405512 | tf_op jit(solution)/shard_map/ppermute | solution.py:376
  37.8 12.1 %collective-permute-start.9 = (bf16[528,128]{1,0:T(8,128)(2,1)}, bf16[528,128]{1,0:T(8,128)(2,1)}, u32[]{:S(2)}, u32[]{:S(2)}) collective-permute-start(bf16[528,128]{1,0:T(8,128)(2,1)} %get-tuple-element.46), channel_id=1, source_target_pairs={{0,28},{4,24},{8,20},{12,16},{16,12},{20,8},{24,4},{28,0},{1,29},{... | collective-permute-start | bytes 405512 | tf_op jit(solution)/shard_map/ppermute | solution.py:376
  53.3 1.5 %collective-permute-start.10 = (f32[128,128]{1,0:T(8,128)}, f32[128,128]{1,0:T(8,128)S(1)}, u32[]{:S(2)}, u32[]{:S(2)}) collective-permute-start(f32[128,128]{1,0:T(8,128)} %mid.1), channel_id=1, source_target_pairs={{0,1},{1,0},{2,3},{3,2},{4,5},{5,4},{6,7},{7,6},{8,9},{9,8},{10,11... | collective-permute-start | bytes 196616 | tf_op jit(solution)/shard_map/ppermute | solution.py:376
  55.6 4.3 %collective-permute-start.11 = (f32[128,128]{1,0:T(8,128)S(1)}, f32[128,128]{1,0:T(8,128)S(1)}, u32[]{:S(2)}, u32[]{:S(2)}) collective-permute-start(f32[128,128]{1,0:T(8,128)S(1)} %add.32.a_ref), channel_id=1, source_target_pairs={{0,2},{1,3},{2,0},{3,1},{4,6},{5,7},{6,4},{7,5},{8,10},{9,11},{10,... | collective-permute-start | bytes 196616 | tf_op jit(solution)/shard_map/ppermute | solution.py:376
  64.2 26.5 %collective-permute-start.16 = (bf16[32,2048]{1,0:T(8,128)(2,1)}, bf16[32,2048]{1,0:T(8,128)(2,1)S(1)}, u32[]{:S(2)}, u32[]{:S(2)}) collective-permute-start(bf16[32,2048]{1,0:T(8,128)(2,1)} %get-tuple-element.52), channel_id=1, source_target_pairs={{0,4},{4,0},{8,12},{12,8},{16,20},{20,16},{24,28},{28,24},{1,5},{5... | collective-permute-start | bytes 393224 | tf_op jit(solution)/shard_map/ppermute | solution.py:376
  65.9 26.0 %collective-permute-start.17 = (bf16[32,2048]{1,0:T(8,128)(2,1)}, bf16[32,2048]{1,0:T(8,128)(2,1)S(1)}, u32[]{:S(2)}, u32[]{:S(2)}) collective-permute-start(bf16[32,2048]{1,0:T(8,128)(2,1)} %get-tuple-element.53), channel_id=1, source_target_pairs={{0,8},{4,12},{8,0},{12,4},{16,24},{20,28},{24,16},{28,20},{1,9},{5... | collective-permute-start | bytes 393224 | tf_op jit(solution)/shard_map/ppermute | solution.py:376
  71.8 39.4 %collective-permute-start.18 = (bf16[32,2048]{1,0:T(8,128)(2,1)}, bf16[32,2048]{1,0:T(8,128)(2,1)S(1)}, u32[]{:S(2)}, u32[]{:S(2)}) collective-permute-start(bf16[32,2048]{1,0:T(8,128)(2,1)} %get-tuple-element.54), channel_id=1, source_target_pairs={{0,12},{4,8},{8,4},{12,0},{16,28},{20,24},{24,20},{28,16},{1,13},{... | collective-permute-start | bytes 393224 | tf_op jit(solution)/shard_map/ppermute | solution.py:376
  71.9 20.0 %copy-start.15 = (bf16[32,2048]{1,0:T(8,128)(2,1)S(1)}, bf16[32,2048]{1,0:T(8,128)(2,1)}, u32[]{:S(2)}) copy-start(bf16[32,2048]{1,0:T(8,128)(2,1)} %get-tuple-element.49) | copy-start | bytes 393220
  71.9 22.2 %copy-start.14 = (bf16[32,2048]{1,0:T(8,128)(2,1)S(1)}, bf16[32,2048]{1,0:T(8,128)(2,1)}, u32[]{:S(2)}) copy-start(bf16[32,2048]{1,0:T(8,128)(2,1)} %get-tuple-element.50) | copy-start | bytes 393220
  72.0 49.5 %collective-permute-start.12 = (bf16[32,2048]{1,0:T(8,128)(2,1)}, bf16[32,2048]{1,0:T(8,128)(2,1)S(1)}, u32[]{:S(2)}, u32[]{:S(2)}) collective-permute-start(bf16[32,2048]{1,0:T(8,128)(2,1)} %get-tuple-element.47), channel_id=1, source_target_pairs={{0,16},{4,20},{8,24},{12,28},{16,0},{20,4},{24,8},{28,12},{1,17},{... | collective-permute-start | bytes 393224 | tf_op jit(solution)/shard_map/ppermute | solution.py:376
  90.7 20.5 %copy-start.7 = (bf16[32,2048]{1,0:T(8,128)(2,1)}, bf16[32,2048]{1,0:T(8,128)(2,1)S(1)}, u32[]{:S(2)}) copy-start(bf16[32,2048]{1,0:T(8,128)(2,1)S(1)} %collective-permute-done.16.refs_10_) | copy-start | bytes 393220
  90.7 30.7 %collective-permute-start.13 = (bf16[32,2048]{1,0:T(8,128)(2,1)S(1)}, bf16[32,2048]{1,0:T(8,128)(2,1)S(1)}, u32[]{:S(2)}, u32[]{:S(2)}) collective-permute-start(bf16[32,2048]{1,0:T(8,128)(2,1)S(1)} %copy-done.16), channel_id=1, source_target_pairs={{0,20},{4,16},{8,28},{12,24},{16,4},{20,0},{24,12},{28,8},{1,21},{... | collective-permute-start | bytes 393224 | tf_op jit(solution)/shard_map/ppermute | solution.py:376
  91.9 29.5 %collective-permute-start.14 = (bf16[32,2048]{1,0:T(8,128)(2,1)S(1)}, bf16[32,2048]{1,0:T(8,128)(2,1)S(1)}, u32[]{:S(2)}, u32[]{:S(2)}) collective-permute-start(bf16[32,2048]{1,0:T(8,128)(2,1)S(1)} %copy-done.15), channel_id=1, source_target_pairs={{0,24},{4,28},{8,16},{12,20},{16,8},{20,12},{24,0},{28,4},{1,25},{... | collective-permute-start | bytes 393224 | tf_op jit(solution)/shard_map/ppermute | solution.py:376
  94.2 27.3 %collective-permute-start.15 = (bf16[32,2048]{1,0:T(8,128)(2,1)S(1)}, bf16[32,2048]{1,0:T(8,128)(2,1)S(1)}, u32[]{:S(2)}, u32[]{:S(2)}) collective-permute-start(bf16[32,2048]{1,0:T(8,128)(2,1)S(1)} %copy-done.14), channel_id=1, source_target_pairs={{0,28},{4,24},{8,20},{12,16},{16,12},{20,8},{24,4},{28,0},{1,29},{... | collective-permute-start | bytes 393224 | tf_op jit(solution)/shard_map/ppermute | solution.py:376
  (12 other events, 73.1 us)

commit v2 on v0

v2 whole, which is shorter than its diff:
```python
import functools
import math

import jax
import jax.numpy as jnp
from jax import lax
from jax.experimental import pallas as pl
from jax.experimental.pallas import tpu as pltpu
from jax.sharding import PartitionSpec as P

HD = 128
CAP = 8
SUB = 4
ROPE_BASE = 500000.0
NEG = -1e30
MIB = 1024 * 1024
F32 = jnp.float32
BF16 = jnp.bfloat16
I32 = jnp.int32
N_CHUNKS = 1

VM = pl.BlockSpec(memory_space=pltpu.VMEM)
SM = pl.BlockSpec(memory_space=pltpu.SMEM)
HBM = pl.BlockSpec(memory_space=pltpu.HBM)


def params(mib):
    return pltpu.CompilerParams(vmem_limit_bytes=mib * MIB)


def dot(a, b):
    return jnp.dot(a, b, preferred_element_type=F32)


def dot_t(a, b):
    return lax.dot_general(a, b, (((1,), (1,)), ((), ())), preferred_element_type=F32)


def iota(shape, dim):
    return lax.broadcasted_iota(I32, shape, dim)


def one_hot(cond):
    return jnp.where(cond, 1.0, 0.0).astype(BF16)


def token_place(p, steps):
    n_sub = SUB * steps
    half = lax.rem(lax.div(p, n_sub), CAP // SUB)
    return half * SUB + lax.rem(p, SUB), lax.rem(lax.div(p, SUB), steps)


def route_kernel(adp_rows, seq, steps, ids_ref, lens_ref, slots_ref, *outs):
    perm_ref, send_ref, slot_ref, len_ref, row_ref = outs
    rows = ids_ref.shape[1]
    pool = slots_ref.shape[1]
    toks = rows * steps
    me = lax.axis_index("grp")
    core = lax.rem(lax.axis_index("tp"), 2)
    sub, lane = iota((rows, rows), 0), iota((rows, rows), 1)
    eye = sub == lane

    def to_col(row):
        return jnp.sum(jnp.where(eye, row, 0.0), axis=1, keepdims=True)

    def to_row(col):
        return jnp.sum(jnp.where(eye, col, 0.0), axis=0, keepdims=True)

    ids_col = to_col(ids_ref[...].astype(F32))
    lens_col = to_col(lens_ref[...].astype(F32))
    span = iota((rows, pool), 1).astype(F32)
    pos = jnp.sum(jnp.where(ids_col == span, slots_ref[...].astype(F32), 0.0), axis=1, keepdims=True)
    pos = pos.astype(I32)
    owner = lax.div(pos, adp_rows)
    slot = (pos - owner * adp_rows).astype(F32)
    key = lax.bitwise_xor(owner, me)
    pair = lax.div(key, 2)
    place = jnp.zeros_like(pair)
    for at, j in enumerate(seq):
        place = jnp.where(pair == j, at, place)
    place = (place * 2 + lax.rem(key, 2)).astype(F32)
    key = key.astype(F32)
    place_row = to_row(place)
    same = place_row == place
    before = same & (lane < sub)
    rank = jnp.sum(jnp.where(before, 1.0, 0.0), axis=1, keepdims=True)
    dest = jnp.sum(jnp.where((place_row < place) | before, 1.0, 0.0), axis=1, keepdims=True)
    dest_row, key_row, rank_row = to_row(dest), to_row(key), to_row(rank)

    def wide(col):
        return jnp.broadcast_to(col, (rows, 128)).astype(BF16)

    row_perm = one_hot(sub.astype(F32) == dest_row)
    row_ref[...] = dot(row_perm, wide(sub[:, :1].astype(F32))).astype(I32)
    row_of, _ = token_place(iota((toks, rows), 0), steps)
    row_of = (row_of + lax.div(iota((toks, rows), 0), CAP * steps) * CAP).astype(F32)
    len_ref[...] = dot(one_hot(row_of == dest_row), wide(lens_col))
    n_pairs = len(seq)
    y = iota((n_pairs * 2 * CAP, rows), 0)
    y_key = (lax.div(y, 2 * CAP) * 2 + core).astype(F32)
    y_rank = (lax.rem(lax.div(y, CAP), 2) * SUB + lax.rem(y, SUB)).astype(F32)
    slot_ref[...] = dot(one_hot((y_key == key_row) & (y_rank == rank_row)), wide(slot)).astype(BF16)

    spread = one_hot(lax.div(iota((rows, toks), 1), steps) == iota((rows, toks), 0))
    info = jnp.concatenate([dest_row, key_row, rank_row] + [dest_row] * 5, axis=0).astype(BF16)
    info = dot(info, spread)
    dest_tok, key_tok, rank_tok = info[0:1], info[1:2], info[2:3]
    p, step_tok = iota((toks, toks), 0), lax.rem(iota((toks, toks), 1), steps)
    p_row, p_step = token_place(p, steps)
    p_row = (p_row + lax.div(p, CAP * steps) * CAP).astype(F32)
    perm = one_hot((p_row == dest_tok) & (p_step == step_tok))
    perm_ref[...] = perm
    n_send = n_pairs * CAP * steps
    p, step_tok = iota((n_send, toks), 0), lax.rem(iota((n_send, toks), 1), steps)
    p_row, p_step = token_place(p, steps)
    p_key = (lax.div(p, CAP * steps) * 2 + core).astype(F32)
    send_ref[...] = one_hot((p_key == key_tok) & (p_row.astype(F32) == rank_tok) & (p_step == step_tok))


def route(adp_rows, seq, steps, adapter_id, lengths, pool_slot):
    rows = adapter_id.shape[0]
    toks = rows * steps
    out = [
        jax.ShapeDtypeStruct((toks, toks), BF16),
        jax.ShapeDtypeStruct((len(seq) * CAP * steps, toks), BF16),
        jax.ShapeDtypeStruct((len(seq) * 2 * CAP, 128), BF16),
        jax.ShapeDtypeStruct((toks, 128), F32),
        jax.ShapeDtypeStruct((rows, 128), I32),
    ]
    return pl.pallas_call(
        functools.partial(route_kernel, adp_rows, seq, steps),
        out_shape=out,
        in_specs=[VM] * 3,
        out_specs=[VM] * len(out),
        compiler_params=params(8),
        name="route",
    )(adapter_id[None, :], lengths[None, :], pool_slot[None, :])


def pack_kernel(n_tok, send_ref, slot_ref, tok_ref, oth_ref, *sends):
    rows, steps, width = tok_ref.shape
    for j in range(0, width, 512):
        for half, ref in enumerate((tok_ref, oth_ref)):
            part = ref[:, :, j : j + 512].reshape(rows * steps, 512)
            got = dot(send_ref[...], part).astype(BF16)
            for k, out in enumerate(sends):
                for c in range(4):
                    at = ((j // 128 + c) * 2 + half) * n_tok
                    out[at : at + n_tok, :] = got[k * n_tok : (k + 1) * n_tok, c * 128 : (c + 1) * 128]
    for k, out in enumerate(sends):
        out[width // 128 * 2 * n_tok :, :] = slot_ref[k * 2 * CAP : (k + 1) * 2 * CAP, :]


def pack(n_pairs, send, slot, tokens, other):
    _, steps, width = tokens.shape
    n_tok = steps * CAP
    out = [jax.ShapeDtypeStruct((width // 128 * 2 * n_tok + 2 * CAP, 128), BF16)] * n_pairs
    return pl.pallas_call(
        functools.partial(pack_kernel, n_tok),
        out_shape=out,
        in_specs=[VM] * 4,
        out_specs=[VM] * len(out),
        compiler_params=params(16),
        name="pack",
    )(send, slot, tokens, other)


def qkv_kernel(n_x, has_acc, chunk, ids_ref, perm_ref, *refs):
    xs, ws = refs[:n_x], refs[n_x : n_x + 3]
    at = n_x + 3
    accs = refs[at : at + 3] if has_acc else (None,) * 3
    at += 3 if has_acc else 0
    outs, raw, xbuf = refs[at : at + 3], refs[at + 3], refs[at + 4]
    bufs, xsem, wsem = refs[at + 5 : at + 8], refs[at + 8], refs[at + 9]
    rows, n_steps, width = xs[0].shape
    per = width // chunk
    n_chunks = n_x * per

    def x_copy(p):
        return pltpu.make_async_copy(xs[p], raw.at[p], xsem.at[p])

    def w_copy(c, i):
        row = pl.multiple_of(ids_ref[c // per] * width + (c % per) * chunk, chunk)
        return pltpu.make_async_copy(
            ws[i].at[pl.ds(row, chunk)], bufs[i].at[c * chunk : (c + 1) * chunk], wsem.at[c, i]
        )

    def begin(c):
        if c < n_chunks:
            if c % per == 0:
                x_copy(c // per).start()
            for i in range(3):
                w_copy(c, i).start()

    ahead = 4
    for c in range(ahead):
        begin(c)
    steps = [(0, 1), (1, 2)] + [(c, min(c + 2, n_chunks)) for c in range(2, n_chunks, 2)]
    for lo, hi in steps:
        for c in range(lo, hi):
            p = c // per
            if c % per == 0:
                x_copy(p).wait()
                for j in range(0, width, chunk):
                    part = raw[p, :, :, j : j + chunk].reshape(rows * n_steps, chunk)
                    xbuf[:, p * width + j : p * width + j + chunk] = dot(perm_ref[...], part).astype(BF16)
            for i in range(3):
                w_copy(c, i).wait()
            begin(c + ahead)
        x = xbuf[:, lo * chunk : hi * chunk]
        for i in range(3):
            got = dot(x, bufs[i][lo * chunk : hi * chunk, :])
            if lo:
                outs[i][...] += got
            else:
                outs[i][...] = accs[i][...] + got if has_acc else got


def qkv(xs, perm, shards, weights, acc):
    rows, steps, width = xs[0].shape
    m = rows * steps
    chunk = min(512, width)
    n_x = len(xs)
    has_acc = acc is not None
    outs = [jax.ShapeDtypeStruct((m, w.shape[1]), F32) for w in weights]
    cols = sum(w.shape[1] for w in weights)
    extra = list(acc) if has_acc else []
    depth = n_x * width
    return pl.pallas_call(
        functools.partial(qkv_kernel, n_x, has_acc, chunk),
        out_shape=outs,
        in_specs=[SM, VM] + [HBM] * (n_x + 3) + [VM] * len(extra),
        out_specs=[VM] * 3,
        scratch_shapes=[pltpu.VMEM((n_x, rows, steps, width), BF16), pltpu.VMEM((m, depth), BF16)]
        + [pltpu.VMEM((depth, w.shape[1]), BF16) for w in weights]
        + [pltpu.SemaphoreType.DMA((n_x,)), pltpu.SemaphoreType.DMA((depth // chunk, 3))],
        compiler_params=params(62),
        cost_estimate=pl.CostEstimate(
            flops=2 * m * depth * cols, bytes_accessed=2 * depth * cols, transcendentals=0
        ),
        name="qkv",
    )(shards, perm, *xs, *weights, *extra)


def slot_mask(tiles, n_tok, cols, rank):
    tiles = tiles.astype(F32)
    rep = n_tok // (2 * CAP)
    slots = jnp.concatenate([tiles[:CAP]] * rep + [tiles[CAP:]] * rep, axis=0)
    slots = jnp.concatenate([slots] * (cols // 128), axis=1)
    return slots == lax.div(iota((n_tok, cols), 1), rank).astype(F32)


def mid_kernel(n_tok, rank, down_ref, oth_ref, *refs):
    ins, out_ref, x_ref, d_ref, sem = refs[:-4], refs[-4], refs[-3], refs[-2], refs[-1]
    loads = [pltpu.make_async_copy(r, d_ref.at[i], sem.at[i]) for i, r in enumerate((down_ref, oth_ref))]
    for c in loads:
        c.start()
    _, cols, width = d_ref.shape
    for k, r in enumerate(ins):
        rows = slice(k * n_tok, (k + 1) * n_tok)
        for c in range(width // 128):
            for half in range(2):
                at = (c * 2 + half) * n_tok
                x_ref[half, rows, c * 128 : (c + 1) * 128] = r[at : at + n_tok, :]
    prod = 0.0
    for half in range(2):
        loads[half].wait()
        prod = prod + dot_t(x_ref[half], d_ref[half])
    for k, r in enumerate(ins):
        mask = slot_mask(r[r.shape[0] - 2 * CAP :, :], n_tok, cols, rank)
        part = jnp.where(mask, prod[k * n_tok : (k + 1) * n_tok], 0.0)
        tot = part[:, :128]
        for c in range(128, cols, 128):
            tot = tot + part[:, c : c + 128]
        out_ref[k * n_tok : (k + 1) * n_tok, :] = tot + pltpu.roll(tot, rank, 1)


def mid(recv, down, other, n_tok, rank):
    n = len(recv)
    cols, width = down.shape
    return pl.pallas_call(
        functools.partial(mid_kernel, n_tok, rank),
        out_shape=jax.ShapeDtypeStruct((n * n_tok, 128), F32),
        in_specs=[HBM] * 2 + [VM] * n,
        out_specs=VM,
        scratch_shapes=[
            pltpu.VMEM((2, n * n_tok, width), BF16),
            pltpu.VMEM((2, cols, width), BF16),
            pltpu.SemaphoreType.DMA((2,)),
        ],
        compiler_params=params(24),
        cost_estimate=pl.CostEstimate(
            flops=4 * n * n_tok * width * cols, bytes_accessed=4 * width * cols, transcendentals=0
        ),
        name="mid",
    )(down, other, *recv)


def up_kernel(n_tok, rank, n_recv, up_ref, oth_ref, a_ref, b_ref, *refs):
    ins, outs, u_ref, sem = refs[:n_recv], refs[n_recv : 2 * n_recv], refs[-2], refs[-1]
    loads = [pltpu.make_async_copy(r, u_ref.at[i], sem.at[i]) for i, r in enumerate((up_ref, oth_ref))]
    for c in loads:
        c.start()
    _, cols, width = u_ref.shape
    total = (a_ref[...] + b_ref[...]).astype(BF16).astype(F32)
    spread = []
    for k in range(n_recv):
        both = jnp.concatenate([total[k * n_tok : (k + 1) * n_tok]] * (cols // 128), axis=1)
        mask = slot_mask(ins[k][...], n_tok, cols, rank)
        spread.append(jnp.where(mask, both, 0.0).astype(BF16))
    rows = jnp.concatenate(spread, axis=0)
    for half in range(2):
        loads[half].wait()
        for j in range(0, width, 512):
            got = dot(rows, u_ref[half, :, j : j + 512]).astype(BF16)
            for k in range(n_recv):
                outs[k][half * n_tok : (half + 1) * n_tok, j : j + 512] = got[k * n_tok : (k + 1) * n_tok]


def up(a, b, recv, up_rows, other, n_tok, rank):
    n = len(recv)
    cols, width = up_rows.shape
    last = recv[0].shape[0] // (2 * CAP) - 1
    tail = pl.BlockSpec((2 * CAP, 128), lambda i: (last, 0))

    def whole(x):
        return pl.BlockSpec(x.shape, lambda i: (0, 0))

    out = jax.ShapeDtypeStruct((2 * n_tok, width), BF16)
    return pl.pallas_call(
        functools.partial(up_kernel, n_tok, rank, n),
        out_shape=[out] * n,
        grid=(1,),
        in_specs=[HBM] * 2 + [whole(a), whole(b)] + [tail] * n,
        out_specs=[whole(out)] * n,
        scratch_shapes=[pltpu.VMEM((2, cols, width), BF16), pltpu.SemaphoreType.DMA((2,))],
        compiler_params=params(20),
        cost_estimate=pl.CostEstimate(
            flops=4 * n * n_tok * width * cols, bytes_accessed=4 * width * cols, transcendentals=0
        ),
        name="up",
    )(up_rows, other, a, b, *recv)


def make_attn_kernel(nb, steps, group):
    halves = CAP // SUB
    n_tok = steps * CAP
    n_sub = steps * SUB
    n_q = group * n_sub

    def kernel(*refs):
        core_ref, rows_ref, q_hbm, k_hbm, v_hbm, tab_hbm, ck_ref, cv_ref = refs[:8]
        lora_refs = refs[8 : 8 + nb]
        out_ref, kbuf, vbuf, obuf, q_ref, k_ref, v_ref, tab_ref, loras, sem, osem = refs[8 + nb :]
        kv_local = k_ref.shape[1] // HD
        span = ck_ref.shape[1]
        scale = 1.0 / math.sqrt(HD)
        is_even = core_ref[0] == 0

        def copies(b):
            at = pl.ds(b * n_tok, n_tok)
            got = [
                pltpu.make_async_copy(src.at[at], dst.at[at], sem.at[b, n])
                for n, (src, dst) in enumerate(
                    ((q_hbm, q_ref), (k_hbm, k_ref), (v_hbm, v_ref), (tab_hbm, tab_ref))
                )
            ]
            got.append(pltpu.make_async_copy(lora_refs[b], loras.at[b], sem.at[b, 4]))
            return got

        for b in range(0, nb, 2):
            for n in (b, b + 1):
                for i in range(CAP):
                    r = rows_ref[n * CAP + i, 0]
                    pltpu.make_async_copy(ck_ref.at[r], kbuf.at[n, i], sem.at[n, 5]).start()
                    pltpu.make_async_copy(cv_ref.at[r], vbuf.at[n, i], sem.at[n, 6]).start()
                for c in copies(n):
                    c.start()

        qi, ki = iota((n_sub, n_sub), 0), iota((n_sub, n_sub), 1)
        new_ok = (lax.rem(qi, SUB) == lax.rem(ki, SUB)) & (lax.div(qi, SUB) >= lax.div(ki, SUB))
        new_bias = jnp.concatenate([jnp.where(new_ok, 0.0, NEG)] * group, axis=0)
        col, sub = iota((CAP, SUB * span), 1), iota((CAP, SUB * span), 0)
        own = lax.div(col, span) == lax.rem(sub, SUB)
        at_pos = lax.rem(col, span).astype(F32)
        y, x = iota((n_tok, n_tok), 0), iota((n_tok, n_tok), 1)
        x_row, x_step = token_place(x, steps)
        turn = one_hot((lax.div(y, steps) == x_row) & (lax.rem(y, steps) == x_step))

        for b in range(nb):
            if b % 2 == 0:
                for n in (b, b + 1):
                    for c in copies(n):
                        c.wait()
                    pltpu.make_async_copy(ck_ref.at[pl.ds(0, CAP)], kbuf.at[n], sem.at[n, 5]).wait()
                    pltpu.make_async_copy(cv_ref.at[pl.ds(0, CAP)], vbuf.at[n], sem.at[n, 6]).wait()
            rows = slice(b * n_tok, (b + 1) * n_tok)
            cos, sin = tab_ref[rows, :HD], tab_ref[rows, HD : 2 * HD]
            mine, theirs = loras.at[2 * (b // 2)], loras.at[2 * (b // 2) + 1]
            biases = []
            for t in range(halves):
                at = b * n_tok + t * n_sub
                lens = tab_ref[at : at + CAP, 2 * HD :][:, :1]
                bias = jnp.where(own & (at_pos < lens), 0.0, NEG)
                biases.append(jnp.concatenate([bias] * (n_q // CAP), axis=0))

            def rope(v):
                return v * cos + pltpu.roll(v, HD // 2, 1) * sin

            work = [(h, t) for h in range(kv_local) for t in range(halves)]
            qs, kns, vns = {}, {}, {}
            for h in range(kv_local):
                hs = slice(h * HD, (h + 1) * HD)
                heads = []
                for g in range(group):
                    cs = slice((h * group + g) * HD, (h * group + g + 1) * HD)
                    if b % 2 == 0:
                        lora = jnp.where(is_even, mine[:n_tok, cs], theirs[n_tok:, cs])
                    else:
                        lora = jnp.where(is_even, theirs[n_tok:, cs], mine[:n_tok, cs])
                    heads.append(rope(q_ref[rows, cs] + lora.astype(F32)).astype(BF16))
                kn = rope(k_ref[rows, hs]).astype(BF16)
                vn = v_ref[rows, hs].astype(BF16)
                for t in range(halves):
                    ts = slice(t * n_sub, (t + 1) * n_sub)
                    qs[h, t] = jnp.concatenate([v[ts] for v in heads], axis=0)
                    kns[h, t], vns[h, t] = kn[ts], vn[ts]
            s1, s2 = {}, {}
            for h, t in work:
                kc = kbuf[b, t * SUB : (t + 1) * SUB, :, h * HD : (h + 1) * HD].reshape(SUB * span, HD)
                s1[h, t] = dot_t(qs[h, t], kc) * scale + biases[t]
                s2[h, t] = dot_t(qs[h, t], kns[h, t]) * scale + new_bias
            p1, p2 = {}, {}
            for w in work:
                top = jnp.maximum(jnp.max(s1[w], axis=1, keepdims=True), jnp.max(s2[w], axis=1, keepdims=True))
                e1 = jnp.exp(s1[w] - top)
                e2 = jnp.exp(s2[w] - top)
                den = jnp.sum(e1, axis=1, keepdims=True) + jnp.sum(e2, axis=1, keepdims=True)
                inv = 1.0 / den
                p1[w], p2[w] = (e1 * inv).astype(BF16), (e2 * inv).astype(BF16)
            parts = {}
            for h, t in work:
                vc = vbuf[b, t * SUB : (t + 1) * SUB, :, h * HD : (h + 1) * HD].reshape(SUB * span, HD)
                o = dot(p1[h, t], vc) + dot(p2[h, t], vns[h, t])
                o = o.astype(BF16)
                parts[h, t] = jnp.concatenate([o[g * n_sub : (g + 1) * n_sub] for g in range(group)], axis=1)
            wide = group * HD
            for h in range(kv_local):
                both = jnp.concatenate([parts[h, t] for t in range(halves)], axis=0)
                mixed = dot(turn, both).astype(BF16)
                obuf[b, :, :, h * wide : (h + 1) * wide] = mixed.reshape(CAP, steps, wide)
            for i in range(CAP):
                r = rows_ref[b * CAP + i, 0]
                pltpu.make_async_copy(obuf.at[b, i], out_ref.at[r], osem).start()
        for b in range(nb):
            pltpu.make_async_copy(obuf.at[b], out_ref.at[pl.ds(0, CAP)], osem).wait()

    return kernel


def attention(steps, core, rows, q, k, v, table, ck, cv, loras):
    n_rows = ck.shape[0]
    nb = n_rows // CAP
    group = q.shape[1] // k.shape[1]
    buf = (nb, CAP) + ck.shape[1:]
    return pl.pallas_call(
        make_attn_kernel(nb, steps, group),
        out_shape=jax.ShapeDtypeStruct((n_rows, steps, q.shape[1]), BF16),
        in_specs=[SM, SM] + [HBM] * (6 + nb),
        out_specs=HBM,
        scratch_shapes=[
            pltpu.VMEM(buf, BF16),
            pltpu.VMEM(buf, BF16),
            pltpu.VMEM((nb, CAP, steps, q.shape[1]), BF16),
            pltpu.VMEM(q.shape, F32),
            pltpu.VMEM(k.shape, F32),
            pltpu.VMEM(v.shape, F32),
            pltpu.VMEM(table.shape, F32),
            pltpu.VMEM((nb,) + loras[0].shape, BF16),
            pltpu.SemaphoreType.DMA((nb, 7)),
            pltpu.SemaphoreType.DMA,
        ],
        compiler_params=params(62),
        name="attn",
    )(core, rows, q, k, v, table, ck, cv, *loras)


def swap(x, n, bit):
    return lax.ppermute(x, "tp", [(i, i ^ bit) for i in range(n)])


def after(x, *deps):
    return lax.optimization_barrier((x, *deps))[0]


def body(
    tokens,
    adapter_id,
    pool_slot,
    lengths,
    w_query,
    w_key,
    w_value,
    pooled_down_weights,
    pool_up,
    cache_key,
    cache_value,
):
    n_grp = lax.axis_size("grp")
    n_tp = lax.axis_size("tp")
    row_count, steps, width = tokens.shape
    adp_rows, _, rank = pooled_down_weights.shape
    n_tok = steps * CAP
    n_blocks = row_count // CAP
    n_pairs = n_grp // 2
    seq = [j for a in range(n_pairs // 2) for j in (n_pairs // 2 + a, a)]
    me = lax.axis_index("tp")
    core = lax.rem(me, 2)

    def cross(x, j):
        perm = [
            (g * n_tp + t, (g ^ (2 * j + t % 2)) * n_tp + t)
            for g in range(n_grp)
            for t in range(n_tp)
        ]
        return lax.ppermute(x, ("grp", "tp"), perm)

    other_tokens = swap(tokens, n_tp, 1)
    perm, send, slot, lens, rows = route(adp_rows, seq, steps, adapter_id, lengths, pool_slot)
    sends = pack(n_pairs, send, slot, tokens, other_tokens)
    recv = {j: cross(sends[j], j) for j in seq}

    first = recv[0]
    up_rows = after(pool_up, sends[0]).reshape(adp_rows * rank, pool_up.shape[2])
    up_other = swap(up_rows, n_tp, 1)
    down = jnp.swapaxes(after(pooled_down_weights, sends[0]), 1, 2).reshape(adp_rows * rank, width)
    down_other = swap(down, n_tp, 1)

    pieces = {0: after(tokens, sends[0])}
    bit = n_tp // 2
    while bit > 1:
        pieces.update({off ^ bit: swap(p, n_tp, bit) for off, p in list(pieces.items())})
        bit //= 2
    far = [o for o in sorted(pieces) if o]
    weights = (w_query, w_key, w_value)

    def shards(offs):
        return jnp.stack([lax.bitwise_xor(me, o) for o in offs]).astype(I32)

    ids = after(shards([0, 1]), first, up_other, down_other)
    acc = qkv([tokens, other_tokens], perm, ids, weights, None)

    half = HD // 2
    inv_freq = jnp.exp(jnp.arange(half, dtype=F32) * (-2.0 * math.log(ROPE_BASE) / HD))
    inv_freq = jnp.concatenate([inv_freq, inv_freq])
    step_of = jnp.tile(jnp.repeat(jnp.arange(steps, dtype=F32), SUB), row_count // SUB)
    lens = after(lens, first)
    angles = (lens + step_of[:, None]) * inv_freq
    sign = jnp.where(jnp.arange(HD) < half, -1.0, 1.0).astype(F32)
    table = jnp.concatenate([jnp.cos(angles), jnp.sin(angles) * sign, lens], axis=1)

    chunk = n_pairs // N_CHUNKS
    groups = [seq[i : i + chunk] for i in range(0, n_pairs, chunk)]
    mids = []
    for i, js in enumerate(groups):
        got = [recv[j] for j in js]
        if i == 0:
            got, acc, table = lax.optimization_barrier((got, acc, table))
        part = mid(got, down, down_other, n_tok, rank)
        bit = 2
        while bit < n_tp // 2:
            part = part + swap(part, n_tp, bit)
            bit *= 2
        mids.append((got, part, swap(part, n_tp, bit)))
    back = {}
    for js, (got, part, other) in zip(groups, mids):
        for j, x in zip(js, up(part, other, got, up_rows, up_other, n_tok, rank)):
            back[j] = cross(x, j)
    late = {}
    for o in far:
        x = after(pieces[o], mids[-1][1])
        late[o] = x
        late[o ^ 1] = swap(x, n_tp, 1)
    ids = after(shards(sorted(late)), back[0])
    q, k, v = qkv([late[o] for o in sorted(late)], perm, ids, weights, acc)
    loras = {}
    for j in seq:
        own = after(back[j], q)
        loras[j] = (own, swap(own, n_tp, 1))
    core_id = core.astype(I32).reshape(1)
    lora_list = [a for j in seq for a in loras[j]]
    if n_grp != n_blocks:
        mine_all = jnp.stack([a[:n_tok] for a in lora_list[0::2]])
        other_all = jnp.stack([a[n_tok:] for a in lora_list[1::2]])
        even = jnp.where(core == 0, mine_all, other_all)
        odd = jnp.where(core == 0, other_all, mine_all)
        full = jnp.stack([even, odd], axis=1).reshape(n_grp, n_tok, even.shape[2])
        span = jnp.arange(pool_slot.shape[0], dtype=I32)
        pos = jnp.sum(jnp.where(adapter_id[:, None] == span[None, :], pool_slot[None, :], 0), axis=1)
        key = lax.bitwise_xor(lax.div(pos, adp_rows), lax.axis_index("grp"))
        order = jnp.array([2 * j + c for j in seq for c in (0, 1)], I32)
        used = jnp.any(key[:, None] == order[None, :], axis=0)
        at = jnp.cumsum(used.astype(I32)) - 1
        pick = (at[None, :] == jnp.arange(n_blocks)[:, None]) & used[None, :]
        chosen = full[jnp.sum(jnp.where(pick, jnp.arange(n_grp)[None, :], 0), axis=1)]
        core_id = jnp.zeros((1,), I32)
        twice = jnp.concatenate([chosen, chosen], axis=1)
        lora_list = [twice[b] for b in range(n_blocks)]
    return attention(steps, core_id, rows[:, :1], q, k, v, table, cache_key, cache_value, lora_list)


def solution(mesh):
    in_specs = (
        P("grp", None, "tp"),
        P("grp"),
        P(),
        P("grp"),
        P(None, "tp"),
        P(None, "tp"),
        P(None, "tp"),
        P("grp", "tp", None),
        P("grp", None, "tp"),
        P("grp", None, "tp"),
        P("grp", None, "tp"),
    )
    out_specs = P("grp", None, "tp")
    return jax.shard_map(body, mesh=mesh, in_specs=in_specs, out_specs=out_specs, check_vma=False)
```

time: 271 us -> 93.1 us (0.34); the launches traced: 266 us -> 92.6 us
  waiting for transfers between devices: 99.8 us -> 13.2 us
  local copies, waits for them, and re-layouts: 64.9 us -> 7.3 us
  Pallas kernels: 0 us -> 47.6 us
  matrix products: 40 us -> 0 us
  blocking collectives: 23.7 us -> 0 us
  between operations: 13.7 us -> 0.37 us
  starting transfers between devices: 11.4 us -> 21.6 us
  other arithmetic: 12.8 us -> 2.62 us
    all_to_all x2 -> x0, waiting for transfers between devices: 99.8 us -> none  [the longest x1 87 us: body(): lax.all_to_all(down_weight_panels, 'grp', split_axis=0, concat_axis=0, ti...]
    pallas_call x0 -> x7, Pallas kernels: none -> 47.6 us  [the longest x2 28.1 us: qkv(): pl.pallas_call(functools.partial(qkv_kernel, n_x, has_acc, chunk), out_sh...]
    dot_general x9 -> x0, matrix products: 40 us -> none  [the longest x3 22.9 us: add_term(): return jnp.dot(piece_rows, matrix, preferred_element_type=jnp.float32)]
    ppermute x0 -> x18, starting transfers between devices: none -> 21.6 us  [the longest x8 17.6 us: cross(): return lax.ppermute(x, ('grp', 'tp'), perm)]
    gather x8 -> x0, local copies, waits for them, and re-layouts: 19.2 us -> none  [the longest x1 4.96 us: body(): down_got[block_owner]]
    reshape x8 -> x0, local copies, waits for them, and re-layouts: 17.4 us -> none  [the longest x1 6.91 us: body(): piece_rows = shard_piece.reshape(count_of_tokens, piece_width)]
    psum x1 -> x0, blocking collectives: 14.1 us -> none  [mid_reduce(): return lax.psum(partial_value_sum, 'tp')]
    ppermute x0 -> x18, waiting for transfers between devices: none -> 13.2 us  [the longest x8 8.76 us: cross(): return lax.ppermute(x, ('grp', 'tp'), perm)]
  transfers between devices with their start and end apart: 3 -> 18, of which waited for: 2 -> 5; matrix products, arithmetic and copies ran while one was open for 26% -> 3% of each run, Pallas kernels for 0% -> 39%
where the time goes in v2:
time: 93.1 us; the launch traced here: 92.6 us
  Pallas kernels  47.6 us (51%)
  starting transfers between devices  21.6 us (23%)
  waiting for transfers between devices  13.2 us (14%)
  local copies, waits for them, and re-layouts  7.3 us (8%)
  other arithmetic  2.62 us (3%)
    pallas_call x2, Pallas kernels, qkv(): pl.pallas_call(functools.partial(qkv_kernel, n_x, has_acc, chunk), out_sh...  28.1 us
    ppermute x8, starting transfers between devices, cross(): return lax.ppermute(x, ('grp', 'tp'), perm)  17.6 us
    pallas_call x1, Pallas kernels, attention(): pl.pallas_call(make_attn_kernel(nb, steps, group), out_shape=jax.ShapeDty...  10.2 us
    ppermute x8, waiting for transfers between devices, cross(): return lax.ppermute(x, ('grp', 'tp'), perm)  8.76 us
    unnamed x34, local copies, waits for them, and re-layouts  7.12 us
    ppermute x10, waiting for transfers between devices, swap(): return lax.ppermute(x, 'tp', [(i, i ^ bit) for i in range(n)])  4.43 us
    pallas_call x1, Pallas kernels, mid(): pl.pallas_call(functools.partial(mid_kernel, n_tok, rank), out_shape=jax....  4.41 us
    ppermute x10, starting transfers between devices, swap(): return lax.ppermute(x, 'tp', [(i, i ^ bit) for i in range(n)])  3.95 us
  transfers between devices with their start and end apart: 18, of which 5 were waited for; matrix products, arithmetic and copies ran while one was open for 3% of the time, Pallas kernels for 39%

profile of v2, /device:TPU:9, one launch (start us, length us, event | category | flops | bytes accessed | tf_op | source)
XLA Modules:
  0.0 92.6 jit_solution(10053880603948739811)
XLA Ops:
  0.0 0.7 collective-permute-start
  0.7 0.7 copy-done.7
  4.5 1.6 %copy-done = bf16[64,4,2048]{2,1,0:T(4,128)(2,1)S(1)} copy-done((bf16[64,4,2048]{2,1,0:T(4,128)(2,1)S(1)}, bf16[64,4,2048]{2,1,0:T(4,128)(2,1)}, u32[]{:S(2)}) %copy-start) | copy-done | bytes 1048600
  6.1 1.4 %pack.1 = (bf16[1040,128]{1,0:T(8,128)(2,1)S(1)}, bf16[1040,128]{1,0:T(8,128)(2,1)}, bf16[1040,128]{1,0:T(8,128)(2,1)}, bf16[1040,128]{1,0:T(8,128)(2,1)}) custom-call(bf16[128,256]{1,0:T(8,128)(2,1)S(1)} %get-tuple-element.44.send_ref, bf16[64,128]{1,0:T(8,128)(2,1)S(1)} %get-tuple-element.45.slot_ref, bf16[64,4,2048]{2,1,0:T(4,128)(2,1)S(1)} %copy-done, ...), custom_call_target="tpu_custom_call" | custom-call | tf_op jit(solution)/shard_map/pack/pallas_call | solution.py:158
  8.0 3.1 %collective-permute-start.4 = (bf16[1040,128]{1,0:T(8,128)(2,1)S(1)}, bf16[1040,128]{1,0:T(8,128)(2,1)S(1)}, u32[]{:S(2)}, u32[]{:S(2)}) collective-permute-start(bf16[1040,128]{1,0:T(8,128)(2,1)S(1)} %get-tuple-element.46), channel_id=1, source_target_pairs={{0,0},{1,5},{2,2},{3,7},{4,4},{5,1},{6,6},{7,3},{8,8},{9,13},{10,1... | collective-permute-start | bytes 798728 | tf_op jit(solution)/shard_map/ppermute | solution.py:526
  11.2 1.3 %collective-permute-start.9 = (bf16[64,4,2048]{2,1,0:T(4,128)(2,1)S(1)}, bf16[64,4,2048]{2,1,0:T(4,128)(2,1)}, u32[]{:S(2)}, u32[]{:S(2)}) collective-permute-start(bf16[64,4,2048]{2,1,0:T(4,128)(2,1)S(1)} %copy-done.1), channel_id=1, source_target_pairs={{0,2},{1,3},{2,0},{3,1},{4,6},{5,7},{6,4},{7,5},{8,10},{9,11},{10,... | collective-permute-start | bytes 3145736 | tf_op jit(solution)/shard_map/ppermute | solution.py:489
  13.3 2.3 %collective-permute-start.3 = (bf16[1040,128]{1,0:T(8,128)(2,1)}, bf16[1040,128]{1,0:T(8,128)(2,1)S(1)}, u32[]{:S(2)}, u32[]{:S(2)}) collective-permute-start(bf16[1040,128]{1,0:T(8,128)(2,1)} %get-tuple-element.49), channel_id=1, source_target_pairs={{0,16},{1,21},{2,18},{3,23},{4,20},{5,17},{6,22},{7,19},{8,24},{9,... | collective-permute-start | bytes 798728 | tf_op jit(solution)/shard_map/ppermute | solution.py:526
  15.6 2.2 %collective-permute-start.5 = (bf16[1040,128]{1,0:T(8,128)(2,1)}, bf16[1040,128]{1,0:T(8,128)(2,1)S(1)}, u32[]{:S(2)}, u32[]{:S(2)}) collective-permute-start(bf16[1040,128]{1,0:T(8,128)(2,1)} %get-tuple-element.50), channel_id=1, source_target_pairs={{0,24},{1,29},{2,26},{3,31},{4,28},{5,25},{6,30},{7,27},{8,16},{9,... | collective-permute-start | bytes 798728 | tf_op jit(solution)/shard_map/ppermute | solution.py:526
  18.4 0.8 pad_maximum_fusion.refs_5_
  19.2 2.1 %collective-permute-start.6 = (bf16[1040,128]{1,0:T(8,128)(2,1)}, bf16[1040,128]{1,0:T(8,128)(2,1)}, u32[]{:S(2)}, u32[]{:S(2)}) collective-permute-start(bf16[1040,128]{1,0:T(8,128)(2,1)} %get-tuple-element.51), channel_id=1, source_target_pairs={{0,8},{1,13},{2,10},{3,15},{4,12},{5,9},{6,14},{7,11},{8,0},{9,5},... | collective-permute-start | bytes 798728 | tf_op jit(solution)/shard_map/ppermute | solution.py:526
  21.3 13.6 %qkv.2 = (f32[256,2048]{1,0:T(8,128)}, f32[256,256]{1,0:T(8,128)}, f32[256,256]{1,0:T(8,128)}) custom-call(s32[2]{0:T(128)} %pad_add_fusion.1.ids_ref, bf16[256,256]{1,0:T(8,128)(2,1)} %copy-done.5, bf16[64,4,2048]{2,1,0:T(4,128)(2,1)} %refs_0_.1, bf16[64,4,2048]{2,1,0:T(4,128)(2,1)} %copy-done.2, bf16[8192,2048]{1,0:T(8,128)(2,1)} %refs_2_.3, ...), custom_call_target="tpu_custom_call" | custom-call | flops 5368709120 | bytes 20971520 | tf_op jit(solution)/shard_map/qkv/pallas_call | solution.py:229
  34.9 3.0 %collective-permute-done.5.refs_2_ = bf16[1040,128]{1,0:T(8,128)(2,1)S(1)} collective-permute-done((bf16[1040,128]{1,0:T(8,128)(2,1)}, bf16[1040,128]{1,0:T(8,128)(2,1)S(1)}, u32[]{:S(2)}, u32[]{:S(2)}) %collective-permute-start.5) | collective-permute-done | bytes 266272 | tf_op jit(solution)/shard_map/ppermute | solution.py:526
  37.9 1.6 %copy-done.3 = bf16[8,2048,64]{1,2,0:T(8,128)(2,1)S(1)} copy-done((bf16[8,2048,64]{1,2,0:T(8,128)(2,1)S(1)}, bf16[8,2048,64]{1,2,0:T(8,128)(2,1)}, u32[]{:S(2)}) %copy-start.3) | copy-done | bytes 2097176
  39.5 4.4 %mid.1.a_ref = f32[128,128]{1,0:T(8,128)S(1)} custom-call(bf16[512,2048]{1,0:T(8,128)(2,1)S(1)} %bitcast.14, bf16[512,2048]{1,0:T(8,128)(2,1)} %collective-permute-done.2.oth_ref, bf16[1040,128]{1,0:T(8,128)(2,1)S(1)} %collective-permute-done.3.refs_0_, bf16[1040,128]{1,0:T(8,128)(2,1)S(1)} %collective-permute-done.4.refs_1_, ...), custom_call_target="tpu_custom_call" | custom-call | flops 536870912 | bytes 4194304 | tf_op jit(solution)/shard_map/mid/pallas_call | solution.py:281
  44.4 2.8 %collective-permute-done.7.b_ref = f32[128,128]{1,0:T(8,128)S(1)} collective-permute-done((f32[128,128]{1,0:T(8,128)S(1)}, f32[128,128]{1,0:T(8,128)S(1)}, u32[]{:S(2)}, u32[]{:S(2)}) %collective-permute-start.7) | collective-permute-done | bytes 65568 | tf_op jit(solution)/shard_map/ppermute | solution.py:489
  47.2 2.9 %up.1 = (bf16[64,2048]{1,0:T(8,128)(2,1)S(1)}, bf16[64,2048]{1,0:T(8,128)(2,1)S(1)}, bf16[64,2048]{1,0:T(8,128)(2,1)S(1)}, bf16[64,2048]{1,0:T(8,128)(2,1)S(1)}) custom-call(bf16[512,2048]{1,0:T(8,128)(2,1)S(1)} %bitcast.16, bf16[512,2048]{1,0:T(8,128)(2,1)} %collective-permute-done.1.oth_ref, f32[128,128]{1,0:T(8,128)S(1)} %mid.1.a_ref, ...), custom_call_target="tpu_custom_call" | custom-call | flops 536870912 | bytes 4194304 | tf_op jit(solution)/shard_map/up/pallas_call | solution.py:330
  50.1 3.1 %collective-permute-start.8 = (bf16[64,2048]{1,0:T(8,128)(2,1)S(1)}, bf16[64,2048]{1,0:T(8,128)(2,1)S(1)}, u32[]{:S(2)}, u32[]{:S(2)}) collective-permute-start(bf16[64,2048]{1,0:T(8,128)(2,1)S(1)} %get-tuple-element.63), channel_id=1, source_target_pairs={{0,0},{1,5},{2,2},{3,7},{4,4},{5,1},{6,6},{7,3},{8,8},{9,13},{10,1... | collective-permute-start | bytes 786440 | tf_op jit(solution)/shard_map/ppermute | solution.py:526
  53.8 1.0 %collective-permute-start.11 = (bf16[64,2048]{1,0:T(8,128)(2,1)S(1)}, bf16[64,2048]{1,0:T(8,128)(2,1)S(1)}, u32[]{:S(2)}, u32[]{:S(2)}) collective-permute-start(bf16[64,2048]{1,0:T(8,128)(2,1)S(1)} %get-tuple-element.74), channel_id=1, source_target_pairs={{0,16},{1,21},{2,18},{3,23},{4,20},{5,17},{6,22},{7,19},{8,24},{9,... | collective-permute-start | bytes 786440 | tf_op jit(solution)/shard_map/ppermute | solution.py:526
  54.8 1.5 %collective-permute-start.14 = (bf16[64,2048]{1,0:T(8,128)(2,1)S(1)}, bf16[64,2048]{1,0:T(8,128)(2,1)S(1)}, u32[]{:S(2)}, u32[]{:S(2)}) collective-permute-start(bf16[64,2048]{1,0:T(8,128)(2,1)S(1)} %get-tuple-element.77), channel_id=1, source_target_pairs={{0,24},{1,29},{2,26},{3,31},{4,28},{5,25},{6,30},{7,27},{8,16},{9,... | collective-permute-start | bytes 786440 | tf_op jit(solution)/shard_map/ppermute | solution.py:526
  56.3 2.2 %collective-permute-start.16 = (bf16[64,2048]{1,0:T(8,128)(2,1)S(1)}, bf16[64,2048]{1,0:T(8,128)(2,1)}, u32[]{:S(2)}, u32[]{:S(2)}) collective-permute-start(bf16[64,2048]{1,0:T(8,128)(2,1)S(1)} %get-tuple-element.79), channel_id=1, source_target_pairs={{0,8},{1,13},{2,10},{3,15},{4,12},{5,9},{6,14},{7,11},{8,0},{9,5},... | collective-permute-start | bytes 786440 | tf_op jit(solution)/shard_map/ppermute | solution.py:526
  58.5 14.6 %qkv.3 = (f32[256,2048]{1,0:T(8,128)}, f32[256,256]{1,0:T(8,128)}, f32[256,256]{1,0:T(8,128)}) custom-call(s32[2]{0:T(128)} %pad_add_fusion.ids_ref, bf16[256,256]{1,0:T(8,128)(2,1)} %copy-done.5, bf16[64,4,2048]{2,1,0:T(4,128)(2,1)} %collective-permute-done.9.refs_0_, bf16[64,4,2048]{2,1,0:T(4,128)(2,1)} %collective-permute-done.10.refs_1_, ...), custom_call_target="tpu_custom_call" | custom-call | flops 5368709120 | bytes 20971520 | tf_op jit(solution)/shard_map/qkv/pallas_call | solution.py:229
  73.7 5.7 %collective-permute-done.14.refs_12_ = bf16[64,2048]{1,0:T(8,128)(2,1)S(1)} collective-permute-done((bf16[64,2048]{1,0:T(8,128)(2,1)S(1)}, bf16[64,2048]{1,0:T(8,128)(2,1)S(1)}, u32[]{:S(2)}, u32[]{:S(2)}) %collective-permute-start.14) | collective-permute-done | bytes 262176 | tf_op jit(solution)/shard_map/ppermute | solution.py:526
  80.0 1.0 %collective-permute-done.15.refs_13_ = bf16[64,2048]{1,0:T(8,128)(2,1)S(1)} collective-permute-done((bf16[64,2048]{1,0:T(8,128)(2,1)S(1)}, bf16[64,2048]{1,0:T(8,128)(2,1)S(1)}, u32[]{:S(2)}, u32[]{:S(2)}) %collective-permute-start.15) | collective-permute-done | bytes 262176 | tf_op jit(solution)/shard_map/ppermute | solution.py:489
  82.3 10.2 %attn.1 = bf16[64,4,2048]{2,1,0:T(4,128)(2,1)} custom-call(s32[1]{0:T(128)} %bitcast.refs_0_, s32[64,1]{1,0:T(8,128)} %bitcast.17, f32[256,2048]{1,0:T(8,128)} %get-tuple-element.70.refs_2_, f32[256,256]{1,0:T(8,128)} %get-tuple-element.71.refs_3_, f32[256,256]{1,0:T(8,128)} %get-tuple-element.72.refs_4_, f32[256,384]{1,0:T(8,128)} %pad_maximum_fusion.refs_5_, ...), custom_call_target="tpu_custom_call" | custom-call | tf_op jit(solution)/shard_map/attn/pallas_call | solution.py:466
  (63 shorter events, 8.5 us)
Async XLA Ops:
  0.0 4.5 %collective-permute-start = (bf16[64,4,2048]{2,1,0:T(4,128)(2,1)}, bf16[64,4,2048]{2,1,0:T(4,128)(2,1)S(1)}, u32[]{:S(2)}, u32[]{:S(2)}) collective-permute-start(bf16[64,4,2048]{2,1,0:T(4,128)(2,1)} %refs_0_.1), channel_id=1, source_target_pairs={{0,1},{1,0},{2,3},{3,2},{4,5},{5,4},{6,7},{7,6},{8,9},{9,8},{10,11... | collective-permute-start | bytes 3145736 | tf_op jit(solution)/shard_map/ppermute | solution.py:489
  4.5 3.0 %copy-start.2 = (bf16[64,4,2048]{2,1,0:T(4,128)(2,1)}, bf16[64,4,2048]{2,1,0:T(4,128)(2,1)S(1)}, u32[]{:S(2)}) copy-start(bf16[64,4,2048]{2,1,0:T(4,128)(2,1)S(1)} %collective-permute-done.oth_ref.refs_1_) | copy-start | bytes 3145732
  6.1 5.1 %copy-start.1 = (bf16[64,4,2048]{2,1,0:T(4,128)(2,1)S(1)}, bf16[64,4,2048]{2,1,0:T(4,128)(2,1)}, u32[]{:S(2)}) copy-start(bf16[64,4,2048]{2,1,0:T(4,128)(2,1)} %refs_0_.1) | copy-start | bytes 3145732
  7.5 11.7 %collective-permute-start.1 = (bf16[512,2048]{1,0:T(8,128)(2,1)}, bf16[512,2048]{1,0:T(8,128)(2,1)}, u32[]{:S(2)}, u32[]{:S(2)}) collective-permute-start(bf16[512,2048]{1,0:T(8,128)(2,1)} %bitcast.15), channel_id=1, source_target_pairs={{0,1},{1,0},{2,3},{3,2},{4,5},{5,4},{6,7},{7,6},{8,9},{9,8},{10,11... | collective-permute-start | bytes 6291464 | tf_op jit(solution)/shard_map/ppermute | solution.py:489
  7.5 13.8 %collective-permute-start.2 = (bf16[512,2048]{1,0:T(8,128)(2,1)}, bf16[512,2048]{1,0:T(8,128)(2,1)}, u32[]{:S(2)}, u32[]{:S(2)}) collective-permute-start(bf16[512,2048]{1,0:T(8,128)(2,1)} %bitcast.13), channel_id=1, source_target_pairs={{0,1},{1,0},{2,3},{3,2},{4,5},{5,4},{6,7},{7,6},{8,9},{9,8},{10,11... | collective-permute-start | bytes 6291464 | tf_op jit(solution)/shard_map/ppermute | solution.py:489
  8.0 7.6 %collective-permute-start.4 = (bf16[1040,128]{1,0:T(8,128)(2,1)S(1)}, bf16[1040,128]{1,0:T(8,128)(2,1)S(1)}, u32[]{:S(2)}, u32[]{:S(2)}) collective-permute-start(bf16[1040,128]{1,0:T(8,128)(2,1)S(1)} %get-tuple-element.46), channel_id=1, source_target_pairs={{0,0},{1,5},{2,2},{3,7},{4,4},{5,1},{6,6},{7,3},{8,8},{9,13},{10,1... | collective-permute-start | bytes 798728 | tf_op jit(solution)/shard_map/ppermute | solution.py:526
  11.2 32.7 %collective-permute-start.9 = (bf16[64,4,2048]{2,1,0:T(4,128)(2,1)S(1)}, bf16[64,4,2048]{2,1,0:T(4,128)(2,1)}, u32[]{:S(2)}, u32[]{:S(2)}) collective-permute-start(bf16[64,4,2048]{2,1,0:T(4,128)(2,1)S(1)} %copy-done.1), channel_id=1, source_target_pairs={{0,2},{1,3},{2,0},{3,1},{4,6},{5,7},{6,4},{7,5},{8,10},{9,11},{10,... | collective-permute-start | bytes 3145736 | tf_op jit(solution)/shard_map/ppermute | solution.py:489
  13.3 21.5 %collective-permute-start.3 = (bf16[1040,128]{1,0:T(8,128)(2,1)}, bf16[1040,128]{1,0:T(8,128)(2,1)S(1)}, u32[]{:S(2)}, u32[]{:S(2)}) collective-permute-start(bf16[1040,128]{1,0:T(8,128)(2,1)} %get-tuple-element.49), channel_id=1, source_target_pairs={{0,16},{1,21},{2,18},{3,23},{4,20},{5,17},{6,22},{7,19},{8,24},{9,... | collective-permute-start | bytes 798728 | tf_op jit(solution)/shard_map/ppermute | solution.py:526
  15.6 22.3 %collective-permute-start.5 = (bf16[1040,128]{1,0:T(8,128)(2,1)}, bf16[1040,128]{1,0:T(8,128)(2,1)S(1)}, u32[]{:S(2)}, u32[]{:S(2)}) collective-permute-start(bf16[1040,128]{1,0:T(8,128)(2,1)} %get-tuple-element.50), channel_id=1, source_target_pairs={{0,24},{1,29},{2,26},{3,31},{4,28},{5,25},{6,30},{7,27},{8,16},{9,... | collective-permute-start | bytes 798728 | tf_op jit(solution)/shard_map/ppermute | solution.py:526
  19.2 18.7 %collective-permute-start.6 = (bf16[1040,128]{1,0:T(8,128)(2,1)}, bf16[1040,128]{1,0:T(8,128)(2,1)}, u32[]{:S(2)}, u32[]{:S(2)}) collective-permute-start(bf16[1040,128]{1,0:T(8,128)(2,1)} %get-tuple-element.51), channel_id=1, source_target_pairs={{0,8},{1,13},{2,10},{3,15},{4,12},{5,9},{6,14},{7,11},{8,0},{9,5},... | collective-permute-start | bytes 798728 | tf_op jit(solution)/shard_map/ppermute | solution.py:526
  39.5 7.7 %copy-start.4 = (bf16[8,64,2048]{2,1,0:T(8,128)(2,1)S(1)}, bf16[8,64,2048]{2,1,0:T(8,128)(2,1)}, u32[]{:S(2)}) copy-start(bf16[8,64,2048]{2,1,0:T(8,128)(2,1)} %param.19) | copy-start | bytes 6291460
  43.9 14.6 %collective-permute-start.10 = (bf16[64,4,2048]{2,1,0:T(4,128)(2,1)}, bf16[64,4,2048]{2,1,0:T(4,128)(2,1)}, u32[]{:S(2)}, u32[]{:S(2)}) collective-permute-start(bf16[64,4,2048]{2,1,0:T(4,128)(2,1)} %collective-permute-done.9.refs_0_), channel_id=1, source_target_pairs={{0,1},{1,0},{2,3},{3,2},{4,5},{5,4},{6,7},{7,6},{8,9},{9,8},{10,11... | collective-permute-start | bytes 3145736 | tf_op jit(solution)/shard_map/ppermute | solution.py:489
  44.0 3.2 %collective-permute-start.7 = (f32[128,128]{1,0:T(8,128)S(1)}, f32[128,128]{1,0:T(8,128)S(1)}, u32[]{:S(2)}, u32[]{:S(2)}) collective-permute-start(f32[128,128]{1,0:T(8,128)S(1)} %mid.1.a_ref), channel_id=1, source_target_pairs={{0,2},{1,3},{2,0},{3,1},{4,6},{5,7},{6,4},{7,5},{8,10},{9,11},{10,... | collective-permute-start | bytes 196616 | tf_op jit(solution)/shard_map/ppermute | solution.py:489
  50.1 8.5 %collective-permute-start.8 = (bf16[64,2048]{1,0:T(8,128)(2,1)S(1)}, bf16[64,2048]{1,0:T(8,128)(2,1)S(1)}, u32[]{:S(2)}, u32[]{:S(2)}) collective-permute-start(bf16[64,2048]{1,0:T(8,128)(2,1)S(1)} %get-tuple-element.63), channel_id=1, source_target_pairs={{0,0},{1,5},{2,2},{3,7},{4,4},{5,1},{6,6},{7,3},{8,8},{9,13},{10,1... | collective-permute-start | bytes 786440 | tf_op jit(solution)/shard_map/ppermute | solution.py:526
  53.8 19.3 %collective-permute-start.11 = (bf16[64,2048]{1,0:T(8,128)(2,1)S(1)}, bf16[64,2048]{1,0:T(8,128)(2,1)S(1)}, u32[]{:S(2)}, u32[]{:S(2)}) collective-permute-start(bf16[64,2048]{1,0:T(8,128)(2,1)S(1)} %get-tuple-element.74), channel_id=1, source_target_pairs={{0,16},{1,21},{2,18},{3,23},{4,20},{5,17},{6,22},{7,19},{8,24},{9,... | collective-permute-start | bytes 786440 | tf_op jit(solution)/shard_map/ppermute | solution.py:526
  54.8 24.6 %collective-permute-start.14 = (bf16[64,2048]{1,0:T(8,128)(2,1)S(1)}, bf16[64,2048]{1,0:T(8,128)(2,1)S(1)}, u32[]{:S(2)}, u32[]{:S(2)}) collective-permute-start(bf16[64,2048]{1,0:T(8,128)(2,1)S(1)} %get-tuple-element.77), channel_id=1, source_target_pairs={{0,24},{1,29},{2,26},{3,31},{4,28},{5,25},{6,30},{7,27},{8,16},{9,... | collective-permute-start | bytes 786440 | tf_op jit(solution)/shard_map/ppermute | solution.py:526
  56.3 23.2 %collective-permute-start.16 = (bf16[64,2048]{1,0:T(8,128)(2,1)S(1)}, bf16[64,2048]{1,0:T(8,128)(2,1)}, u32[]{:S(2)}, u32[]{:S(2)}) collective-permute-start(bf16[64,2048]{1,0:T(8,128)(2,1)S(1)} %get-tuple-element.79), channel_id=1, source_target_pairs={{0,8},{1,13},{2,10},{3,15},{4,12},{5,9},{6,14},{7,11},{8,0},{9,5},... | collective-permute-start | bytes 786440 | tf_op jit(solution)/shard_map/ppermute | solution.py:526
  58.5 14.7 %copy-start.10 = (bf16[64,2048]{1,0:T(8,128)(2,1)}, bf16[64,2048]{1,0:T(8,128)(2,1)S(1)}, u32[]{:S(2)}) copy-start(bf16[64,2048]{1,0:T(8,128)(2,1)S(1)} %collective-permute-done.8.refs_10_) | copy-start | bytes 786436
  73.1 8.4 %copy-start.11 = (bf16[64,2048]{1,0:T(8,128)(2,1)}, bf16[64,2048]{1,0:T(8,128)(2,1)S(1)}, u32[]{:S(2)}) copy-start(bf16[64,2048]{1,0:T(8,128)(2,1)S(1)} %collective-permute-done.11.refs_8_) | copy-start | bytes 786436
  73.1 6.8 %collective-permute-start.12 = (bf16[64,2048]{1,0:T(8,128)(2,1)S(1)}, bf16[64,2048]{1,0:T(8,128)(2,1)S(1)}, u32[]{:S(2)}, u32[]{:S(2)}) collective-permute-start(bf16[64,2048]{1,0:T(8,128)(2,1)S(1)} %collective-permute-done.11.refs_8_), channel_id=1, source_target_pairs={{0,1},{1,0},{2,3},{3,2},{4,5},{5,4},{6,7},{7,6},{8,9},{9,8},{10,11... | collective-permute-start | bytes 786440 | tf_op jit(solution)/shard_map/ppermute | solution.py:489
  73.2 6.7 %collective-permute-start.13 = (bf16[64,2048]{1,0:T(8,128)(2,1)S(1)}, bf16[64,2048]{1,0:T(8,128)(2,1)S(1)}, u32[]{:S(2)}, u32[]{:S(2)}) collective-permute-start(bf16[64,2048]{1,0:T(8,128)(2,1)S(1)} %collective-permute-done.8.refs_10_), channel_id=1, source_target_pairs={{0,1},{1,0},{2,3},{3,2},{4,5},{5,4},{6,7},{7,6},{8,9},{9,8},{10,11... | collective-permute-start | bytes 786440 | tf_op jit(solution)/shard_map/ppermute | solution.py:489
  79.4 2.1 %copy-start.12 = (bf16[64,2048]{1,0:T(8,128)(2,1)}, bf16[64,2048]{1,0:T(8,128)(2,1)S(1)}, u32[]{:S(2)}) copy-start(bf16[64,2048]{1,0:T(8,128)(2,1)S(1)} %collective-permute-done.14.refs_12_) | copy-start | bytes 786436
  79.4 1.5 %collective-permute-start.15 = (bf16[64,2048]{1,0:T(8,128)(2,1)S(1)}, bf16[64,2048]{1,0:T(8,128)(2,1)S(1)}, u32[]{:S(2)}, u32[]{:S(2)}) collective-permute-start(bf16[64,2048]{1,0:T(8,128)(2,1)S(1)} %collective-permute-done.14.refs_12_), channel_id=1, source_target_pairs={{0,1},{1,0},{2,3},{3,2},{4,5},{5,4},{6,7},{7,6},{8,9},{9,8},{10,11... | collective-permute-start | bytes 786440 | tf_op jit(solution)/shard_map/ppermute | solution.py:489
  79.4 2.1 %collective-permute-start.17 = (bf16[64,2048]{1,0:T(8,128)(2,1)}, bf16[64,2048]{1,0:T(8,128)(2,1)S(1)}, u32[]{:S(2)}, u32[]{:S(2)}) collective-permute-start(bf16[64,2048]{1,0:T(8,128)(2,1)} %collective-permute-done.16.refs_14_), channel_id=1, source_target_pairs={{0,1},{1,0},{2,3},{3,2},{4,5},{5,4},{6,7},{7,6},{8,9},{9,8},{10,11... | collective-permute-start | bytes 786440 | tf_op jit(solution)/shard_map/ppermute | solution.py:489
  (11 other events, 11.1 us)

commit v3 on v2

v3 whole, which is shorter than its diff:
```python
import functools
import math

import jax
import jax.numpy as jnp
from jax import lax
from jax.experimental import pallas as pl
from jax.experimental.pallas import tpu as pltpu
from jax.sharding import PartitionSpec as P

HD = 128
CAP = 8
SUB = 4
ROPE_BASE = 500000.0
NEG = -1e30
MIB = 1024 * 1024
F32 = jnp.float32
BF16 = jnp.bfloat16
I32 = jnp.int32
FIRST_STEPS = (256, 256)
STEP = 512
PARTS = 4
AHEAD = 4
TOGETHER = 2

TINY = pl.CostEstimate(flops=1, bytes_accessed=1, transcendentals=0)
COST = pl.CostEstimate(flops=10**10, bytes_accessed=3 * 10**7, transcendentals=0)
VM = pl.BlockSpec(memory_space=pltpu.VMEM)
SM = pl.BlockSpec(memory_space=pltpu.SMEM)
HBM = pl.BlockSpec(memory_space=pltpu.HBM)


def params(mib):
    return pltpu.CompilerParams(vmem_limit_bytes=int(mib * MIB))


def dot(a, b):
    return jnp.dot(a, b, preferred_element_type=F32)


def dot_t(a, b):
    return lax.dot_general(a, b, (((1,), (1,)), ((), ())), preferred_element_type=F32)


def iota(shape, dim):
    return lax.broadcasted_iota(I32, shape, dim)


def one_hot(cond):
    return jnp.where(cond, 1.0, 0.0).astype(BF16)


def token_place(p, steps):
    n_sub = SUB * steps
    half = lax.rem(lax.div(p, n_sub), CAP // SUB)
    return half * SUB + lax.rem(p, SUB), lax.rem(lax.div(p, SUB), steps)


def route_kernel(adp_rows, seq, steps, ids_ref, lens_ref, slots_ref, *outs):
    perm_ref, send_ref, slot_ref, len_ref, row_ref = outs
    rows = ids_ref.shape[1]
    pool = slots_ref.shape[1]
    toks = rows * steps
    me = lax.axis_index("grp")
    core = lax.rem(lax.axis_index("tp"), 2)
    sub, lane = iota((rows, rows), 0), iota((rows, rows), 1)
    eye = sub == lane

    def to_col(row):
        return jnp.sum(jnp.where(eye, row, 0.0), axis=1, keepdims=True)

    def to_row(col):
        return jnp.sum(jnp.where(eye, col, 0.0), axis=0, keepdims=True)

    ids_col = to_col(ids_ref[...].astype(F32))
    lens_col = to_col(lens_ref[...].astype(F32))
    span = iota((rows, pool), 1).astype(F32)
    pos = jnp.sum(jnp.where(ids_col == span, slots_ref[...].astype(F32), 0.0), axis=1, keepdims=True)
    pos = pos.astype(I32)
    owner = lax.div(pos, adp_rows)
    slot = (pos - owner * adp_rows).astype(F32)
    key = lax.bitwise_xor(owner, me)
    pair = lax.div(key, 2)
    place = jnp.zeros_like(pair)
    for at, j in enumerate(seq):
        place = jnp.where(pair == j, at, place)
    place = (place * 2 + lax.rem(key, 2)).astype(F32)
    key = key.astype(F32)
    place_row = to_row(place)
    same = place_row == place
    before = same & (lane < sub)
    rank = jnp.sum(jnp.where(before, 1.0, 0.0), axis=1, keepdims=True)
    dest = jnp.sum(jnp.where((place_row < place) | before, 1.0, 0.0), axis=1, keepdims=True)
    dest_row, key_row, rank_row = to_row(dest), to_row(key), to_row(rank)

    def wide(col):
        return jnp.broadcast_to(col, (rows, 128)).astype(BF16)

    row_perm = one_hot(sub.astype(F32) == dest_row)
    ids = jnp.broadcast_to(lane[:1].astype(F32), (8, rows)).astype(BF16)
    row_ref[...] = dot_t(ids, row_perm).astype(I32)
    row_of, _ = token_place(iota((toks, rows), 0), steps)
    row_of = (row_of + lax.div(iota((toks, rows), 0), CAP * steps) * CAP).astype(F32)
    len_ref[...] = dot(one_hot(row_of == dest_row), wide(lens_col))
    n_pairs = len(seq)
    y = iota((n_pairs * 2 * CAP, rows), 0)
    y_key = (lax.div(y, 2 * CAP) * 2 + core).astype(F32)
    y_rank = (lax.rem(lax.div(y, CAP), 2) * SUB + lax.rem(y, SUB)).astype(F32)
    slot_ref[...] = dot(one_hot((y_key == key_row) & (y_rank == rank_row)), wide(slot)).astype(BF16)

    spread = one_hot(lax.div(iota((rows, toks), 1), steps) == iota((rows, toks), 0))
    info = jnp.concatenate([dest_row, key_row, rank_row] + [dest_row] * 5, axis=0).astype(BF16)
    info = dot(info, spread)
    dest_tok, key_tok, rank_tok = info[0:1], info[1:2], info[2:3]
    p, step_tok = iota((toks, toks), 0), lax.rem(iota((toks, toks), 1), steps)
    p_row, p_step = token_place(p, steps)
    p_row = (p_row + lax.div(p, CAP * steps) * CAP).astype(F32)
    perm = one_hot((p_row == dest_tok) & (p_step == step_tok))
    perm_ref[...] = perm
    n_send = n_pairs * CAP * steps
    p, step_tok = iota((n_send, toks), 0), lax.rem(iota((n_send, toks), 1), steps)
    p_row, p_step = token_place(p, steps)
    p_key = (lax.div(p, CAP * steps) * 2 + core).astype(F32)
    send_ref[...] = one_hot((p_key == key_tok) & (p_row.astype(F32) == rank_tok) & (p_step == step_tok))


def route(adp_rows, seq, steps, adapter_id, lengths, pool_slot):
    rows = adapter_id.shape[0]
    toks = rows * steps
    out = [
        jax.ShapeDtypeStruct((toks, toks), BF16),
        jax.ShapeDtypeStruct((len(seq) * CAP * steps, toks), BF16),
        jax.ShapeDtypeStruct((len(seq) * 2 * CAP, 128), BF16),
        jax.ShapeDtypeStruct((toks, 128), F32),
        jax.ShapeDtypeStruct((8, rows), I32),
    ]
    return pl.pallas_call(
        functools.partial(route_kernel, adp_rows, seq, steps),
        out_shape=out,
        in_specs=[VM] * 3,
        out_specs=[VM] * len(out),
        compiler_params=params(62),
        name="route",
    )(adapter_id[None, :], lengths[None, :], pool_slot[None, :])


def pack_kernel(n_tok, send_ref, slot_ref, tok_ref, oth_ref, *sends):
    rows, steps, width = tok_ref.shape
    for j in range(0, width, 512):
        for half, ref in enumerate((tok_ref, oth_ref)):
            part = ref[:, :, j : j + 512].reshape(rows * steps, 512)
            got = dot(send_ref[...], part).astype(BF16)
            for k, out in enumerate(sends):
                for c in range(4):
                    at = ((j // 128 + c) * 2 + half) * n_tok
                    out[at : at + n_tok, :] = got[k * n_tok : (k + 1) * n_tok, c * 128 : (c + 1) * 128]
    for k, out in enumerate(sends):
        out[width // 128 * 2 * n_tok :, :] = slot_ref[k * 2 * CAP : (k + 1) * 2 * CAP, :]


def pack(n_pairs, send, slot, tokens, other):
    _, steps, width = tokens.shape
    n_tok = steps * CAP
    out = [jax.ShapeDtypeStruct((width // 128 * 2 * n_tok + 2 * CAP, 128), BF16)] * n_pairs
    return pl.pallas_call(
        functools.partial(pack_kernel, n_tok),
        out_shape=out,
        in_specs=[VM] * 4,
        out_specs=[VM] * len(out),
        compiler_params=params(62),
        name="pack",
    )(send, slot, tokens, other)


def qkv_kernel(n_x, has_acc, steps, ids_ref, perm_ref, *refs):
    xs, ws = refs[:n_x], refs[n_x : n_x + 3]
    at = n_x + 3
    accs = refs[at : at + 3] if has_acc else (None,) * 3
    at += 3 if has_acc else 0
    outs, raw, xbuf = refs[at : at + 3], refs[at + 3], refs[at + 4]
    bufs, xsem, wsem = refs[at + 5 : at + 8], refs[at + 8], refs[at + 9]
    rows, n_steps, width = xs[0].shape

    def x_copy(p):
        return pltpu.make_async_copy(xs[p], raw.at[p], xsem.at[p])

    def w_copy(n, i):
        lo, size = steps[n]
        row = pl.multiple_of(ids_ref[lo // width] * width + lo % width, 256)
        return pltpu.make_async_copy(ws[i].at[pl.ds(row, size)], bufs[i].at[lo : lo + size], wsem.at[n, i])

    def begin(n):
        if n < len(steps):
            if steps[n][0] % width == 0:
                x_copy(steps[n][0] // width).start()
            for i in range(3):
                w_copy(n, i).start()

    begin(0)
    begin(1)
    for n, (lo, size) in enumerate(steps):
        begin(n + 2)
        if lo % width == 0:
            p = lo // width
            x_copy(p).wait()
            for j in range(0, width, 512):
                part = raw[p, :, :, j : j + 512].reshape(rows * n_steps, 512)
                xbuf[:, lo + j : lo + j + 512] = dot(perm_ref[...], part).astype(BF16)
        for i in range(3):
            w_copy(n, i).wait()
        x = xbuf[:, lo : lo + size]
        for i in range(3):
            got = dot(x, bufs[i][lo : lo + size, :])
            if lo:
                outs[i][...] += got
            else:
                outs[i][...] = accs[i][...] + got if has_acc else got


def qkv(xs, perm, shards, weights, acc):
    rows, steps, width = xs[0].shape
    m = rows * steps
    n_x = len(xs)
    has_acc = acc is not None
    outs = [jax.ShapeDtypeStruct((m, w.shape[1]), F32) for w in weights]
    cols = sum(w.shape[1] for w in weights)
    extra = list(acc) if has_acc else []
    depth = n_x * width
    plan, at = [], 0
    for size in FIRST_STEPS:
        plan.append((at, size))
        at += size
    while at < depth:
        plan.append((at, min(STEP, width - at % width)))
        at += plan[-1][1]
    return pl.pallas_call(
        functools.partial(qkv_kernel, n_x, has_acc, plan),
        out_shape=outs,
        in_specs=[SM, VM] + [HBM] * (n_x + 3) + [VM] * len(extra),
        out_specs=[VM] * 3,
        scratch_shapes=[pltpu.VMEM((n_x, rows, steps, width), BF16), pltpu.VMEM((m, depth), BF16)]
        + [pltpu.VMEM((depth, w.shape[1]), BF16) for w in weights]
        + [pltpu.SemaphoreType.DMA((n_x,)), pltpu.SemaphoreType.DMA((len(plan), 3))],
        compiler_params=params(60.5),
        cost_estimate=COST,
        name="qkv",
    )(shards, perm, *xs, *weights, *extra)


def panel_loads(srcs, dst, sem):
    size = dst.shape[1] // PARTS
    loads = []
    for i, src in enumerate(srcs):
        at = [pl.ds(p * size, size) for p in range(PARTS)]
        loads.append([pltpu.make_async_copy(src.at[a], dst.at[i, a], sem.at[i, p]) for p, a in enumerate(at)])
        for c in loads[-1]:
            c.start()
    return loads


def slot_mask(tiles, n_tok, cols, rank):
    tiles = tiles.astype(F32)
    rep = n_tok // (2 * CAP)
    slots = jnp.concatenate([tiles[:CAP]] * rep + [tiles[CAP:]] * rep, axis=0)
    slots = jnp.concatenate([slots] * (cols // 128), axis=1)
    return slots == lax.div(iota((n_tok, cols), 1), rank).astype(F32)


def mid_kernel(n_tok, rank, down_ref, oth_ref, *refs):
    ins, out_ref, x_ref, d_ref, sem = refs[:-4], refs[-4], refs[-3], refs[-2], refs[-1]
    _, cols, width = d_ref.shape
    loads = panel_loads((down_ref, oth_ref), d_ref, sem)
    for k, r in enumerate(ins):
        rows = slice(k * n_tok, (k + 1) * n_tok)
        for c in range(width // 128):
            for half in range(2):
                at = (c * 2 + half) * n_tok
                x_ref[half, rows, c * 128 : (c + 1) * 128] = r[at : at + n_tok, :]
    prod = 0.0
    for half in range(2):
        for c in loads[half]:
            c.wait()
        prod = prod + dot_t(x_ref[half], d_ref[half])
    for k, r in enumerate(ins):
        mask = slot_mask(r[r.shape[0] - 2 * CAP :, :], n_tok, cols, rank)
        part = jnp.where(mask, prod[k * n_tok : (k + 1) * n_tok], 0.0)
        tot = part[:, :128]
        for c in range(128, cols, 128):
            tot = tot + part[:, c : c + 128]
        out_ref[k * n_tok : (k + 1) * n_tok, :] = tot + pltpu.roll(tot, rank, 1)


def mid(recv, down, other, n_tok, rank):
    n = len(recv)
    cols, width = down.shape
    return pl.pallas_call(
        functools.partial(mid_kernel, n_tok, rank),
        out_shape=jax.ShapeDtypeStruct((n * n_tok, 128), F32),
        in_specs=[HBM] * 2 + [VM] * n,
        out_specs=VM,
        scratch_shapes=[
            pltpu.VMEM((2, n * n_tok, width), BF16),
            pltpu.VMEM((2, cols, width), BF16),
            pltpu.SemaphoreType.DMA((2, PARTS)),
        ],
        compiler_params=params(24),
        cost_estimate=COST,
        name="mid",
    )(down, other, *recv)


def up_kernel(n_tok, rank, n_recv, up_ref, oth_ref, a_ref, b_ref, *refs):
    ins, outs, u_ref, sem = refs[:n_recv], refs[n_recv : 2 * n_recv], refs[-2], refs[-1]
    _, cols, width = u_ref.shape
    loads = panel_loads((up_ref, oth_ref), u_ref, sem)
    total = (a_ref[...] + b_ref[...]).astype(BF16).astype(F32)
    spread = []
    for k in range(n_recv):
        both = jnp.concatenate([total[k * n_tok : (k + 1) * n_tok]] * (cols // 128), axis=1)
        mask = slot_mask(ins[k][...], n_tok, cols, rank)
        spread.append(jnp.where(mask, both, 0.0).astype(BF16))
    rows = jnp.concatenate(spread, axis=0)
    for half in range(2):
        for c in loads[half]:
            c.wait()
        for j in range(0, width, 512):
            got = dot(rows, u_ref[half, :, j : j + 512]).astype(BF16)
            for k in range(n_recv):
                outs[k][half * n_tok : (half + 1) * n_tok, j : j + 512] = got[k * n_tok : (k + 1) * n_tok]


def up(a, b, recv, up_rows, other, n_tok, rank):
    n = len(recv)
    cols, width = up_rows.shape
    last = recv[0].shape[0] // (2 * CAP) - 1
    tail = pl.BlockSpec((2 * CAP, 128), lambda i: (last, 0))

    def whole(x):
        return pl.BlockSpec(x.shape, lambda i: (0, 0))

    out = jax.ShapeDtypeStruct((2 * n_tok, width), BF16)
    return pl.pallas_call(
        functools.partial(up_kernel, n_tok, rank, n),
        out_shape=[out] * n,
        grid=(1,),
        in_specs=[HBM] * 2 + [whole(a), whole(b)] + [tail] * n,
        out_specs=[whole(out)] * n,
        scratch_shapes=[pltpu.VMEM((2, cols, width), BF16), pltpu.SemaphoreType.DMA((2, PARTS))],
        compiler_params=params(20),
        cost_estimate=COST,
        name="up",
    )(up_rows, other, a, b, *recv)


def make_attn_kernel(plan, steps, group, has_prev):
    nb = len(plan)
    halves = CAP // SUB
    n_tok = steps * CAP
    n_sub = steps * SUB
    n_q = group * n_sub

    def kernel(*refs):
        core_ref, rows_ref, q_hbm, k_hbm, v_hbm, tab_hbm, ck_ref, cv_ref = refs[:8]
        lora_refs = refs[8 : 8 + nb]
        at = 8 + nb + int(has_prev)
        out_ref, kbuf, vbuf, obuf, q_ref, k_ref, v_ref, tab_ref, loras, sem, osem = refs[at:]
        kv_local = k_ref.shape[1] // HD
        span = ck_ref.shape[1]
        scale = 1.0 / math.sqrt(HD)
        core = core_ref[0]
        blocks = [2 * j + (1 - core if other else core) for j, other in plan]

        def copies(b):
            at, to = pl.ds(pl.multiple_of(blocks[b] * n_tok, n_tok), n_tok), pl.ds(b * n_tok, n_tok)
            got = [
                pltpu.make_async_copy(src.at[at], dst.at[to], sem.at[b, n])
                for n, (src, dst) in enumerate(
                    ((q_hbm, q_ref), (k_hbm, k_ref), (v_hbm, v_ref), (tab_hbm, tab_ref))
                )
            ]
            part = pl.ds(n_tok if plan[b][1] else 0, n_tok)
            got.append(pltpu.make_async_copy(lora_refs[b].at[part], loras.at[b], sem.at[b, 4]))
            return got

        def begin(b):
            for i in range(CAP):
                r = rows_ref[blocks[b] * CAP + i]
                pltpu.make_async_copy(ck_ref.at[r], kbuf.at[b, i], sem.at[b, 5]).start()
                pltpu.make_async_copy(cv_ref.at[r], vbuf.at[b, i], sem.at[b, 6]).start()
            for c in copies(b):
                c.start()

        for b in range(min(AHEAD, nb)):
            begin(b)

        qi, ki = iota((n_sub, n_sub), 0), iota((n_sub, n_sub), 1)
        new_ok = (lax.rem(qi, SUB) == lax.rem(ki, SUB)) & (lax.div(qi, SUB) >= lax.div(ki, SUB))
        new_bias = jnp.concatenate([jnp.where(new_ok, 0.0, NEG)] * group, axis=0)
        col, sub = iota((CAP, SUB * span), 1), iota((CAP, SUB * span), 0)
        own = lax.div(col, span) == lax.rem(sub, SUB)
        at_pos = lax.rem(col, span).astype(F32)
        y, x = iota((n_tok, n_tok), 0), iota((n_tok, n_tok), 1)
        x_row, x_step = token_place(x, steps)
        turn = one_hot((lax.div(y, steps) == x_row) & (lax.rem(y, steps) == x_step))

        wide = group * HD
        for start in range(0, nb, TOGETHER):
            these = range(start, min(start + TOGETHER, nb))
            for b in these:
                if b + AHEAD < nb:
                    begin(b + AHEAD)
            for b in these:
                for c in copies(b):
                    c.wait()
                pltpu.make_async_copy(ck_ref.at[pl.ds(0, CAP)], kbuf.at[b], sem.at[b, 5]).wait()
                pltpu.make_async_copy(cv_ref.at[pl.ds(0, CAP)], vbuf.at[b], sem.at[b, 6]).wait()
            work = [(b, h, t) for b in these for h in range(kv_local) for t in range(halves)]
            biases, qs, kns, vns = {}, {}, {}, {}
            for b in these:
                rows = slice(b * n_tok, (b + 1) * n_tok)
                cos, sin = tab_ref[rows, :HD], tab_ref[rows, HD : 2 * HD]

                def rope(v):
                    return v * cos + pltpu.roll(v, HD // 2, 1) * sin

                for t in range(halves):
                    at = b * n_tok + t * n_sub
                    lens = tab_ref[at : at + CAP, 2 * HD :][:, :1]
                    bias = jnp.where(own & (at_pos < lens), 0.0, NEG)
                    biases[b, t] = jnp.concatenate([bias] * (n_q // CAP), axis=0)
                for h in range(kv_local):
                    hs = slice(h * HD, (h + 1) * HD)
                    heads = []
                    for g in range(group):
                        cs = slice((h * group + g) * HD, (h * group + g + 1) * HD)
                        heads.append(rope(q_ref[rows, cs] + loras[b, :, cs].astype(F32)).astype(BF16))
                    kn = rope(k_ref[rows, hs]).astype(BF16)
                    vn = v_ref[rows, hs].astype(BF16)
                    for t in range(halves):
                        ts = slice(t * n_sub, (t + 1) * n_sub)
                        qs[b, h, t] = jnp.concatenate([v[ts] for v in heads], axis=0)
                        kns[b, h, t], vns[b, h, t] = kn[ts], vn[ts]
            s1, s2 = {}, {}
            for w in work:
                b, h, t = w
                kc = kbuf[b, t * SUB : (t + 1) * SUB, :, h * HD : (h + 1) * HD].reshape(SUB * span, HD)
                s1[w] = dot_t(qs[w], kc) * scale + biases[b, t]
                s2[w] = dot_t(qs[w], kns[w]) * scale + new_bias
            p1, p2 = {}, {}
            for w in work:
                top = jnp.maximum(jnp.max(s1[w], axis=1, keepdims=True), jnp.max(s2[w], axis=1, keepdims=True))
                e1 = jnp.exp(s1[w] - top)
                e2 = jnp.exp(s2[w] - top)
                den = jnp.sum(e1, axis=1, keepdims=True) + jnp.sum(e2, axis=1, keepdims=True)
                inv = 1.0 / den
                p1[w], p2[w] = (e1 * inv).astype(BF16), (e2 * inv).astype(BF16)
            parts = {}
            for w in work:
                b, h, t = w
                vc = vbuf[b, t * SUB : (t + 1) * SUB, :, h * HD : (h + 1) * HD].reshape(SUB * span, HD)
                o = dot(p1[w], vc) + dot(p2[w], vns[w])
                o = o.astype(BF16)
                parts[w] = jnp.concatenate([o[g * n_sub : (g + 1) * n_sub] for g in range(group)], axis=1)
            for b in these:
                for h in range(kv_local):
                    both = jnp.concatenate([parts[b, h, t] for t in range(halves)], axis=0)
                    mixed = dot(turn, both).astype(BF16)
                    obuf[b, :, :, h * wide : (h + 1) * wide] = mixed.reshape(CAP, steps, wide)
                for i in range(CAP):
                    r = rows_ref[blocks[b] * CAP + i]
                    pltpu.make_async_copy(obuf.at[b, i], out_ref.at[r], osem).start()
        for b in range(nb):
            pltpu.make_async_copy(obuf.at[b], out_ref.at[pl.ds(0, CAP)], osem).wait()

    return kernel


def attention(plan, steps, core, rows, q, k, v, table, ck, cv, loras, prev):
    n_rows = ck.shape[0]
    nb = len(plan)
    n = nb * CAP * steps
    group = q.shape[1] // k.shape[1]
    buf = (nb, CAP) + ck.shape[1:]
    extra = [] if prev is None else [prev]
    return pl.pallas_call(
        make_attn_kernel(plan, steps, group, bool(extra)),
        out_shape=jax.ShapeDtypeStruct((n_rows, steps, q.shape[1]), BF16),
        in_specs=[SM, SM] + [HBM] * (6 + nb + len(extra)),
        out_specs=HBM,
        scratch_shapes=[
            pltpu.VMEM(buf, BF16),
            pltpu.VMEM(buf, BF16),
            pltpu.VMEM((nb, CAP, steps, q.shape[1]), BF16),
            pltpu.VMEM((n, q.shape[1]), F32),
            pltpu.VMEM((n, k.shape[1]), F32),
            pltpu.VMEM((n, v.shape[1]), F32),
            pltpu.VMEM((n, table.shape[1]), F32),
            pltpu.VMEM((nb, CAP * steps, q.shape[1]), BF16),
            pltpu.SemaphoreType.DMA((nb, 7)),
            pltpu.SemaphoreType.DMA,
        ],
        input_output_aliases={8 + nb: 0} if extra else {},
        compiler_params=params(62),
        cost_estimate=TINY,
        name="attn",
    )(core, rows, q, k, v, table, ck, cv, *loras, *extra)


def swap(x, n, bit):
    return lax.ppermute(x, "tp", [(i, i ^ bit) for i in range(n)])


def after(x, *deps):
    return lax.optimization_barrier((x, *deps))[0]


def body(
    tokens,
    adapter_id,
    pool_slot,
    lengths,
    w_query,
    w_key,
    w_value,
    pooled_down_weights,
    pool_up,
    cache_key,
    cache_value,
):
    n_grp = lax.axis_size("grp")
    n_tp = lax.axis_size("tp")
    row_count, steps, width = tokens.shape
    adp_rows, _, rank = pooled_down_weights.shape
    n_tok = steps * CAP
    n_blocks = row_count // CAP
    n_pairs = n_grp // 2
    seq = [*range(n_pairs // 2, n_pairs), *range(n_pairs // 2)]
    me = lax.axis_index("tp")
    core = lax.rem(me, 2)

    def cross(x, j):
        perm = [
            (g * n_tp + t, (g ^ (2 * j + t % 2)) * n_tp + t)
            for g in range(n_grp)
            for t in range(n_tp)
        ]
        return lax.ppermute(x, ("grp", "tp"), perm)

    other_tokens = swap(tokens, n_tp, 1)
    perm, send, slot, lens, rows = route(adp_rows, seq, steps, adapter_id, lengths, pool_slot)
    rows = rows[0]
    sends = pack(n_pairs, send, slot, tokens, other_tokens)
    recv = {j: cross(sends[j], j) for j in seq}

    first = recv[0]
    up_rows = after(pool_up, sends[0]).reshape(adp_rows * rank, pool_up.shape[2])
    up_other = swap(up_rows, n_tp, 1)
    down = jnp.swapaxes(after(pooled_down_weights, sends[0]), 1, 2).reshape(adp_rows * rank, width)
    down_other = swap(down, n_tp, 1)

    weights = (w_query, w_key, w_value)

    def shards(offs):
        return jnp.stack([lax.bitwise_xor(me, o) for o in offs]).astype(I32)

    ids = after(shards([0, 1]), up_other, down_other)
    acc = qkv([tokens, other_tokens], perm, ids, weights, None)
    pieces = {0: tokens}
    bit = n_tp // 2
    while bit > 1:
        pieces.update({off ^ bit: swap(p, n_tp, bit) for off, p in list(pieces.items())})
        bit //= 2
    far = [o for o in sorted(pieces) if o]

    half = HD // 2
    inv_freq = jnp.exp(jnp.arange(half, dtype=F32) * (-2.0 * math.log(ROPE_BASE) / HD))
    inv_freq = jnp.concatenate([inv_freq, inv_freq])
    step_of = jnp.tile(jnp.repeat(jnp.arange(steps, dtype=F32), SUB), row_count // SUB)
    lens = after(lens, first)
    angles = (lens + step_of[:, None]) * inv_freq
    sign = jnp.where(jnp.arange(HD) < half, -1.0, 1.0).astype(F32)
    table = jnp.concatenate([jnp.cos(angles), jnp.sin(angles) * sign, lens], axis=1)

    got = [recv[j] for j in seq]
    got, acc, table = lax.optimization_barrier((got, acc, table))
    part = mid(got, down, down_other, n_tok, rank)
    bit = 2
    while bit < n_tp // 2:
        part = part + swap(part, n_tp, bit)
        bit *= 2
    sent = up(part, swap(part, n_tp, bit), got, up_rows, up_other, n_tok, rank)
    back = {j: cross(x, j) for j, x in zip(seq, sent)}
    late = {}
    for o in far:
        x = after(pieces[o], sent[0])
        late[o] = x
        late[o ^ 1] = swap(x, n_tp, 1)
    ids = after(shards(sorted(late)), back[0])
    q, k, v = qkv([late[o] for o in sorted(late)], perm, ids, weights, acc)

    def attend(plan, loras, core_id, prev):
        return attention(
            plan, steps, core_id, rows, q, k, v, table, cache_key, cache_value, loras, prev
        )

    if n_grp == n_blocks:
        core_id = core.astype(I32).reshape(1)
        own = {j: after(back[j], q) for j in seq}
        other = {j: swap(own[j], n_tp, 1) for j in seq}
        plan = [(j, o) for j in seq for o in (False, True)]
        placed = [(seq.index(j), o) for j, o in plan]
        return attend(placed, [(other if o else own)[j] for j, o in plan], core_id, None)

    pairs = [(back[j], swap(back[j], n_tp, 1)) for j in seq]
    mine_all = jnp.stack([a[:n_tok] for a, _ in pairs])
    other_all = jnp.stack([a[n_tok:] for _, a in pairs])
    even = jnp.where(core == 0, mine_all, other_all)
    odd = jnp.where(core == 0, other_all, mine_all)
    full = jnp.stack([even, odd], axis=1).reshape(n_grp, n_tok, even.shape[2])
    span = jnp.arange(pool_slot.shape[0], dtype=I32)
    pos = jnp.sum(jnp.where(adapter_id[:, None] == span[None, :], pool_slot[None, :], 0), axis=1)
    key = lax.bitwise_xor(lax.div(pos, adp_rows), lax.axis_index("grp"))
    order = jnp.array([2 * j + c for j in seq for c in (0, 1)], I32)
    used = jnp.any(key[:, None] == order[None, :], axis=0)
    at = jnp.cumsum(used.astype(I32)) - 1
    pick = (at[None, :] == jnp.arange(n_blocks)[:, None]) & used[None, :]
    chosen = full[jnp.sum(jnp.where(pick, jnp.arange(n_grp)[None, :], 0), axis=1)]
    twice = jnp.concatenate([chosen, chosen], axis=1)
    plan = [(b // 2, b % 2 == 1) for b in range(n_blocks)]
    return attend(plan, [twice[b] for b in range(n_blocks)], jnp.zeros((1,), I32), None)


def solution(mesh):
    in_specs = (
        P("grp", None, "tp"),
        P("grp"),
        P(),
        P("grp"),
        P(None, "tp"),
        P(None, "tp"),
        P(None, "tp"),
        P("grp", "tp", None),
        P("grp", None, "tp"),
        P("grp", None, "tp"),
        P("grp", None, "tp"),
    )
    out_specs = P("grp", None, "tp")
    return jax.shard_map(body, mesh=mesh, in_specs=in_specs, out_specs=out_specs, check_vma=False)
```

time: 93.1 us -> 88 us (0.945)
  Pallas kernels: 47.6 us -> 45.1 us
  local copies, waits for them, and re-layouts: 7.3 us -> 5.54 us
    unnamed x34 -> x30, local copies, waits for them, and re-layouts: 7.12 us -> 4.1 us
    pallas_call x3, Pallas kernels: 38.3 us -> 35.3 us  [the longest x2 27 us: qkv(): pl.pallas_call(functools.partial(qkv_kernel, n_x, has_acc, plan), out_sha...]
    pallas_call x1, Pallas kernels: 1.43 us -> 3.07 us  [pack(): pl.pallas_call(functools.partial(pack_kernel, n_tok), out_shape=out, in_s...]
    pallas_call x1, Pallas kernels: 2.86 us -> 1.27 us  [up(): pl.pallas_call(functools.partial(up_kernel, n_tok, rank, n), out_shape=[o...]
    pallas_call x1, Pallas kernels: 0.55 us -> 1.91 us  [route(): pl.pallas_call(functools.partial(route_kernel, adp_rows, seq, steps), out...]
    squeeze x0 -> x1, local copies, waits for them, and re-layouts: none -> 1.25 us  [body(): rows = rows[0]]
    pallas_call x1, Pallas kernels: 4.41 us -> 3.44 us  [mid(): pl.pallas_call(functools.partial(mid_kernel, n_tok, rank), out_shape=jax....]
  transfers between devices with their start and end apart: 18 -> 18, of which waited for: 5 -> 6; matrix products, arithmetic and copies ran while one was open for 3% -> 5% of each run, Pallas kernels for 39% -> 38%
where the time goes in v3:
time: 88 us; the launch traced here: 87.7 us
  Pallas kernels  45.1 us (51%)
  starting transfers between devices  21.6 us (25%)
  waiting for transfers between devices  12.5 us (14%)
  local copies, waits for them, and re-layouts  5.54 us (6%)
  other arithmetic  2.65 us (3%)
    pallas_call x2, Pallas kernels, qkv(): pl.pallas_call(functools.partial(qkv_kernel, n_x, has_acc, plan), out_sha...  27 us
    ppermute x8, starting transfers between devices, cross(): return lax.ppermute(x, ('grp', 'tp'), perm)  17.5 us
    pallas_call x1, Pallas kernels, attention(): pl.pallas_call(make_attn_kernel(plan, steps, group, bool(extra)), out_sha...  8.33 us
    ppermute x8, waiting for transfers between devices, cross(): return lax.ppermute(x, ('grp', 'tp'), perm)  7.87 us
    ppermute x10, waiting for transfers between devices, swap(): return lax.ppermute(x, 'tp', [(i, i ^ bit) for i in range(n)])  4.59 us
    ppermute x10, starting transfers between devices, swap(): return lax.ppermute(x, 'tp', [(i, i ^ bit) for i in range(n)])  4.11 us
    unnamed x30, local copies, waits for them, and re-layouts  4.1 us
    pallas_call x1, Pallas kernels, mid(): pl.pallas_call(functools.partial(mid_kernel, n_tok, rank), out_shape=jax....  3.44 us
  transfers between devices with their start and end apart: 18, of which 6 were waited for; matrix products, arithmetic and copies ran while one was open for 5% of the time, Pallas kernels for 38%

profile of v3, /device:TPU:9, one launch (start us, length us, event | category | flops | bytes accessed | tf_op | source)
XLA Modules:
  0.0 87.7 jit_solution(1277910594506158611)
XLA Ops:
  0.7 1.9 %route.1 = (bf16[256,256]{1,0:T(8,128)(2,1)}, bf16[128,256]{1,0:T(8,128)(2,1)}, bf16[64,128]{1,0:T(8,128)(2,1)}, f32[256,128]{1,0:T(8,128)}, s32[8,64]{1,0:T(8,128)}) custom-call(s32[1,64]{1,0:T(1,128)} %bitcast.18, s32[1,64]{1,0:T(1,128)} %bitcast.19, s32[1,64]{1,0:T(1,128)} %bitcast.20), custom_call_target="tpu_custom_call" | custom-call | tf_op jit(solution)/shard_map/route/pallas_call | solution.py:137
  3.2 1.0 %copy-done.4 = bf16[64,4,2048]{2,1,0:T(4,128)(2,1)} copy-done((bf16[64,4,2048]{2,1,0:T(4,128)(2,1)}, bf16[64,4,2048]{2,1,0:T(4,128)(2,1)S(1)}, u32[]{:S(2)}) %copy-start.4) | copy-done | bytes 1048600
  4.1 3.1 %pack.1 = (bf16[1040,128]{1,0:T(8,128)(2,1)}, bf16[1040,128]{1,0:T(8,128)(2,1)}, bf16[1040,128]{1,0:T(8,128)(2,1)}, bf16[1040,128]{1,0:T(8,128)(2,1)}) custom-call(bf16[128,256]{1,0:T(8,128)(2,1)} %get-tuple-element.43.send_ref, bf16[64,128]{1,0:T(8,128)(2,1)} %get-tuple-element.44.slot_ref, bf16[64,4,2048]{2,1,0:T(4,128)(2,1)} %refs_0_.1, ...), custom_call_target="tpu_custom_call" | custom-call | tf_op jit(solution)/shard_map/pack/pallas_call | solution.py:165
  7.7 1.2 %collective-permute-start.9 = (bf16[64,4,2048]{2,1,0:T(4,128)(2,1)}, bf16[64,4,2048]{2,1,0:T(4,128)(2,1)}, u32[]{:S(2)}, u32[]{:S(2)}) collective-permute-start(bf16[64,4,2048]{2,1,0:T(4,128)(2,1)} %refs_0_.1), channel_id=1, source_target_pairs={{0,2},{1,3},{2,0},{3,1},{4,6},{5,7},{6,4},{7,5},{8,10},{9,11},{10,... | collective-permute-start | bytes 3145736 | tf_op jit(solution)/shard_map/ppermute | solution.py:510
  8.9 3.1 %collective-permute-start.5 = (bf16[1040,128]{1,0:T(8,128)(2,1)}, bf16[1040,128]{1,0:T(8,128)(2,1)S(1)}, u32[]{:S(2)}, u32[]{:S(2)}) collective-permute-start(bf16[1040,128]{1,0:T(8,128)(2,1)} %get-tuple-element.45), channel_id=1, source_target_pairs={{0,0},{1,5},{2,2},{3,7},{4,4},{5,1},{6,6},{7,3},{8,8},{9,13},{10,1... | collective-permute-start | bytes 798728 | tf_op jit(solution)/shard_map/ppermute | solution.py:547
  13.0 2.3 %collective-permute-start.3 = (bf16[1040,128]{1,0:T(8,128)(2,1)}, bf16[1040,128]{1,0:T(8,128)(2,1)S(1)}, u32[]{:S(2)}, u32[]{:S(2)}) collective-permute-start(bf16[1040,128]{1,0:T(8,128)(2,1)} %get-tuple-element.48), channel_id=1, source_target_pairs={{0,16},{1,21},{2,18},{3,23},{4,20},{5,17},{6,22},{7,19},{8,24},{9,... | collective-permute-start | bytes 798728 | tf_op jit(solution)/shard_map/ppermute | solution.py:547
  15.3 1.4 %collective-permute-done.5.refs_2_ = bf16[1040,128]{1,0:T(8,128)(2,1)S(1)} collective-permute-done((bf16[1040,128]{1,0:T(8,128)(2,1)}, bf16[1040,128]{1,0:T(8,128)(2,1)S(1)}, u32[]{:S(2)}, u32[]{:S(2)}) %collective-permute-start.5) | collective-permute-done | bytes 266272 | tf_op jit(solution)/shard_map/ppermute | solution.py:547
  16.7 2.3 %collective-permute-start.4 = (bf16[1040,128]{1,0:T(8,128)(2,1)}, bf16[1040,128]{1,0:T(8,128)(2,1)S(1)}, u32[]{:S(2)}, u32[]{:S(2)}) collective-permute-start(bf16[1040,128]{1,0:T(8,128)(2,1)} %get-tuple-element.49), channel_id=1, source_target_pairs={{0,24},{1,29},{2,26},{3,31},{4,28},{5,25},{6,30},{7,27},{8,16},{9,... | collective-permute-start | bytes 798728 | tf_op jit(solution)/shard_map/ppermute | solution.py:547
  20.3 1.4 %copy-done.2 = bf16[512,2048]{1,0:T(8,128)(2,1)} copy-done((bf16[512,2048]{1,0:T(8,128)(2,1)}, bf16[512,2048]{1,0:T(8,128)(2,1)S(1)}, u32[]{:S(2)}) %copy-start.2) | copy-done | bytes 2097176
  21.7 2.1 %collective-permute-start.6 = (bf16[1040,128]{1,0:T(8,128)(2,1)}, bf16[1040,128]{1,0:T(8,128)(2,1)S(1)}, u32[]{:S(2)}, u32[]{:S(2)}) collective-permute-start(bf16[1040,128]{1,0:T(8,128)(2,1)} %get-tuple-element.50), channel_id=1, source_target_pairs={{0,8},{1,13},{2,10},{3,15},{4,12},{5,9},{6,14},{7,11},{8,0},{9,5},... | collective-permute-start | bytes 798728 | tf_op jit(solution)/shard_map/ppermute | solution.py:547
  23.8 13.1 %qkv.2 = (f32[256,2048]{1,0:T(8,128)}, f32[256,256]{1,0:T(8,128)}, f32[256,256]{1,0:T(8,128)}) custom-call(s32[2]{0:T(128)} %pad_add_fusion.1.ids_ref, bf16[256,256]{1,0:T(8,128)(2,1)} %get-tuple-element.52.perm_ref, bf16[64,4,2048]{2,1,0:T(4,128)(2,1)} %refs_0_.1, bf16[64,4,2048]{2,1,0:T(4,128)(2,1)} %copy-done.4, bf16[8192,2048]{1,0:T(8,128)(2,1)} %refs_2_.3, ...), custom_call_target="tpu_custom_call" | custom-call | flops 10000000000 | bytes 30000000 | tf_op jit(solution)/shard_map/qkv/pallas_call | solution.py:236
  37.0 1.9 %collective-permute-done.4.refs_1_ = bf16[1040,128]{1,0:T(8,128)(2,1)S(1)} collective-permute-done((bf16[1040,128]{1,0:T(8,128)(2,1)}, bf16[1040,128]{1,0:T(8,128)(2,1)S(1)}, u32[]{:S(2)}, u32[]{:S(2)}) %collective-permute-start.4) | collective-permute-done | bytes 266272 | tf_op jit(solution)/shard_map/ppermute | solution.py:547
  38.9 3.4 %mid.1.a_ref = f32[128,128]{1,0:T(8,128)S(1)} custom-call(bf16[512,2048]{1,0:T(8,128)(2,1)S(1)} %bitcast.15, bf16[512,2048]{1,0:T(8,128)(2,1)} %collective-permute-done.2.oth_ref, bf16[1040,128]{1,0:T(8,128)(2,1)S(1)} %collective-permute-done.3.refs_0_, bf16[1040,128]{1,0:T(8,128)(2,1)S(1)} %collective-permute-done.4.refs_1_, ...), custom_call_target="tpu_custom_call" | custom-call | flops 10000000000 | bytes 30000000 | tf_op jit(solution)/shard_map/mid/pallas_call | solution.py:296
  42.7 3.6 %collective-permute-done.7.b_ref = f32[128,128]{1,0:T(8,128)S(1)} collective-permute-done((f32[128,128]{1,0:T(8,128)S(1)}, f32[128,128]{1,0:T(8,128)S(1)}, u32[]{:S(2)}, u32[]{:S(2)}) %collective-permute-start.7) | collective-permute-done | bytes 65568 | tf_op jit(solution)/shard_map/ppermute | solution.py:510
  46.3 1.3 %up.1 = (bf16[64,2048]{1,0:T(8,128)(2,1)S(1)}, bf16[64,2048]{1,0:T(8,128)(2,1)S(1)}, bf16[64,2048]{1,0:T(8,128)(2,1)S(1)}, bf16[64,2048]{1,0:T(8,128)(2,1)S(1)}) custom-call(bf16[512,2048]{1,0:T(8,128)(2,1)S(1)} %bitcast.17, bf16[512,2048]{1,0:T(8,128)(2,1)S(1)} %copy-done.3, f32[128,128]{1,0:T(8,128)S(1)} %mid.1.a_ref, ...), custom_call_target="tpu_custom_call" | custom-call | flops 10000000000 | bytes 30000000 | tf_op jit(solution)/shard_map/up/pallas_call | solution.py:342
  48.3 3.0 %collective-permute-start.8 = (bf16[64,2048]{1,0:T(8,128)(2,1)S(1)}, bf16[64,2048]{1,0:T(8,128)(2,1)S(1)}, u32[]{:S(2)}, u32[]{:S(2)}) collective-permute-start(bf16[64,2048]{1,0:T(8,128)(2,1)S(1)} %get-tuple-element.62), channel_id=1, source_target_pairs={{0,0},{1,5},{2,2},{3,7},{4,4},{5,1},{6,6},{7,3},{8,8},{9,13},{10,1... | collective-permute-start | bytes 786440 | tf_op jit(solution)/shard_map/ppermute | solution.py:547
  51.9 1.1 %collective-permute-start.11 = (bf16[64,2048]{1,0:T(8,128)(2,1)S(1)}, bf16[64,2048]{1,0:T(8,128)(2,1)S(1)}, u32[]{:S(2)}, u32[]{:S(2)}) collective-permute-start(bf16[64,2048]{1,0:T(8,128)(2,1)S(1)} %get-tuple-element.64), channel_id=1, source_target_pairs={{0,16},{1,21},{2,18},{3,23},{4,20},{5,17},{6,22},{7,19},{8,24},{9,... | collective-permute-start | bytes 786440 | tf_op jit(solution)/shard_map/ppermute | solution.py:547
  53.0 1.4 %collective-permute-start.13 = (bf16[64,2048]{1,0:T(8,128)(2,1)S(1)}, bf16[64,2048]{1,0:T(8,128)(2,1)S(1)}, u32[]{:S(2)}, u32[]{:S(2)}) collective-permute-start(bf16[64,2048]{1,0:T(8,128)(2,1)S(1)} %get-tuple-element.74), channel_id=1, source_target_pairs={{0,24},{1,29},{2,26},{3,31},{4,28},{5,25},{6,30},{7,27},{8,16},{9,... | collective-permute-start | bytes 786440 | tf_op jit(solution)/shard_map/ppermute | solution.py:547
  54.5 2.1 %collective-permute-start.16 = (bf16[64,2048]{1,0:T(8,128)(2,1)S(1)}, bf16[64,2048]{1,0:T(8,128)(2,1)S(1)}, u32[]{:S(2)}, u32[]{:S(2)}) collective-permute-start(bf16[64,2048]{1,0:T(8,128)(2,1)S(1)} %get-tuple-element.77), channel_id=1, source_target_pairs={{0,8},{1,13},{2,10},{3,15},{4,12},{5,9},{6,14},{7,11},{8,0},{9,5},... | collective-permute-start | bytes 786440 | tf_op jit(solution)/shard_map/ppermute | solution.py:547
  56.6 1.0 %copy-done.5 = bf16[64,4,2048]{2,1,0:T(4,128)(2,1)} copy-done((bf16[64,4,2048]{2,1,0:T(4,128)(2,1)}, bf16[64,4,2048]{2,1,0:T(4,128)(2,1)S(1)}, u32[]{:S(2)}) %copy-start.5) | copy-done | bytes 1048600
  57.6 13.9 %qkv.3 = (f32[256,2048]{1,0:T(8,128)}, f32[256,256]{1,0:T(8,128)}, f32[256,256]{1,0:T(8,128)}) custom-call(s32[2]{0:T(128)} %pad_add_fusion.ids_ref, bf16[256,256]{1,0:T(8,128)(2,1)} %get-tuple-element.52.perm_ref, bf16[64,4,2048]{2,1,0:T(4,128)(2,1)} %collective-permute-done.9.refs_0_, bf16[64,4,2048]{2,1,0:T(4,128)(2,1)} %copy-done.5, ...), custom_call_target="tpu_custom_call" | custom-call | flops 10000000000 | bytes 30000000 | tf_op jit(solution)/shard_map/qkv/pallas_call | solution.py:236
  71.6 4.5 %collective-permute-done.13.refs_10_ = bf16[64,2048]{1,0:T(8,128)(2,1)S(1)} collective-permute-done((bf16[64,2048]{1,0:T(8,128)(2,1)S(1)}, bf16[64,2048]{1,0:T(8,128)(2,1)S(1)}, u32[]{:S(2)}, u32[]{:S(2)}) %collective-permute-start.13) | collective-permute-done | bytes 262176 | tf_op jit(solution)/shard_map/ppermute | solution.py:547
  76.7 1.3 %slice_bitcast_fusion.refs_1_ = s32[64]{0:T(128)} fusion(s32[8,64]{1,0:T(8,128)} %get-tuple-element.42), kind=kLoop, calls=%fused_computation.9 | loop fusion | bytes 512 | tf_op jit(solution)/shard_map/squeeze | solution.py:551
  79.2 8.3 %attn.1 = bf16[64,4,2048]{2,1,0:T(4,128)(2,1)} custom-call(s32[1]{0:T(128)} %bitcast.refs_0_, s32[64]{0:T(128)} %slice_bitcast_fusion.refs_1_, f32[256,2048]{1,0:T(8,128)} %get-tuple-element.69.refs_2_, f32[256,256]{1,0:T(8,128)} %get-tuple-element.70.refs_3_, f32[256,256]{1,0:T(8,128)} %get-tuple-element.71.refs_4_, f32[256,384]{1,0:T(8,128)} %pad_maximum_fusion.refs_5_, ...), custom_call_target="tpu_custom_call" | custom-call | flops 1 | bytes 1 | tf_op jit(solution)/shard_map/attn/pallas_call | solution.py:485
  (60 shorter events, 7.5 us)
Async XLA Ops:
  0.0 3.2 %collective-permute-start = (bf16[64,4,2048]{2,1,0:T(4,128)(2,1)}, bf16[64,4,2048]{2,1,0:T(4,128)(2,1)S(1)}, u32[]{:S(2)}, u32[]{:S(2)}) collective-permute-start(bf16[64,4,2048]{2,1,0:T(4,128)(2,1)} %refs_0_.1), channel_id=1, source_target_pairs={{0,1},{1,0},{2,3},{3,2},{4,5},{5,4},{6,7},{7,6},{8,9},{9,8},{10,11... | collective-permute-start | bytes 3145736 | tf_op jit(solution)/shard_map/ppermute | solution.py:510
  2.6 16.4 %copy-start.6 = (f32[256,128]{1,0:T(8,128)S(1)}, f32[256,128]{1,0:T(8,128)}, u32[]{:S(2)}) copy-start(f32[256,128]{1,0:T(8,128)} %get-tuple-element.57) | copy-start | bytes 393220
  7.2 13.1 %collective-permute-start.1 = (bf16[512,2048]{1,0:T(8,128)(2,1)}, bf16[512,2048]{1,0:T(8,128)(2,1)S(1)}, u32[]{:S(2)}, u32[]{:S(2)}) collective-permute-start(bf16[512,2048]{1,0:T(8,128)(2,1)} %bitcast.16), channel_id=1, source_target_pairs={{0,1},{1,0},{2,3},{3,2},{4,5},{5,4},{6,7},{7,6},{8,9},{9,8},{10,11... | collective-permute-start | bytes 6291464 | tf_op jit(solution)/shard_map/ppermute | solution.py:510
  7.6 16.2 %collective-permute-start.2 = (bf16[512,2048]{1,0:T(8,128)(2,1)}, bf16[512,2048]{1,0:T(8,128)(2,1)}, u32[]{:S(2)}, u32[]{:S(2)}) collective-permute-start(bf16[512,2048]{1,0:T(8,128)(2,1)} %bitcast.14), channel_id=1, source_target_pairs={{0,1},{1,0},{2,3},{3,2},{4,5},{5,4},{6,7},{7,6},{8,9},{9,8},{10,11... | collective-permute-start | bytes 6291464 | tf_op jit(solution)/shard_map/ppermute | solution.py:510
  7.7 39.8 %collective-permute-start.9 = (bf16[64,4,2048]{2,1,0:T(4,128)(2,1)}, bf16[64,4,2048]{2,1,0:T(4,128)(2,1)}, u32[]{:S(2)}, u32[]{:S(2)}) collective-permute-start(bf16[64,4,2048]{2,1,0:T(4,128)(2,1)} %refs_0_.1), channel_id=1, source_target_pairs={{0,2},{1,3},{2,0},{3,1},{4,6},{5,7},{6,4},{7,5},{8,10},{9,11},{10,... | collective-permute-start | bytes 3145736 | tf_op jit(solution)/shard_map/ppermute | solution.py:510
  8.9 7.8 %collective-permute-start.5 = (bf16[1040,128]{1,0:T(8,128)(2,1)}, bf16[1040,128]{1,0:T(8,128)(2,1)S(1)}, u32[]{:S(2)}, u32[]{:S(2)}) collective-permute-start(bf16[1040,128]{1,0:T(8,128)(2,1)} %get-tuple-element.45), channel_id=1, source_target_pairs={{0,0},{1,5},{2,2},{3,7},{4,4},{5,1},{6,6},{7,3},{8,8},{9,13},{10,1... | collective-permute-start | bytes 798728 | tf_op jit(solution)/shard_map/ppermute | solution.py:547
  13.0 23.9 %collective-permute-start.3 = (bf16[1040,128]{1,0:T(8,128)(2,1)}, bf16[1040,128]{1,0:T(8,128)(2,1)S(1)}, u32[]{:S(2)}, u32[]{:S(2)}) collective-permute-start(bf16[1040,128]{1,0:T(8,128)(2,1)} %get-tuple-element.48), channel_id=1, source_target_pairs={{0,16},{1,21},{2,18},{3,23},{4,20},{5,17},{6,22},{7,19},{8,24},{9,... | collective-permute-start | bytes 798728 | tf_op jit(solution)/shard_map/ppermute | solution.py:547
  16.7 22.2 %collective-permute-start.4 = (bf16[1040,128]{1,0:T(8,128)(2,1)}, bf16[1040,128]{1,0:T(8,128)(2,1)S(1)}, u32[]{:S(2)}, u32[]{:S(2)}) collective-permute-start(bf16[1040,128]{1,0:T(8,128)(2,1)} %get-tuple-element.49), channel_id=1, source_target_pairs={{0,24},{1,29},{2,26},{3,31},{4,28},{5,25},{6,30},{7,27},{8,16},{9,... | collective-permute-start | bytes 798728 | tf_op jit(solution)/shard_map/ppermute | solution.py:547
  21.7 17.2 %collective-permute-start.6 = (bf16[1040,128]{1,0:T(8,128)(2,1)}, bf16[1040,128]{1,0:T(8,128)(2,1)S(1)}, u32[]{:S(2)}, u32[]{:S(2)}) collective-permute-start(bf16[1040,128]{1,0:T(8,128)(2,1)} %get-tuple-element.50), channel_id=1, source_target_pairs={{0,8},{1,13},{2,10},{3,15},{4,12},{5,9},{6,14},{7,11},{8,0},{9,5},... | collective-permute-start | bytes 798728 | tf_op jit(solution)/shard_map/ppermute | solution.py:547
  23.8 15.1 %copy-start = (bf16[8,2048,64]{1,2,0:T(8,128)(2,1)S(1)}, bf16[8,2048,64]{1,2,0:T(8,128)(2,1)}, u32[]{:S(2)}) copy-start(bf16[8,2048,64]{1,2,0:T(8,128)(2,1)} %param.18) | copy-start | bytes 6291460
  38.9 7.4 %copy-start.1 = (bf16[8,64,2048]{2,1,0:T(8,128)(2,1)S(1)}, bf16[8,64,2048]{2,1,0:T(8,128)(2,1)}, u32[]{:S(2)}) copy-start(bf16[8,64,2048]{2,1,0:T(8,128)(2,1)} %param.19) | copy-start | bytes 6291460
  38.9 7.4 %copy-start.3 = (bf16[512,2048]{1,0:T(8,128)(2,1)S(1)}, bf16[512,2048]{1,0:T(8,128)(2,1)}, u32[]{:S(2)}) copy-start(bf16[512,2048]{1,0:T(8,128)(2,1)} %copy-done.2) | copy-start | bytes 6291460
  42.4 3.9 %collective-permute-start.7 = (f32[128,128]{1,0:T(8,128)S(1)}, f32[128,128]{1,0:T(8,128)S(1)}, u32[]{:S(2)}, u32[]{:S(2)}) collective-permute-start(f32[128,128]{1,0:T(8,128)S(1)} %mid.1.a_ref), channel_id=1, source_target_pairs={{0,2},{1,3},{2,0},{3,1},{4,6},{5,7},{6,4},{7,5},{8,10},{9,11},{10,... | collective-permute-start | bytes 196616 | tf_op jit(solution)/shard_map/ppermute | solution.py:510
  47.6 9.0 %collective-permute-start.10 = (bf16[64,4,2048]{2,1,0:T(4,128)(2,1)}, bf16[64,4,2048]{2,1,0:T(4,128)(2,1)S(1)}, u32[]{:S(2)}, u32[]{:S(2)}) collective-permute-start(bf16[64,4,2048]{2,1,0:T(4,128)(2,1)} %collective-permute-done.9.refs_0_), channel_id=1, source_target_pairs={{0,1},{1,0},{2,3},{3,2},{4,5},{5,4},{6,7},{7,6},{8,9},{9,8},{10,11... | collective-permute-start | bytes 3145736 | tf_op jit(solution)/shard_map/ppermute | solution.py:510
  48.3 8.3 %collective-permute-start.8 = (bf16[64,2048]{1,0:T(8,128)(2,1)S(1)}, bf16[64,2048]{1,0:T(8,128)(2,1)S(1)}, u32[]{:S(2)}, u32[]{:S(2)}) collective-permute-start(bf16[64,2048]{1,0:T(8,128)(2,1)S(1)} %get-tuple-element.62), channel_id=1, source_target_pairs={{0,0},{1,5},{2,2},{3,7},{4,4},{5,1},{6,6},{7,3},{8,8},{9,13},{10,1... | collective-permute-start | bytes 786440 | tf_op jit(solution)/shard_map/ppermute | solution.py:547
  51.9 19.6 %collective-permute-start.11 = (bf16[64,2048]{1,0:T(8,128)(2,1)S(1)}, bf16[64,2048]{1,0:T(8,128)(2,1)S(1)}, u32[]{:S(2)}, u32[]{:S(2)}) collective-permute-start(bf16[64,2048]{1,0:T(8,128)(2,1)S(1)} %get-tuple-element.64), channel_id=1, source_target_pairs={{0,16},{1,21},{2,18},{3,23},{4,20},{5,17},{6,22},{7,19},{8,24},{9,... | collective-permute-start | bytes 786440 | tf_op jit(solution)/shard_map/ppermute | solution.py:547
  53.0 23.1 %collective-permute-start.13 = (bf16[64,2048]{1,0:T(8,128)(2,1)S(1)}, bf16[64,2048]{1,0:T(8,128)(2,1)S(1)}, u32[]{:S(2)}, u32[]{:S(2)}) collective-permute-start(bf16[64,2048]{1,0:T(8,128)(2,1)S(1)} %get-tuple-element.74), channel_id=1, source_target_pairs={{0,24},{1,29},{2,26},{3,31},{4,28},{5,25},{6,30},{7,27},{8,16},{9,... | collective-permute-start | bytes 786440 | tf_op jit(solution)/shard_map/ppermute | solution.py:547
  54.5 22.2 %collective-permute-start.16 = (bf16[64,2048]{1,0:T(8,128)(2,1)S(1)}, bf16[64,2048]{1,0:T(8,128)(2,1)S(1)}, u32[]{:S(2)}, u32[]{:S(2)}) collective-permute-start(bf16[64,2048]{1,0:T(8,128)(2,1)S(1)} %get-tuple-element.77), channel_id=1, source_target_pairs={{0,8},{1,13},{2,10},{3,15},{4,12},{5,9},{6,14},{7,11},{8,0},{9,5},... | collective-permute-start | bytes 786440 | tf_op jit(solution)/shard_map/ppermute | solution.py:547
  56.6 19.5 %copy-start.7 = (bf16[64,2048]{1,0:T(8,128)(2,1)}, bf16[64,2048]{1,0:T(8,128)(2,1)S(1)}, u32[]{:S(2)}) copy-start(bf16[64,2048]{1,0:T(8,128)(2,1)S(1)} %collective-permute-done.8.refs_12_) | copy-start | bytes 786436
  71.5 7.6 %copy-start.8 = (bf16[64,2048]{1,0:T(8,128)(2,1)}, bf16[64,2048]{1,0:T(8,128)(2,1)S(1)}, u32[]{:S(2)}) copy-start(bf16[64,2048]{1,0:T(8,128)(2,1)S(1)} %collective-permute-done.11.refs_8_) | copy-start | bytes 786436
  71.5 6.4 %collective-permute-start.12 = (bf16[64,2048]{1,0:T(8,128)(2,1)S(1)}, bf16[64,2048]{1,0:T(8,128)(2,1)S(1)}, u32[]{:S(2)}, u32[]{:S(2)}) collective-permute-start(bf16[64,2048]{1,0:T(8,128)(2,1)S(1)} %collective-permute-done.11.refs_8_), channel_id=1, source_target_pairs={{0,1},{1,0},{2,3},{3,2},{4,5},{5,4},{6,7},{7,6},{8,9},{9,8},{10,11... | collective-permute-start | bytes 786440 | tf_op jit(solution)/shard_map/ppermute | solution.py:510
  76.1 1.9 %collective-permute-start.14 = (bf16[64,2048]{1,0:T(8,128)(2,1)S(1)}, bf16[64,2048]{1,0:T(8,128)(2,1)S(1)}, u32[]{:S(2)}, u32[]{:S(2)}) collective-permute-start(bf16[64,2048]{1,0:T(8,128)(2,1)S(1)} %collective-permute-done.13.refs_10_), channel_id=1, source_target_pairs={{0,1},{1,0},{2,3},{3,2},{4,5},{5,4},{6,7},{7,6},{8,9},{9,8},{10,11... | collective-permute-start | bytes 786440 | tf_op jit(solution)/shard_map/ppermute | solution.py:510
  76.1 1.9 %collective-permute-start.15 = (bf16[64,2048]{1,0:T(8,128)(2,1)S(1)}, bf16[64,2048]{1,0:T(8,128)(2,1)S(1)}, u32[]{:S(2)}, u32[]{:S(2)}) collective-permute-start(bf16[64,2048]{1,0:T(8,128)(2,1)S(1)} %collective-permute-done.8.refs_12_), channel_id=1, source_target_pairs={{0,1},{1,0},{2,3},{3,2},{4,5},{5,4},{6,7},{7,6},{8,9},{9,8},{10,11... | collective-permute-start | bytes 786440 | tf_op jit(solution)/shard_map/ppermute | solution.py:510
  76.7 1.8 %collective-permute-start.17 = (bf16[64,2048]{1,0:T(8,128)(2,1)S(1)}, bf16[64,2048]{1,0:T(8,128)(2,1)S(1)}, u32[]{:S(2)}, u32[]{:S(2)}) collective-permute-start(bf16[64,2048]{1,0:T(8,128)(2,1)S(1)} %collective-permute-done.16.refs_14_), channel_id=1, source_target_pairs={{0,1},{1,0},{2,3},{3,2},{4,5},{5,4},{6,7},{7,6},{8,9},{9,8},{10,11... | collective-permute-start | bytes 786440 | tf_op jit(solution)/shard_map/ppermute | solution.py:510
  (9 other events, 12.9 us)

commit v4 on v3

--- a/solution.py
+++ b/solution.py
@@ -24,6 +24,7 @@
 TOGETHER = 2
 
 TINY = pl.CostEstimate(flops=1, bytes_accessed=1, transcendentals=0)
+QKV_COST = pl.CostEstimate(flops=10**11, bytes_accessed=3 * 10**8, transcendentals=0)
 COST = pl.CostEstimate(flops=10**10, bytes_accessed=3 * 10**7, transcendentals=0)
 VM = pl.BlockSpec(memory_space=pltpu.VMEM)
 SM = pl.BlockSpec(memory_space=pltpu.SMEM)
@@ -98,7 +99,7 @@
 
     row_perm = one_hot(sub.astype(F32) == dest_row)
     ids = jnp.broadcast_to(lane[:1].astype(F32), (8, rows)).astype(BF16)
-    row_ref[...] = dot_t(ids, row_perm).astype(I32)
+    row_ref[...] = dot_t(ids, row_perm)[:1].astype(I32)
     row_of, _ = token_place(iota((toks, rows), 0), steps)
     row_of = (row_of + lax.div(iota((toks, rows), 0), CAP * steps) * CAP).astype(F32)
     len_ref[...] = dot(one_hot(row_of == dest_row), wide(lens_col))
@@ -132,7 +133,7 @@
         jax.ShapeDtypeStruct((len(seq) * CAP * steps, toks), BF16),
         jax.ShapeDtypeStruct((len(seq) * 2 * CAP, 128), BF16),
         jax.ShapeDtypeStruct((toks, 128), F32),
-        jax.ShapeDtypeStruct((8, rows), I32),
+        jax.ShapeDtypeStruct((1, rows), I32),
     ]
     return pl.pallas_call(
         functools.partial(route_kernel, adp_rows, seq, steps),
@@ -242,7 +243,7 @@
         + [pltpu.VMEM((depth, w.shape[1]), BF16) for w in weights]
         + [pltpu.SemaphoreType.DMA((n_x,)), pltpu.SemaphoreType.DMA((len(plan), 3))],
         compiler_params=params(60.5),
-        cost_estimate=COST,
+        cost_estimate=QKV_COST,
         name="qkv",
     )(shards, perm, *xs, *weights, *extra)
 
@@ -384,7 +385,7 @@
 
         def begin(b):
             for i in range(CAP):
-                r = rows_ref[blocks[b] * CAP + i]
+                r = rows_ref[0, blocks[b] * CAP + i]
                 pltpu.make_async_copy(ck_ref.at[r], kbuf.at[b, i], sem.at[b, 5]).start()
                 pltpu.make_async_copy(cv_ref.at[r], vbuf.at[b, i], sem.at[b, 6]).start()
             for c in copies(b):
@@ -467,7 +468,7 @@
                     mixed = dot(turn, both).astype(BF16)
                     obuf[b, :, :, h * wide : (h + 1) * wide] = mixed.reshape(CAP, steps, wide)
                 for i in range(CAP):
-                    r = rows_ref[blocks[b] * CAP + i]
+                    r = rows_ref[0, blocks[b] * CAP + i]
                     pltpu.make_async_copy(obuf.at[b, i], out_ref.at[r], osem).start()
         for b in range(nb):
             pltpu.make_async_copy(obuf.at[b], out_ref.at[pl.ds(0, CAP)], osem).wait()
@@ -548,7 +549,6 @@
 
     other_tokens = swap(tokens, n_tp, 1)
     perm, send, slot, lens, rows = route(adp_rows, seq, steps, adapter_id, lengths, pool_slot)
-    rows = rows[0]
     sends = pack(n_pairs, send, slot, tokens, other_tokens)
     recv = {j: cross(sends[j], j) for j in seq}
 
@@ -565,7 +565,7 @@
 
     ids = after(shards([0, 1]), up_other, down_other)
     acc = qkv([tokens, other_tokens], perm, ids, weights, None)
-    pieces = {0: tokens}
+    pieces = {0: after(tokens, sends[0])}
     bit = n_tp // 2
     while bit > 1:
         pieces.update({off ^ bit: swap(p, n_tp, bit) for off, p in list(pieces.items())})

time: 88 us -> 86.5 us (0.983)
  waiting for transfers between devices: 12.5 us -> 15.4 us
  starting transfers between devices: 21.6 us -> 19.2 us
  local copies, waits for them, and re-layouts: 5.54 us -> 3.29 us
    ppermute x8, starting transfers between devices: 17.5 us -> 14.2 us  [cross(): return lax.ppermute(x, ('grp', 'tp'), perm)]
    ppermute x8, waiting for transfers between devices: 7.87 us -> 10.6 us  [cross(): return lax.ppermute(x, ('grp', 'tp'), perm)]
    squeeze x1 -> x0, local copies, waits for them, and re-layouts: 1.25 us -> none  [body(): rows = rows[0]]
    unnamed x30 -> x28, local copies, waits for them, and re-layouts: 4.1 us -> 3.11 us
    ppermute x10, starting transfers between devices: 4.11 us -> 5.04 us  [swap(): return lax.ppermute(x, 'tp', [(i, i ^ bit) for i in range(n)])]
  transfers between devices with their start and end apart: 18 -> 18, of which waited for: 6 -> 8; matrix products, arithmetic and copies ran while one was open for 5% -> 3% of each run, Pallas kernels for 38% -> 39%
where the time goes in v4:
time: 86.5 us; the launch traced here: 86.2 us
  Pallas kernels  45.2 us (52%)
  starting transfers between devices  19.2 us (22%)
  waiting for transfers between devices  15.4 us (18%)
  local copies, waits for them, and re-layouts  3.29 us (4%)
  other arithmetic  2.68 us (3%)
    pallas_call x2, Pallas kernels, qkv(): pl.pallas_call(functools.partial(qkv_kernel, n_x, has_acc, plan), out_sha...  27.1 us
    ppermute x8, starting transfers between devices, cross(): return lax.ppermute(x, ('grp', 'tp'), perm)  14.2 us
    ppermute x8, waiting for transfers between devices, cross(): return lax.ppermute(x, ('grp', 'tp'), perm)  10.6 us
    pallas_call x1, Pallas kernels, attention(): pl.pallas_call(make_attn_kernel(plan, steps, group, bool(extra)), out_sha...  8.32 us
    ppermute x10, starting transfers between devices, swap(): return lax.ppermute(x, 'tp', [(i, i ^ bit) for i in range(n)])  5.04 us
    ppermute x10, waiting for transfers between devices, swap(): return lax.ppermute(x, 'tp', [(i, i ^ bit) for i in range(n)])  4.88 us
    pallas_call x1, Pallas kernels, mid(): pl.pallas_call(functools.partial(mid_kernel, n_tok, rank), out_shape=jax....  3.44 us
    unnamed x28, local copies, waits for them, and re-layouts  3.11 us
  transfers between devices with their start and end apart: 18, of which 8 were waited for; matrix products, arithmetic and copies ran while one was open for 3% of the time, Pallas kernels for 39%

profile of v4, /device:TPU:9, one launch (start us, length us, event | category | flops | bytes accessed | tf_op | source)
XLA Modules:
  0.0 86.2 jit_solution(10652975612536262990)
XLA Ops:
  0.7 1.9 %route.1 = (bf16[256,256]{1,0:T(8,128)(2,1)}, bf16[128,256]{1,0:T(8,128)(2,1)}, bf16[64,128]{1,0:T(8,128)(2,1)}, f32[256,128]{1,0:T(8,128)}, s32[1,64]{1,0:T(1,128)}) custom-call(s32[1,64]{1,0:T(1,128)} %bitcast.16, s32[1,64]{1,0:T(1,128)} %bitcast.17, s32[1,64]{1,0:T(1,128)} %bitcast.18), custom_call_target="tpu_custom_call" | custom-call | tf_op jit(solution)/shard_map/route/pallas_call | solution.py:138
  3.2 1.0 %copy-done.4 = bf16[64,4,2048]{2,1,0:T(4,128)(2,1)} copy-done((bf16[64,4,2048]{2,1,0:T(4,128)(2,1)}, bf16[64,4,2048]{2,1,0:T(4,128)(2,1)S(1)}, u32[]{:S(2)}) %copy-start.4) | copy-done | bytes 1048600
  4.1 3.1 %pack.1 = (bf16[1040,128]{1,0:T(8,128)(2,1)}, bf16[1040,128]{1,0:T(8,128)(2,1)}, bf16[1040,128]{1,0:T(8,128)(2,1)}, bf16[1040,128]{1,0:T(8,128)(2,1)}) custom-call(bf16[128,256]{1,0:T(8,128)(2,1)} %get-tuple-element.44.send_ref, bf16[64,128]{1,0:T(8,128)(2,1)} %get-tuple-element.45.slot_ref, bf16[64,4,2048]{2,1,0:T(4,128)(2,1)} %refs_0_.1, ...), custom_call_target="tpu_custom_call" | custom-call | tf_op jit(solution)/shard_map/pack/pallas_call | solution.py:166
  7.7 3.1 %collective-permute-start.5 = (bf16[1040,128]{1,0:T(8,128)(2,1)}, bf16[1040,128]{1,0:T(8,128)(2,1)S(1)}, u32[]{:S(2)}, u32[]{:S(2)}) collective-permute-start(bf16[1040,128]{1,0:T(8,128)(2,1)} %get-tuple-element.46), channel_id=1, source_target_pairs={{0,0},{1,5},{2,2},{3,7},{4,4},{5,1},{6,6},{7,3},{8,8},{9,13},{10,1... | collective-permute-start | bytes 798728 | tf_op jit(solution)/shard_map/ppermute | solution.py:548
  11.7 2.2 %collective-permute-start.3 = (bf16[1040,128]{1,0:T(8,128)(2,1)}, bf16[1040,128]{1,0:T(8,128)(2,1)S(1)}, u32[]{:S(2)}, u32[]{:S(2)}) collective-permute-start(bf16[1040,128]{1,0:T(8,128)(2,1)} %get-tuple-element.49), channel_id=1, source_target_pairs={{0,16},{1,21},{2,18},{3,23},{4,20},{5,17},{6,22},{7,19},{8,24},{9,... | collective-permute-start | bytes 798728 | tf_op jit(solution)/shard_map/ppermute | solution.py:548
  14.0 1.4 %collective-permute-done.5.refs_2_ = bf16[1040,128]{1,0:T(8,128)(2,1)S(1)} collective-permute-done((bf16[1040,128]{1,0:T(8,128)(2,1)}, bf16[1040,128]{1,0:T(8,128)(2,1)S(1)}, u32[]{:S(2)}, u32[]{:S(2)}) %collective-permute-start.5) | collective-permute-done | bytes 266272 | tf_op jit(solution)/shard_map/ppermute | solution.py:548
  15.4 1.1 %collective-permute-start.6 = (bf16[1040,128]{1,0:T(8,128)(2,1)}, bf16[1040,128]{1,0:T(8,128)(2,1)S(1)}, u32[]{:S(2)}, u32[]{:S(2)}) collective-permute-start(bf16[1040,128]{1,0:T(8,128)(2,1)} %get-tuple-element.51), channel_id=1, source_target_pairs={{0,8},{1,13},{2,10},{3,15},{4,12},{5,9},{6,14},{7,11},{8,0},{9,5},... | collective-permute-start | bytes 798728 | tf_op jit(solution)/shard_map/ppermute | solution.py:548
  17.1 0.8 pad_maximum_fusion.refs_5_
  17.9 1.4 %copy-done.2 = bf16[512,2048]{1,0:T(8,128)(2,1)} copy-done((bf16[512,2048]{1,0:T(8,128)(2,1)}, bf16[512,2048]{1,0:T(8,128)(2,1)S(1)}, u32[]{:S(2)}) %copy-start.2) | copy-done | bytes 2097176
  19.2 1.2 %collective-permute-start.9 = (bf16[64,4,2048]{2,1,0:T(4,128)(2,1)}, bf16[64,4,2048]{2,1,0:T(4,128)(2,1)}, u32[]{:S(2)}, u32[]{:S(2)}) collective-permute-start(bf16[64,4,2048]{2,1,0:T(4,128)(2,1)} %refs_0_.1), channel_id=1, source_target_pairs={{0,2},{1,3},{2,0},{3,1},{4,6},{5,7},{6,4},{7,5},{8,10},{9,11},{10,... | collective-permute-start | bytes 3145736 | tf_op jit(solution)/shard_map/ppermute | solution.py:511
  20.5 13.1 %qkv.2 = (f32[256,2048]{1,0:T(8,128)}, f32[256,256]{1,0:T(8,128)}, f32[256,256]{1,0:T(8,128)}) custom-call(s32[2]{0:T(128)} %pad_add_fusion.1.ids_ref, bf16[256,256]{1,0:T(8,128)(2,1)} %get-tuple-element.53.perm_ref, bf16[64,4,2048]{2,1,0:T(4,128)(2,1)} %refs_0_.1, bf16[64,4,2048]{2,1,0:T(4,128)(2,1)} %copy-done.4, bf16[8192,2048]{1,0:T(8,128)(2,1)} %refs_2_.3, ...), custom_call_target="tpu_custom_call" | custom-call | flops 99999997952 | bytes 300000000 | tf_op jit(solution)/shard_map/qkv/pallas_call | solution.py:237
  33.6 3.7 %collective-permute-done.4.refs_1_ = bf16[1040,128]{1,0:T(8,128)(2,1)S(1)} collective-permute-done((bf16[1040,128]{1,0:T(8,128)(2,1)}, bf16[1040,128]{1,0:T(8,128)(2,1)S(1)}, u32[]{:S(2)}, u32[]{:S(2)}) %collective-permute-start.4) | collective-permute-done | bytes 266272 | tf_op jit(solution)/shard_map/ppermute | solution.py:548
  37.4 3.4 %mid.1.a_ref = f32[128,128]{1,0:T(8,128)S(1)} custom-call(bf16[512,2048]{1,0:T(8,128)(2,1)S(1)} %bitcast.13, bf16[512,2048]{1,0:T(8,128)(2,1)} %collective-permute-done.2.oth_ref, bf16[1040,128]{1,0:T(8,128)(2,1)S(1)} %collective-permute-done.3.refs_0_, bf16[1040,128]{1,0:T(8,128)(2,1)S(1)} %collective-permute-done.4.refs_1_, ...), custom_call_target="tpu_custom_call" | custom-call | flops 10000000000 | bytes 30000000 | tf_op jit(solution)/shard_map/mid/pallas_call | solution.py:297
  40.8 1.3 %collective-permute-start.7 = (f32[128,128]{1,0:T(8,128)S(1)}, f32[128,128]{1,0:T(8,128)S(1)}, u32[]{:S(2)}, u32[]{:S(2)}) collective-permute-start(f32[128,128]{1,0:T(8,128)S(1)} %mid.1.a_ref), channel_id=1, source_target_pairs={{0,2},{1,3},{2,0},{3,1},{4,6},{5,7},{6,4},{7,5},{8,10},{9,11},{10,... | collective-permute-start | bytes 196616 | tf_op jit(solution)/shard_map/ppermute | solution.py:511
  42.1 2.6 %collective-permute-done.7.b_ref = f32[128,128]{1,0:T(8,128)S(1)} collective-permute-done((f32[128,128]{1,0:T(8,128)S(1)}, f32[128,128]{1,0:T(8,128)S(1)}, u32[]{:S(2)}, u32[]{:S(2)}) %collective-permute-start.7) | collective-permute-done | bytes 65568 | tf_op jit(solution)/shard_map/ppermute | solution.py:511
  44.8 1.3 %up.1 = (bf16[64,2048]{1,0:T(8,128)(2,1)S(1)}, bf16[64,2048]{1,0:T(8,128)(2,1)S(1)}, bf16[64,2048]{1,0:T(8,128)(2,1)S(1)}, bf16[64,2048]{1,0:T(8,128)(2,1)S(1)}) custom-call(bf16[512,2048]{1,0:T(8,128)(2,1)S(1)} %bitcast.15, bf16[512,2048]{1,0:T(8,128)(2,1)S(1)} %copy-done.3, f32[128,128]{1,0:T(8,128)S(1)} %mid.1.a_ref, ...), custom_call_target="tpu_custom_call" | custom-call | flops 10000000000 | bytes 30000000 | tf_op jit(solution)/shard_map/up/pallas_call | solution.py:343
  46.8 3.3 %collective-permute-start.8 = (bf16[64,2048]{1,0:T(8,128)(2,1)S(1)}, bf16[64,2048]{1,0:T(8,128)(2,1)S(1)}, u32[]{:S(2)}, u32[]{:S(2)}) collective-permute-start(bf16[64,2048]{1,0:T(8,128)(2,1)S(1)} %get-tuple-element.63), channel_id=1, source_target_pairs={{0,0},{1,5},{2,2},{3,7},{4,4},{5,1},{6,6},{7,3},{8,8},{9,13},{10,1... | collective-permute-start | bytes 786440 | tf_op jit(solution)/shard_map/ppermute | solution.py:548
  51.4 1.6 %collective-permute-start.13 = (bf16[64,2048]{1,0:T(8,128)(2,1)S(1)}, bf16[64,2048]{1,0:T(8,128)(2,1)S(1)}, u32[]{:S(2)}, u32[]{:S(2)}) collective-permute-start(bf16[64,2048]{1,0:T(8,128)(2,1)S(1)} %get-tuple-element.76), channel_id=1, source_target_pairs={{0,24},{1,29},{2,26},{3,31},{4,28},{5,25},{6,30},{7,27},{8,16},{9,... | collective-permute-start | bytes 786440 | tf_op jit(solution)/shard_map/ppermute | solution.py:548
  53.0 2.1 %collective-permute-start.16 = (bf16[64,2048]{1,0:T(8,128)(2,1)S(1)}, bf16[64,2048]{1,0:T(8,128)(2,1)S(1)}, u32[]{:S(2)}, u32[]{:S(2)}) collective-permute-start(bf16[64,2048]{1,0:T(8,128)(2,1)S(1)} %get-tuple-element.79), channel_id=1, source_target_pairs={{0,8},{1,13},{2,10},{3,15},{4,12},{5,9},{6,14},{7,11},{8,0},{9,5},... | collective-permute-start | bytes 786440 | tf_op jit(solution)/shard_map/ppermute | solution.py:548
  55.1 14.0 %qkv.3 = (f32[256,2048]{1,0:T(8,128)}, f32[256,256]{1,0:T(8,128)}, f32[256,256]{1,0:T(8,128)}) custom-call(s32[2]{0:T(128)} %pad_add_fusion.ids_ref, bf16[256,256]{1,0:T(8,128)(2,1)} %get-tuple-element.53.perm_ref, bf16[64,4,2048]{2,1,0:T(4,128)(2,1)} %collective-permute-done.9.refs_0_, bf16[64,4,2048]{2,1,0:T(4,128)(2,1)} %collective-permute-done.10.refs_1_, ...), custom_call_target="tpu_custom_call" | custom-call | flops 99999997952 | bytes 300000000 | tf_op jit(solution)/shard_map/qkv/pallas_call | solution.py:237
  69.2 5.4 %collective-permute-done.13.refs_10_ = bf16[64,2048]{1,0:T(8,128)(2,1)S(1)} collective-permute-done((bf16[64,2048]{1,0:T(8,128)(2,1)S(1)}, bf16[64,2048]{1,0:T(8,128)(2,1)S(1)}, u32[]{:S(2)}, u32[]{:S(2)}) %collective-permute-start.13) | collective-permute-done | bytes 262176 | tf_op jit(solution)/shard_map/ppermute | solution.py:548
  75.3 0.9 %collective-permute-done.14.refs_11_ = bf16[64,2048]{1,0:T(8,128)(2,1)S(1)} collective-permute-done((bf16[64,2048]{1,0:T(8,128)(2,1)S(1)}, bf16[64,2048]{1,0:T(8,128)(2,1)S(1)}, u32[]{:S(2)}, u32[]{:S(2)}) %collective-permute-start.14) | collective-permute-done | bytes 262176 | tf_op jit(solution)/shard_map/ppermute | solution.py:511
  76.9 0.7 copy-done.13
  77.7 8.3 %attn.1 = bf16[64,4,2048]{2,1,0:T(4,128)(2,1)} custom-call(s32[1]{0:T(128)} %bitcast.refs_0_, s32[1,64]{1,0:T(1,128)} %get-tuple-element.43.refs_1_, f32[256,2048]{1,0:T(8,128)} %get-tuple-element.71.refs_2_, f32[256,256]{1,0:T(8,128)} %get-tuple-element.72.refs_3_, f32[256,256]{1,0:T(8,128)} %get-tuple-element.73.refs_4_, ...), custom_call_target="tpu_custom_call" | custom-call | flops 1 | bytes 1 | tf_op jit(solution)/shard_map/attn/pallas_call | solution.py:486
  (57 shorter events, 6.7 us)
Async XLA Ops:
  0.0 3.2 %collective-permute-start = (bf16[64,4,2048]{2,1,0:T(4,128)(2,1)}, bf16[64,4,2048]{2,1,0:T(4,128)(2,1)S(1)}, u32[]{:S(2)}, u32[]{:S(2)}) collective-permute-start(bf16[64,4,2048]{2,1,0:T(4,128)(2,1)} %refs_0_.1), channel_id=1, source_target_pairs={{0,1},{1,0},{2,3},{3,2},{4,5},{5,4},{6,7},{7,6},{8,9},{9,8},{10,11... | collective-permute-start | bytes 3145736 | tf_op jit(solution)/shard_map/ppermute | solution.py:511
  2.6 13.9 %copy-start.5 = (f32[256,128]{1,0:T(8,128)S(1)}, f32[256,128]{1,0:T(8,128)}, u32[]{:S(2)}) copy-start(f32[256,128]{1,0:T(8,128)} %get-tuple-element.58) | copy-start | bytes 393220
  7.2 10.6 %collective-permute-start.1 = (bf16[512,2048]{1,0:T(8,128)(2,1)}, bf16[512,2048]{1,0:T(8,128)(2,1)S(1)}, u32[]{:S(2)}, u32[]{:S(2)}) collective-permute-start(bf16[512,2048]{1,0:T(8,128)(2,1)} %bitcast.14), channel_id=1, source_target_pairs={{0,1},{1,0},{2,3},{3,2},{4,5},{5,4},{6,7},{7,6},{8,9},{9,8},{10,11... | collective-permute-start | bytes 6291464 | tf_op jit(solution)/shard_map/ppermute | solution.py:511
  7.6 12.9 %collective-permute-start.2 = (bf16[512,2048]{1,0:T(8,128)(2,1)}, bf16[512,2048]{1,0:T(8,128)(2,1)}, u32[]{:S(2)}, u32[]{:S(2)}) collective-permute-start(bf16[512,2048]{1,0:T(8,128)(2,1)} %bitcast.12), channel_id=1, source_target_pairs={{0,1},{1,0},{2,3},{3,2},{4,5},{5,4},{6,7},{7,6},{8,9},{9,8},{10,11... | collective-permute-start | bytes 6291464 | tf_op jit(solution)/shard_map/ppermute | solution.py:511
  7.7 7.7 %collective-permute-start.5 = (bf16[1040,128]{1,0:T(8,128)(2,1)}, bf16[1040,128]{1,0:T(8,128)(2,1)S(1)}, u32[]{:S(2)}, u32[]{:S(2)}) collective-permute-start(bf16[1040,128]{1,0:T(8,128)(2,1)} %get-tuple-element.46), channel_id=1, source_target_pairs={{0,0},{1,5},{2,2},{3,7},{4,4},{5,1},{6,6},{7,3},{8,8},{9,13},{10,1... | collective-permute-start | bytes 798728 | tf_op jit(solution)/shard_map/ppermute | solution.py:548
  11.7 21.9 %collective-permute-start.3 = (bf16[1040,128]{1,0:T(8,128)(2,1)}, bf16[1040,128]{1,0:T(8,128)(2,1)S(1)}, u32[]{:S(2)}, u32[]{:S(2)}) collective-permute-start(bf16[1040,128]{1,0:T(8,128)(2,1)} %get-tuple-element.49), channel_id=1, source_target_pairs={{0,16},{1,21},{2,18},{3,23},{4,20},{5,17},{6,22},{7,19},{8,24},{9,... | collective-permute-start | bytes 798728 | tf_op jit(solution)/shard_map/ppermute | solution.py:548
  14.0 23.4 %collective-permute-start.4 = (bf16[1040,128]{1,0:T(8,128)(2,1)}, bf16[1040,128]{1,0:T(8,128)(2,1)S(1)}, u32[]{:S(2)}, u32[]{:S(2)}) collective-permute-start(bf16[1040,128]{1,0:T(8,128)(2,1)} %get-tuple-element.50), channel_id=1, source_target_pairs={{0,24},{1,29},{2,26},{3,31},{4,28},{5,25},{6,30},{7,27},{8,16},{9,... | collective-permute-start | bytes 798728 | tf_op jit(solution)/shard_map/ppermute | solution.py:548
  15.4 22.0 %collective-permute-start.6 = (bf16[1040,128]{1,0:T(8,128)(2,1)}, bf16[1040,128]{1,0:T(8,128)(2,1)S(1)}, u32[]{:S(2)}, u32[]{:S(2)}) collective-permute-start(bf16[1040,128]{1,0:T(8,128)(2,1)} %get-tuple-element.51), channel_id=1, source_target_pairs={{0,8},{1,13},{2,10},{3,15},{4,12},{5,9},{6,14},{7,11},{8,0},{9,5},... | collective-permute-start | bytes 798728 | tf_op jit(solution)/shard_map/ppermute | solution.py:548
  19.2 26.8 %collective-permute-start.9 = (bf16[64,4,2048]{2,1,0:T(4,128)(2,1)}, bf16[64,4,2048]{2,1,0:T(4,128)(2,1)}, u32[]{:S(2)}, u32[]{:S(2)}) collective-permute-start(bf16[64,4,2048]{2,1,0:T(4,128)(2,1)} %refs_0_.1), channel_id=1, source_target_pairs={{0,2},{1,3},{2,0},{3,1},{4,6},{5,7},{6,4},{7,5},{8,10},{9,11},{10,... | collective-permute-start | bytes 3145736 | tf_op jit(solution)/shard_map/ppermute | solution.py:511
  20.5 16.9 %copy-start = (bf16[8,2048,64]{1,2,0:T(8,128)(2,1)S(1)}, bf16[8,2048,64]{1,2,0:T(8,128)(2,1)}, u32[]{:S(2)}) copy-start(bf16[8,2048,64]{1,2,0:T(8,128)(2,1)} %param.18) | copy-start | bytes 6291460
  37.4 7.4 %copy-start.1 = (bf16[8,64,2048]{2,1,0:T(8,128)(2,1)S(1)}, bf16[8,64,2048]{2,1,0:T(8,128)(2,1)}, u32[]{:S(2)}) copy-start(bf16[8,64,2048]{2,1,0:T(8,128)(2,1)} %param.19) | copy-start | bytes 6291460
  37.4 7.4 %copy-start.3 = (bf16[512,2048]{1,0:T(8,128)(2,1)S(1)}, bf16[512,2048]{1,0:T(8,128)(2,1)}, u32[]{:S(2)}) copy-start(bf16[512,2048]{1,0:T(8,128)(2,1)} %copy-done.2) | copy-start | bytes 6291460
  40.8 3.9 %collective-permute-start.7 = (f32[128,128]{1,0:T(8,128)S(1)}, f32[128,128]{1,0:T(8,128)S(1)}, u32[]{:S(2)}, u32[]{:S(2)}) collective-permute-start(f32[128,128]{1,0:T(8,128)S(1)} %mid.1.a_ref), channel_id=1, source_target_pairs={{0,2},{1,3},{2,0},{3,1},{4,6},{5,7},{6,4},{7,5},{8,10},{9,11},{10,... | collective-permute-start | bytes 196616 | tf_op jit(solution)/shard_map/ppermute | solution.py:511
  46.1 9.1 %collective-permute-start.10 = (bf16[64,4,2048]{2,1,0:T(4,128)(2,1)}, bf16[64,4,2048]{2,1,0:T(4,128)(2,1)}, u32[]{:S(2)}, u32[]{:S(2)}) collective-permute-start(bf16[64,4,2048]{2,1,0:T(4,128)(2,1)} %collective-permute-done.9.refs_0_), channel_id=1, source_target_pairs={{0,1},{1,0},{2,3},{3,2},{4,5},{5,4},{6,7},{7,6},{8,9},{9,8},{10,11... | collective-permute-start | bytes 3145736 | tf_op jit(solution)/shard_map/ppermute | solution.py:511
  46.8 8.4 %collective-permute-start.8 = (bf16[64,2048]{1,0:T(8,128)(2,1)S(1)}, bf16[64,2048]{1,0:T(8,128)(2,1)S(1)}, u32[]{:S(2)}, u32[]{:S(2)}) collective-permute-start(bf16[64,2048]{1,0:T(8,128)(2,1)S(1)} %get-tuple-element.63), channel_id=1, source_target_pairs={{0,0},{1,5},{2,2},{3,7},{4,4},{5,1},{6,6},{7,3},{8,8},{9,13},{10,1... | collective-permute-start | bytes 786440 | tf_op jit(solution)/shard_map/ppermute | solution.py:548
  50.7 18.4 %collective-permute-start.11 = (bf16[64,2048]{1,0:T(8,128)(2,1)S(1)}, bf16[64,2048]{1,0:T(8,128)(2,1)S(1)}, u32[]{:S(2)}, u32[]{:S(2)}) collective-permute-start(bf16[64,2048]{1,0:T(8,128)(2,1)S(1)} %get-tuple-element.66), channel_id=1, source_target_pairs={{0,16},{1,21},{2,18},{3,23},{4,20},{5,17},{6,22},{7,19},{8,24},{9,... | collective-permute-start | bytes 786440 | tf_op jit(solution)/shard_map/ppermute | solution.py:548
  51.4 23.3 %collective-permute-start.13 = (bf16[64,2048]{1,0:T(8,128)(2,1)S(1)}, bf16[64,2048]{1,0:T(8,128)(2,1)S(1)}, u32[]{:S(2)}, u32[]{:S(2)}) collective-permute-start(bf16[64,2048]{1,0:T(8,128)(2,1)S(1)} %get-tuple-element.76), channel_id=1, source_target_pairs={{0,24},{1,29},{2,26},{3,31},{4,28},{5,25},{6,30},{7,27},{8,16},{9,... | collective-permute-start | bytes 786440 | tf_op jit(solution)/shard_map/ppermute | solution.py:548
  53.0 22.2 %collective-permute-start.16 = (bf16[64,2048]{1,0:T(8,128)(2,1)S(1)}, bf16[64,2048]{1,0:T(8,128)(2,1)S(1)}, u32[]{:S(2)}, u32[]{:S(2)}) collective-permute-start(bf16[64,2048]{1,0:T(8,128)(2,1)S(1)} %get-tuple-element.79), channel_id=1, source_target_pairs={{0,8},{1,13},{2,10},{3,15},{4,12},{5,9},{6,14},{7,11},{8,0},{9,5},... | collective-permute-start | bytes 786440 | tf_op jit(solution)/shard_map/ppermute | solution.py:548
  55.1 19.5 %copy-start.6 = (bf16[64,2048]{1,0:T(8,128)(2,1)}, bf16[64,2048]{1,0:T(8,128)(2,1)S(1)}, u32[]{:S(2)}) copy-start(bf16[64,2048]{1,0:T(8,128)(2,1)S(1)} %collective-permute-done.8.refs_12_) | copy-start | bytes 786436
  69.1 8.5 %copy-start.7 = (bf16[64,2048]{1,0:T(8,128)(2,1)}, bf16[64,2048]{1,0:T(8,128)(2,1)S(1)}, u32[]{:S(2)}) copy-start(bf16[64,2048]{1,0:T(8,128)(2,1)S(1)} %collective-permute-done.11.refs_8_) | copy-start | bytes 786436
  69.1 6.1 %collective-permute-start.12 = (bf16[64,2048]{1,0:T(8,128)(2,1)S(1)}, bf16[64,2048]{1,0:T(8,128)(2,1)S(1)}, u32[]{:S(2)}, u32[]{:S(2)}) collective-permute-start(bf16[64,2048]{1,0:T(8,128)(2,1)S(1)} %collective-permute-done.11.refs_8_), channel_id=1, source_target_pairs={{0,1},{1,0},{2,3},{3,2},{4,5},{5,4},{6,7},{7,6},{8,9},{9,8},{10,11... | collective-permute-start | bytes 786440 | tf_op jit(solution)/shard_map/ppermute | solution.py:511
  74.7 1.5 %collective-permute-start.14 = (bf16[64,2048]{1,0:T(8,128)(2,1)S(1)}, bf16[64,2048]{1,0:T(8,128)(2,1)S(1)}, u32[]{:S(2)}, u32[]{:S(2)}) collective-permute-start(bf16[64,2048]{1,0:T(8,128)(2,1)S(1)} %collective-permute-done.13.refs_10_), channel_id=1, source_target_pairs={{0,1},{1,0},{2,3},{3,2},{4,5},{5,4},{6,7},{7,6},{8,9},{9,8},{10,11... | collective-permute-start | bytes 786440 | tf_op jit(solution)/shard_map/ppermute | solution.py:511
  74.7 1.9 %collective-permute-start.15 = (bf16[64,2048]{1,0:T(8,128)(2,1)S(1)}, bf16[64,2048]{1,0:T(8,128)(2,1)S(1)}, u32[]{:S(2)}, u32[]{:S(2)}) collective-permute-start(bf16[64,2048]{1,0:T(8,128)(2,1)S(1)} %collective-permute-done.8.refs_12_), channel_id=1, source_target_pairs={{0,1},{1,0},{2,3},{3,2},{4,5},{5,4},{6,7},{7,6},{8,9},{9,8},{10,11... | collective-permute-start | bytes 786440 | tf_op jit(solution)/shard_map/ppermute | solution.py:511
  75.2 1.8 %collective-permute-start.17 = (bf16[64,2048]{1,0:T(8,128)(2,1)S(1)}, bf16[64,2048]{1,0:T(8,128)(2,1)S(1)}, u32[]{:S(2)}, u32[]{:S(2)}) collective-permute-start(bf16[64,2048]{1,0:T(8,128)(2,1)S(1)} %collective-permute-done.16.refs_14_), channel_id=1, source_target_pairs={{0,1},{1,0},{2,3},{3,2},{4,5},{5,4},{6,7},{7,6},{8,9},{9,8},{10,11... | collective-permute-start | bytes 786440 | tf_op jit(solution)/shard_map/ppermute | solution.py:511
  (8 other events, 13.6 us)

commit v5 on v4

--- a/solution.py
+++ b/solution.py
@@ -173,7 +173,9 @@
     )(send, slot, tokens, other)
 
 
-def qkv_kernel(n_x, has_acc, steps, ids_ref, perm_ref, *refs):
+def qkv_kernel(offsets, has_acc, steps, perm_ref, *refs):
+    n_x = len(offsets)
+    me = lax.axis_index("tp")
     xs, ws = refs[:n_x], refs[n_x : n_x + 3]
     at = n_x + 3
     accs = refs[at : at + 3] if has_acc else (None,) * 3
@@ -187,7 +189,8 @@
 
     def w_copy(n, i):
         lo, size = steps[n]
-        row = pl.multiple_of(ids_ref[lo // width] * width + lo % width, 256)
+        shard = lax.bitwise_xor(me, offsets[lo // width])
+        row = pl.multiple_of(shard * width + lo % width, 256)
         return pltpu.make_async_copy(ws[i].at[pl.ds(row, size)], bufs[i].at[lo : lo + size], wsem.at[n, i])
 
     def begin(n):
@@ -218,7 +221,7 @@
                 outs[i][...] = accs[i][...] + got if has_acc else got
 
 
-def qkv(xs, perm, shards, weights, acc):
+def qkv(xs, perm, offsets, weights, acc):
     rows, steps, width = xs[0].shape
     m = rows * steps
     n_x = len(xs)
@@ -235,9 +238,9 @@
         plan.append((at, min(STEP, width - at % width)))
         at += plan[-1][1]
     return pl.pallas_call(
-        functools.partial(qkv_kernel, n_x, has_acc, plan),
+        functools.partial(qkv_kernel, tuple(offsets), has_acc, plan),
         out_shape=outs,
-        in_specs=[SM, VM] + [HBM] * (n_x + 3) + [VM] * len(extra),
+        in_specs=[VM] + [HBM] * (n_x + 3) + [VM] * len(extra),
         out_specs=[VM] * 3,
         scratch_shapes=[pltpu.VMEM((n_x, rows, steps, width), BF16), pltpu.VMEM((m, depth), BF16)]
         + [pltpu.VMEM((depth, w.shape[1]), BF16) for w in weights]
@@ -245,7 +248,7 @@
         compiler_params=params(60.5),
         cost_estimate=QKV_COST,
         name="qkv",
-    )(shards, perm, *xs, *weights, *extra)
+    )(perm, *xs, *weights, *extra)
 
 
 def panel_loads(srcs, dst, sem):
@@ -560,11 +563,8 @@
 
     weights = (w_query, w_key, w_value)
 
-    def shards(offs):
-        return jnp.stack([lax.bitwise_xor(me, o) for o in offs]).astype(I32)
-
-    ids = after(shards([0, 1]), up_other, down_other)
-    acc = qkv([tokens, other_tokens], perm, ids, weights, None)
+    ready = after(perm, up_other, down_other)
+    acc = qkv([tokens, other_tokens], ready, [0, 1], weights, None)
     pieces = {0: after(tokens, sends[0])}
     bit = n_tp // 2
     while bit > 1:
@@ -595,8 +595,9 @@
         x = after(pieces[o], sent[0])
         late[o] = x
         late[o ^ 1] = swap(x, n_tp, 1)
-    ids = after(shards(sorted(late)), back[0])
-    q, k, v = qkv([late[o] for o in sorted(late)], perm, ids, weights, acc)
+    offsets = sorted(late)
+    ready = after(perm, back[0])
+    q, k, v = qkv([late[o] for o in offsets], ready, offsets, weights, acc)
 
     def attend(plan, loras, core_id, prev):
         return attention(

time: 86.5 us -> 85.3 us (0.986)
  other arithmetic: 2.68 us -> 1.43 us
    another operation x2 -> x0, other arithmetic: 1.25 us -> none  [shards(): return jnp.stack([lax.bitwise_xor(me, o) for o in offs]).astype(I32)]
  transfers between devices with their start and end apart: 18 -> 18, of which waited for: 8 -> 8; matrix products, arithmetic and copies ran while one was open for 3% -> 2% of each run, Pallas kernels for 39% -> 40%
where the time goes in v5:
time: 85.3 us; the launch traced here: 85 us
  Pallas kernels  45.2 us (53%)
  starting transfers between devices  19.7 us (23%)
  waiting for transfers between devices  15.2 us (18%)
  local copies, waits for them, and re-layouts  3.29 us (4%)
  other arithmetic  1.43 us (2%)
    pallas_call x2, Pallas kernels, qkv(): pl.pallas_call(functools.partial(qkv_kernel, tuple(offsets), has_acc, pla...  27.1 us
    ppermute x8, starting transfers between devices, cross(): return lax.ppermute(x, ('grp', 'tp'), perm)  14.5 us
    ppermute x8, waiting for transfers between devices, cross(): return lax.ppermute(x, ('grp', 'tp'), perm)  10.4 us
    pallas_call x1, Pallas kernels, attention(): pl.pallas_call(make_attn_kernel(plan, steps, group, bool(extra)), out_sha...  8.32 us
    ppermute x10, starting transfers between devices, swap(): return lax.ppermute(x, 'tp', [(i, i ^ bit) for i in range(n)])  5.16 us
    ppermute x10, waiting for transfers between devices, swap(): return lax.ppermute(x, 'tp', [(i, i ^ bit) for i in range(n)])  4.8 us
    pallas_call x1, Pallas kernels, mid(): pl.pallas_call(functools.partial(mid_kernel, n_tok, rank), out_shape=jax....  3.45 us
    unnamed x28, local copies, waits for them, and re-layouts  3.11 us
  transfers between devices with their start and end apart: 18, of which 8 were waited for; matrix products, arithmetic and copies ran while one was open for 2% of the time, Pallas kernels for 40%

profile of v5, /device:TPU:9, one launch (start us, length us, event | category | flops | bytes accessed | tf_op | source)
XLA Modules:
  0.0 85.0 jit_solution(4018797483962690650)
XLA Ops:
  0.7 1.9 %route.1 = (bf16[256,256]{1,0:T(8,128)(2,1)}, bf16[128,256]{1,0:T(8,128)(2,1)}, bf16[64,128]{1,0:T(8,128)(2,1)}, f32[256,128]{1,0:T(8,128)}, s32[1,64]{1,0:T(1,128)}) custom-call(s32[1,64]{1,0:T(1,128)} %bitcast.12, s32[1,64]{1,0:T(1,128)} %bitcast.13, s32[1,64]{1,0:T(1,128)} %bitcast.14), custom_call_target="tpu_custom_call" | custom-call | tf_op jit(solution)/shard_map/route/pallas_call | solution.py:138
  3.2 1.0 %copy-done.4 = bf16[64,4,2048]{2,1,0:T(4,128)(2,1)} copy-done((bf16[64,4,2048]{2,1,0:T(4,128)(2,1)}, bf16[64,4,2048]{2,1,0:T(4,128)(2,1)S(1)}, u32[]{:S(2)}) %copy-start.4) | copy-done | bytes 1048600
  4.1 3.1 %pack.1 = (bf16[1040,128]{1,0:T(8,128)(2,1)}, bf16[1040,128]{1,0:T(8,128)(2,1)}, bf16[1040,128]{1,0:T(8,128)(2,1)}, bf16[1040,128]{1,0:T(8,128)(2,1)}) custom-call(bf16[128,256]{1,0:T(8,128)(2,1)} %get-tuple-element.45.send_ref, bf16[64,128]{1,0:T(8,128)(2,1)} %get-tuple-element.46.slot_ref, bf16[64,4,2048]{2,1,0:T(4,128)(2,1)} %refs_0_.1, ...), custom_call_target="tpu_custom_call" | custom-call | tf_op jit(solution)/shard_map/pack/pallas_call | solution.py:166
  7.7 3.1 %collective-permute-start.5 = (bf16[1040,128]{1,0:T(8,128)(2,1)}, bf16[1040,128]{1,0:T(8,128)(2,1)S(1)}, u32[]{:S(2)}, u32[]{:S(2)}) collective-permute-start(bf16[1040,128]{1,0:T(8,128)(2,1)} %get-tuple-element.47), channel_id=1, source_target_pairs={{0,0},{1,5},{2,2},{3,7},{4,4},{5,1},{6,6},{7,3},{8,8},{9,13},{10,1... | collective-permute-start | bytes 798728 | tf_op jit(solution)/shard_map/ppermute | solution.py:551
  11.1 2.3 %collective-permute-start.3 = (bf16[1040,128]{1,0:T(8,128)(2,1)}, bf16[1040,128]{1,0:T(8,128)(2,1)S(1)}, u32[]{:S(2)}, u32[]{:S(2)}) collective-permute-start(bf16[1040,128]{1,0:T(8,128)(2,1)} %get-tuple-element.50), channel_id=1, source_target_pairs={{0,16},{1,21},{2,18},{3,23},{4,20},{5,17},{6,22},{7,19},{8,24},{9,... | collective-permute-start | bytes 798728 | tf_op jit(solution)/shard_map/ppermute | solution.py:551
  13.4 2.0 %collective-permute-done.5.refs_2_ = bf16[1040,128]{1,0:T(8,128)(2,1)S(1)} collective-permute-done((bf16[1040,128]{1,0:T(8,128)(2,1)}, bf16[1040,128]{1,0:T(8,128)(2,1)S(1)}, u32[]{:S(2)}, u32[]{:S(2)}) %collective-permute-start.5) | collective-permute-done | bytes 266272 | tf_op jit(solution)/shard_map/ppermute | solution.py:551
  15.4 1.3 %collective-permute-start.6 = (bf16[1040,128]{1,0:T(8,128)(2,1)}, bf16[1040,128]{1,0:T(8,128)(2,1)S(1)}, u32[]{:S(2)}, u32[]{:S(2)}) collective-permute-start(bf16[1040,128]{1,0:T(8,128)(2,1)} %get-tuple-element.52), channel_id=1, source_target_pairs={{0,8},{1,13},{2,10},{3,15},{4,12},{5,9},{6,14},{7,11},{8,0},{9,5},... | collective-permute-start | bytes 798728 | tf_op jit(solution)/shard_map/ppermute | solution.py:551
  17.3 0.8 pad_maximum_fusion.refs_5_
  18.1 1.4 %copy-done.2 = bf16[512,2048]{1,0:T(8,128)(2,1)} copy-done((bf16[512,2048]{1,0:T(8,128)(2,1)}, bf16[512,2048]{1,0:T(8,128)(2,1)S(1)}, u32[]{:S(2)}) %copy-start.2) | copy-done | bytes 2097176
  19.5 1.2 %collective-permute-start.9 = (bf16[64,4,2048]{2,1,0:T(4,128)(2,1)}, bf16[64,4,2048]{2,1,0:T(4,128)(2,1)}, u32[]{:S(2)}, u32[]{:S(2)}) collective-permute-start(bf16[64,4,2048]{2,1,0:T(4,128)(2,1)} %refs_0_.1), channel_id=1, source_target_pairs={{0,2},{1,3},{2,0},{3,1},{4,6},{5,7},{6,4},{7,5},{8,10},{9,11},{10,... | collective-permute-start | bytes 3145736 | tf_op jit(solution)/shard_map/ppermute | solution.py:514
  20.7 13.1 %qkv.2 = (f32[256,2048]{1,0:T(8,128)}, f32[256,256]{1,0:T(8,128)}, f32[256,256]{1,0:T(8,128)}) custom-call(bf16[256,256]{1,0:T(8,128)(2,1)} %get-tuple-element.64.perm_ref, bf16[64,4,2048]{2,1,0:T(4,128)(2,1)} %refs_0_.1, bf16[64,4,2048]{2,1,0:T(4,128)(2,1)} %copy-done.4, bf16[8192,2048]{1,0:T(8,128)(2,1)} %refs_2_.3, bf16[8192,256]{1,0:T(8,128)(2,1)} %refs_3_.3, ...), custom_call_target="tpu_custom_call" | custom-call | flops 99999997952 | bytes 300000000 | tf_op jit(solution)/shard_map/qkv/pallas_call | solution.py:240
  33.9 2.9 %collective-permute-done.4.refs_1_ = bf16[1040,128]{1,0:T(8,128)(2,1)S(1)} collective-permute-done((bf16[1040,128]{1,0:T(8,128)(2,1)}, bf16[1040,128]{1,0:T(8,128)(2,1)S(1)}, u32[]{:S(2)}, u32[]{:S(2)}) %collective-permute-start.4) | collective-permute-done | bytes 266272 | tf_op jit(solution)/shard_map/ppermute | solution.py:551
  36.8 3.4 %mid.1.a_ref = f32[128,128]{1,0:T(8,128)S(1)} custom-call(bf16[512,2048]{1,0:T(8,128)(2,1)S(1)} %bitcast.9, bf16[512,2048]{1,0:T(8,128)(2,1)} %collective-permute-done.2.oth_ref, bf16[1040,128]{1,0:T(8,128)(2,1)S(1)} %collective-permute-done.3.refs_0_, bf16[1040,128]{1,0:T(8,128)(2,1)S(1)} %collective-permute-done.4.refs_1_, ...), custom_call_target="tpu_custom_call" | custom-call | flops 10000000000 | bytes 30000000 | tf_op jit(solution)/shard_map/mid/pallas_call | solution.py:300
  40.2 1.3 %collective-permute-start.7 = (f32[128,128]{1,0:T(8,128)S(1)}, f32[128,128]{1,0:T(8,128)S(1)}, u32[]{:S(2)}, u32[]{:S(2)}) collective-permute-start(f32[128,128]{1,0:T(8,128)S(1)} %mid.1.a_ref), channel_id=1, source_target_pairs={{0,2},{1,3},{2,0},{3,1},{4,6},{5,7},{6,4},{7,5},{8,10},{9,11},{10,... | collective-permute-start | bytes 196616 | tf_op jit(solution)/shard_map/ppermute | solution.py:514
  41.5 2.6 %collective-permute-done.7.b_ref = f32[128,128]{1,0:T(8,128)S(1)} collective-permute-done((f32[128,128]{1,0:T(8,128)S(1)}, f32[128,128]{1,0:T(8,128)S(1)}, u32[]{:S(2)}, u32[]{:S(2)}) %collective-permute-start.7) | collective-permute-done | bytes 65568 | tf_op jit(solution)/shard_map/ppermute | solution.py:514
  44.1 1.3 %up.1 = (bf16[64,2048]{1,0:T(8,128)(2,1)S(1)}, bf16[64,2048]{1,0:T(8,128)(2,1)S(1)}, bf16[64,2048]{1,0:T(8,128)(2,1)S(1)}, bf16[64,2048]{1,0:T(8,128)(2,1)S(1)}) custom-call(bf16[512,2048]{1,0:T(8,128)(2,1)S(1)} %bitcast.11, bf16[512,2048]{1,0:T(8,128)(2,1)S(1)} %copy-done.3, f32[128,128]{1,0:T(8,128)S(1)} %mid.1.a_ref, ...), custom_call_target="tpu_custom_call" | custom-call | flops 10000000000 | bytes 30000000 | tf_op jit(solution)/shard_map/up/pallas_call | solution.py:346
  45.4 0.8 collective-permute-start.10
  46.2 3.2 %collective-permute-start.8 = (bf16[64,2048]{1,0:T(8,128)(2,1)S(1)}, bf16[64,2048]{1,0:T(8,128)(2,1)S(1)}, u32[]{:S(2)}, u32[]{:S(2)}) collective-permute-start(bf16[64,2048]{1,0:T(8,128)(2,1)S(1)} %get-tuple-element.63), channel_id=1, source_target_pairs={{0,0},{1,5},{2,2},{3,7},{4,4},{5,1},{6,6},{7,3},{8,8},{9,13},{10,1... | collective-permute-start | bytes 786440 | tf_op jit(solution)/shard_map/ppermute | solution.py:551
  50.2 1.7 %collective-permute-start.13 = (bf16[64,2048]{1,0:T(8,128)(2,1)S(1)}, bf16[64,2048]{1,0:T(8,128)(2,1)S(1)}, u32[]{:S(2)}, u32[]{:S(2)}) collective-permute-start(bf16[64,2048]{1,0:T(8,128)(2,1)S(1)} %get-tuple-element.76), channel_id=1, source_target_pairs={{0,24},{1,29},{2,26},{3,31},{4,28},{5,25},{6,30},{7,27},{8,16},{9,... | collective-permute-start | bytes 786440 | tf_op jit(solution)/shard_map/ppermute | solution.py:551
  51.9 2.1 %collective-permute-start.16 = (bf16[64,2048]{1,0:T(8,128)(2,1)S(1)}, bf16[64,2048]{1,0:T(8,128)(2,1)S(1)}, u32[]{:S(2)}, u32[]{:S(2)}) collective-permute-start(bf16[64,2048]{1,0:T(8,128)(2,1)S(1)} %get-tuple-element.79), channel_id=1, source_target_pairs={{0,8},{1,13},{2,10},{3,15},{4,12},{5,9},{6,14},{7,11},{8,0},{9,5},... | collective-permute-start | bytes 786440 | tf_op jit(solution)/shard_map/ppermute | solution.py:551
  54.0 14.0 %qkv.3 = (f32[256,2048]{1,0:T(8,128)}, f32[256,256]{1,0:T(8,128)}, f32[256,256]{1,0:T(8,128)}) custom-call(bf16[256,256]{1,0:T(8,128)(2,1)} %get-tuple-element.64.perm_ref, bf16[64,4,2048]{2,1,0:T(4,128)(2,1)} %collective-permute-done.9.refs_0_, bf16[64,4,2048]{2,1,0:T(4,128)(2,1)} %collective-permute-done.10.refs_1_, bf16[8192,2048]{1,0:T(8,128)(2,1)} %refs_2_.3, ...), custom_call_target="tpu_custom_call" | custom-call | flops 99999997952 | bytes 300000000 | tf_op jit(solution)/shard_map/qkv/pallas_call | solution.py:240
  68.0 5.4 %collective-permute-done.13.refs_10_ = bf16[64,2048]{1,0:T(8,128)(2,1)S(1)} collective-permute-done((bf16[64,2048]{1,0:T(8,128)(2,1)S(1)}, bf16[64,2048]{1,0:T(8,128)(2,1)S(1)}, u32[]{:S(2)}, u32[]{:S(2)}) %collective-permute-start.13) | collective-permute-done | bytes 262176 | tf_op jit(solution)/shard_map/ppermute | solution.py:551
  74.1 0.9 %collective-permute-done.14.refs_11_ = bf16[64,2048]{1,0:T(8,128)(2,1)S(1)} collective-permute-done((bf16[64,2048]{1,0:T(8,128)(2,1)S(1)}, bf16[64,2048]{1,0:T(8,128)(2,1)S(1)}, u32[]{:S(2)}, u32[]{:S(2)}) %collective-permute-start.14) | collective-permute-done | bytes 262176 | tf_op jit(solution)/shard_map/ppermute | solution.py:514
  76.5 8.3 %attn.1 = bf16[64,4,2048]{2,1,0:T(4,128)(2,1)} custom-call(s32[1]{0:T(128)} %bitcast.refs_0_, s32[1,64]{1,0:T(1,128)} %get-tuple-element.43.refs_1_, f32[256,2048]{1,0:T(8,128)} %get-tuple-element.71.refs_2_, f32[256,256]{1,0:T(8,128)} %get-tuple-element.72.refs_3_, f32[256,256]{1,0:T(8,128)} %get-tuple-element.73.refs_4_, ...), custom_call_target="tpu_custom_call" | custom-call | flops 1 | bytes 1 | tf_op jit(solution)/shard_map/attn/pallas_call | solution.py:489
  (55 shorter events, 5.5 us)
Async XLA Ops:
  0.0 3.2 %collective-permute-start = (bf16[64,4,2048]{2,1,0:T(4,128)(2,1)}, bf16[64,4,2048]{2,1,0:T(4,128)(2,1)S(1)}, u32[]{:S(2)}, u32[]{:S(2)}) collective-permute-start(bf16[64,4,2048]{2,1,0:T(4,128)(2,1)} %refs_0_.1), channel_id=1, source_target_pairs={{0,1},{1,0},{2,3},{3,2},{4,5},{5,4},{6,7},{7,6},{8,9},{9,8},{10,11... | collective-permute-start | bytes 3145736 | tf_op jit(solution)/shard_map/ppermute | solution.py:514
  2.6 14.1 %copy-start.5 = (f32[256,128]{1,0:T(8,128)S(1)}, f32[256,128]{1,0:T(8,128)}, u32[]{:S(2)}) copy-start(f32[256,128]{1,0:T(8,128)} %get-tuple-element.58) | copy-start | bytes 393220
  7.2 10.9 %collective-permute-start.1 = (bf16[512,2048]{1,0:T(8,128)(2,1)}, bf16[512,2048]{1,0:T(8,128)(2,1)S(1)}, u32[]{:S(2)}, u32[]{:S(2)}) collective-permute-start(bf16[512,2048]{1,0:T(8,128)(2,1)} %bitcast.10), channel_id=1, source_target_pairs={{0,1},{1,0},{2,3},{3,2},{4,5},{5,4},{6,7},{7,6},{8,9},{9,8},{10,11... | collective-permute-start | bytes 6291464 | tf_op jit(solution)/shard_map/ppermute | solution.py:514
  7.6 13.1 %collective-permute-start.2 = (bf16[512,2048]{1,0:T(8,128)(2,1)}, bf16[512,2048]{1,0:T(8,128)(2,1)}, u32[]{:S(2)}, u32[]{:S(2)}) collective-permute-start(bf16[512,2048]{1,0:T(8,128)(2,1)} %bitcast.8), channel_id=1, source_target_pairs={{0,1},{1,0},{2,3},{3,2},{4,5},{5,4},{6,7},{7,6},{8,9},{9,8},{10,11... | collective-permute-start | bytes 6291464 | tf_op jit(solution)/shard_map/ppermute | solution.py:514
  7.7 7.7 %collective-permute-start.5 = (bf16[1040,128]{1,0:T(8,128)(2,1)}, bf16[1040,128]{1,0:T(8,128)(2,1)S(1)}, u32[]{:S(2)}, u32[]{:S(2)}) collective-permute-start(bf16[1040,128]{1,0:T(8,128)(2,1)} %get-tuple-element.47), channel_id=1, source_target_pairs={{0,0},{1,5},{2,2},{3,7},{4,4},{5,1},{6,6},{7,3},{8,8},{9,13},{10,1... | collective-permute-start | bytes 798728 | tf_op jit(solution)/shard_map/ppermute | solution.py:551
  11.1 22.7 %collective-permute-start.3 = (bf16[1040,128]{1,0:T(8,128)(2,1)}, bf16[1040,128]{1,0:T(8,128)(2,1)S(1)}, u32[]{:S(2)}, u32[]{:S(2)}) collective-permute-start(bf16[1040,128]{1,0:T(8,128)(2,1)} %get-tuple-element.50), channel_id=1, source_target_pairs={{0,16},{1,21},{2,18},{3,23},{4,20},{5,17},{6,22},{7,19},{8,24},{9,... | collective-permute-start | bytes 798728 | tf_op jit(solution)/shard_map/ppermute | solution.py:551
  13.4 23.4 %collective-permute-start.4 = (bf16[1040,128]{1,0:T(8,128)(2,1)}, bf16[1040,128]{1,0:T(8,128)(2,1)S(1)}, u32[]{:S(2)}, u32[]{:S(2)}) collective-permute-start(bf16[1040,128]{1,0:T(8,128)(2,1)} %get-tuple-element.51), channel_id=1, source_target_pairs={{0,24},{1,29},{2,26},{3,31},{4,28},{5,25},{6,30},{7,27},{8,16},{9,... | collective-permute-start | bytes 798728 | tf_op jit(solution)/shard_map/ppermute | solution.py:551
  15.4 21.4 %collective-permute-start.6 = (bf16[1040,128]{1,0:T(8,128)(2,1)}, bf16[1040,128]{1,0:T(8,128)(2,1)S(1)}, u32[]{:S(2)}, u32[]{:S(2)}) collective-permute-start(bf16[1040,128]{1,0:T(8,128)(2,1)} %get-tuple-element.52), channel_id=1, source_target_pairs={{0,8},{1,13},{2,10},{3,15},{4,12},{5,9},{6,14},{7,11},{8,0},{9,5},... | collective-permute-start | bytes 798728 | tf_op jit(solution)/shard_map/ppermute | solution.py:551
  19.5 25.9 %collective-permute-start.9 = (bf16[64,4,2048]{2,1,0:T(4,128)(2,1)}, bf16[64,4,2048]{2,1,0:T(4,128)(2,1)}, u32[]{:S(2)}, u32[]{:S(2)}) collective-permute-start(bf16[64,4,2048]{2,1,0:T(4,128)(2,1)} %refs_0_.1), channel_id=1, source_target_pairs={{0,2},{1,3},{2,0},{3,1},{4,6},{5,7},{6,4},{7,5},{8,10},{9,11},{10,... | collective-permute-start | bytes 3145736 | tf_op jit(solution)/shard_map/ppermute | solution.py:514
  20.7 16.1 %copy-start = (bf16[8,2048,64]{1,2,0:T(8,128)(2,1)S(1)}, bf16[8,2048,64]{1,2,0:T(8,128)(2,1)}, u32[]{:S(2)}) copy-start(bf16[8,2048,64]{1,2,0:T(8,128)(2,1)} %param.18) | copy-start | bytes 6291460
  36.8 7.3 %copy-start.1 = (bf16[8,64,2048]{2,1,0:T(8,128)(2,1)S(1)}, bf16[8,64,2048]{2,1,0:T(8,128)(2,1)}, u32[]{:S(2)}) copy-start(bf16[8,64,2048]{2,1,0:T(8,128)(2,1)} %param.19) | copy-start | bytes 6291460
  36.8 7.3 %copy-start.3 = (bf16[512,2048]{1,0:T(8,128)(2,1)S(1)}, bf16[512,2048]{1,0:T(8,128)(2,1)}, u32[]{:S(2)}) copy-start(bf16[512,2048]{1,0:T(8,128)(2,1)} %copy-done.2) | copy-start | bytes 6291460
  40.2 3.8 %collective-permute-start.7 = (f32[128,128]{1,0:T(8,128)S(1)}, f32[128,128]{1,0:T(8,128)S(1)}, u32[]{:S(2)}, u32[]{:S(2)}) collective-permute-start(f32[128,128]{1,0:T(8,128)S(1)} %mid.1.a_ref), channel_id=1, source_target_pairs={{0,2},{1,3},{2,0},{3,1},{4,6},{5,7},{6,4},{7,5},{8,10},{9,11},{10,... | collective-permute-start | bytes 196616 | tf_op jit(solution)/shard_map/ppermute | solution.py:514
  45.4 8.6 %collective-permute-start.10 = (bf16[64,4,2048]{2,1,0:T(4,128)(2,1)}, bf16[64,4,2048]{2,1,0:T(4,128)(2,1)}, u32[]{:S(2)}, u32[]{:S(2)}) collective-permute-start(bf16[64,4,2048]{2,1,0:T(4,128)(2,1)} %collective-permute-done.9.refs_0_), channel_id=1, source_target_pairs={{0,1},{1,0},{2,3},{3,2},{4,5},{5,4},{6,7},{7,6},{8,9},{9,8},{10,11... | collective-permute-start | bytes 3145736 | tf_op jit(solution)/shard_map/ppermute | solution.py:514
  46.2 7.8 %collective-permute-start.8 = (bf16[64,2048]{1,0:T(8,128)(2,1)S(1)}, bf16[64,2048]{1,0:T(8,128)(2,1)S(1)}, u32[]{:S(2)}, u32[]{:S(2)}) collective-permute-start(bf16[64,2048]{1,0:T(8,128)(2,1)S(1)} %get-tuple-element.63), channel_id=1, source_target_pairs={{0,0},{1,5},{2,2},{3,7},{4,4},{5,1},{6,6},{7,3},{8,8},{9,13},{10,1... | collective-permute-start | bytes 786440 | tf_op jit(solution)/shard_map/ppermute | solution.py:551
  49.4 18.5 %collective-permute-start.11 = (bf16[64,2048]{1,0:T(8,128)(2,1)S(1)}, bf16[64,2048]{1,0:T(8,128)(2,1)S(1)}, u32[]{:S(2)}, u32[]{:S(2)}) collective-permute-start(bf16[64,2048]{1,0:T(8,128)(2,1)S(1)} %get-tuple-element.66), channel_id=1, source_target_pairs={{0,16},{1,21},{2,18},{3,23},{4,20},{5,17},{6,22},{7,19},{8,24},{9,... | collective-permute-start | bytes 786440 | tf_op jit(solution)/shard_map/ppermute | solution.py:551
  50.2 23.3 %collective-permute-start.13 = (bf16[64,2048]{1,0:T(8,128)(2,1)S(1)}, bf16[64,2048]{1,0:T(8,128)(2,1)S(1)}, u32[]{:S(2)}, u32[]{:S(2)}) collective-permute-start(bf16[64,2048]{1,0:T(8,128)(2,1)S(1)} %get-tuple-element.76), channel_id=1, source_target_pairs={{0,24},{1,29},{2,26},{3,31},{4,28},{5,25},{6,30},{7,27},{8,16},{9,... | collective-permute-start | bytes 786440 | tf_op jit(solution)/shard_map/ppermute | solution.py:551
  51.9 22.1 %collective-permute-start.16 = (bf16[64,2048]{1,0:T(8,128)(2,1)S(1)}, bf16[64,2048]{1,0:T(8,128)(2,1)S(1)}, u32[]{:S(2)}, u32[]{:S(2)}) collective-permute-start(bf16[64,2048]{1,0:T(8,128)(2,1)S(1)} %get-tuple-element.79), channel_id=1, source_target_pairs={{0,8},{1,13},{2,10},{3,15},{4,12},{5,9},{6,14},{7,11},{8,0},{9,5},... | collective-permute-start | bytes 786440 | tf_op jit(solution)/shard_map/ppermute | solution.py:551
  54.0 19.5 %copy-start.6 = (bf16[64,2048]{1,0:T(8,128)(2,1)}, bf16[64,2048]{1,0:T(8,128)(2,1)S(1)}, u32[]{:S(2)}) copy-start(bf16[64,2048]{1,0:T(8,128)(2,1)S(1)} %collective-permute-done.8.refs_12_) | copy-start | bytes 786436
  67.9 8.5 %copy-start.7 = (bf16[64,2048]{1,0:T(8,128)(2,1)}, bf16[64,2048]{1,0:T(8,128)(2,1)S(1)}, u32[]{:S(2)}) copy-start(bf16[64,2048]{1,0:T(8,128)(2,1)S(1)} %collective-permute-done.11.refs_8_) | copy-start | bytes 786436
  68.0 6.1 %collective-permute-start.12 = (bf16[64,2048]{1,0:T(8,128)(2,1)S(1)}, bf16[64,2048]{1,0:T(8,128)(2,1)S(1)}, u32[]{:S(2)}, u32[]{:S(2)}) collective-permute-start(bf16[64,2048]{1,0:T(8,128)(2,1)S(1)} %collective-permute-done.11.refs_8_), channel_id=1, source_target_pairs={{0,1},{1,0},{2,3},{3,2},{4,5},{5,4},{6,7},{7,6},{8,9},{9,8},{10,11... | collective-permute-start | bytes 786440 | tf_op jit(solution)/shard_map/ppermute | solution.py:514
  73.5 1.5 %collective-permute-start.14 = (bf16[64,2048]{1,0:T(8,128)(2,1)S(1)}, bf16[64,2048]{1,0:T(8,128)(2,1)S(1)}, u32[]{:S(2)}, u32[]{:S(2)}) collective-permute-start(bf16[64,2048]{1,0:T(8,128)(2,1)S(1)} %collective-permute-done.13.refs_10_), channel_id=1, source_target_pairs={{0,1},{1,0},{2,3},{3,2},{4,5},{5,4},{6,7},{7,6},{8,9},{9,8},{10,11... | collective-permute-start | bytes 786440 | tf_op jit(solution)/shard_map/ppermute | solution.py:514
  73.5 1.9 %collective-permute-start.15 = (bf16[64,2048]{1,0:T(8,128)(2,1)S(1)}, bf16[64,2048]{1,0:T(8,128)(2,1)S(1)}, u32[]{:S(2)}, u32[]{:S(2)}) collective-permute-start(bf16[64,2048]{1,0:T(8,128)(2,1)S(1)} %collective-permute-done.8.refs_12_), channel_id=1, source_target_pairs={{0,1},{1,0},{2,3},{3,2},{4,5},{5,4},{6,7},{7,6},{8,9},{9,8},{10,11... | collective-permute-start | bytes 786440 | tf_op jit(solution)/shard_map/ppermute | solution.py:514
  74.0 1.8 %collective-permute-start.17 = (bf16[64,2048]{1,0:T(8,128)(2,1)S(1)}, bf16[64,2048]{1,0:T(8,128)(2,1)S(1)}, u32[]{:S(2)}, u32[]{:S(2)}) collective-permute-start(bf16[64,2048]{1,0:T(8,128)(2,1)S(1)} %collective-permute-done.16.refs_14_), channel_id=1, source_target_pairs={{0,1},{1,0},{2,3},{3,2},{4,5},{5,4},{6,7},{7,6},{8,9},{9,8},{10,11... | collective-permute-start | bytes 786440 | tf_op jit(solution)/shard_map/ppermute | solution.py:514
  (8 other events, 13.6 us)

commit v6 on v5

--- a/solution.py
+++ b/solution.py
@@ -284,7 +284,8 @@
     for half in range(2):
         for c in loads[half]:
             c.wait()
-        prod = prod + dot_t(x_ref[half], d_ref[half])
+        prod = prod + dot_t(d_ref[half], x_ref[half])
+    prod = jnp.transpose(prod)
     for k, r in enumerate(ins):
         mask = slot_mask(r[r.shape[0] - 2 * CAP :, :], n_tok, cols, rank)
         part = jnp.where(mask, prod[k * n_tok : (k + 1) * n_tok], 0.0)
@@ -538,7 +539,7 @@
     n_tok = steps * CAP
     n_blocks = row_count // CAP
     n_pairs = n_grp // 2
-    seq = [*range(n_pairs // 2, n_pairs), *range(n_pairs // 2)]
+    seq = [*range(n_pairs // 2, n_pairs), *reversed(range(n_pairs // 2))]
     me = lax.axis_index("tp")
     core = lax.rem(me, 2)
 

time: 85.3 us -> 85.2 us (level)
  no operation moved by 1% of the time
where the time goes in v6:
time: 85.2 us; the launch traced here: 84.8 us
  Pallas kernels  45 us (53%)
  starting transfers between devices  19.6 us (23%)
  waiting for transfers between devices  15.2 us (18%)
  local copies, waits for them, and re-layouts  3.29 us (4%)
  other arithmetic  1.43 us (2%)
    pallas_call x2, Pallas kernels, qkv(): pl.pallas_call(functools.partial(qkv_kernel, tuple(offsets), has_acc, pla...  27.1 us
    ppermute x8, starting transfers between devices, cross(): return lax.ppermute(x, ('grp', 'tp'), perm)  14.5 us
    ppermute x8, waiting for transfers between devices, cross(): return lax.ppermute(x, ('grp', 'tp'), perm)  10.2 us
    pallas_call x1, Pallas kernels, attention(): pl.pallas_call(make_attn_kernel(plan, steps, group, bool(extra)), out_sha...  8.32 us
    ppermute x10, starting transfers between devices, swap(): return lax.ppermute(x, 'tp', [(i, i ^ bit) for i in range(n)])  5.11 us
    ppermute x10, waiting for transfers between devices, swap(): return lax.ppermute(x, 'tp', [(i, i ^ bit) for i in range(n)])  4.95 us
    pallas_call x1, Pallas kernels, mid(): pl.pallas_call(functools.partial(mid_kernel, n_tok, rank), out_shape=jax....  3.26 us
    unnamed x28, local copies, waits for them, and re-layouts  3.11 us
  transfers between devices with their start and end apart: 18, of which 8 were waited for; matrix products, arithmetic and copies ran while one was open for 2% of the time, Pallas kernels for 40%

profile of v6, /device:TPU:9, one launch (start us, length us, event | category | flops | bytes accessed | tf_op | source)
XLA Modules:
  0.0 84.8 jit_solution(5843674503888127512)
XLA Ops:
  0.7 1.9 %route.1 = (bf16[256,256]{1,0:T(8,128)(2,1)}, bf16[128,256]{1,0:T(8,128)(2,1)}, bf16[64,128]{1,0:T(8,128)(2,1)}, f32[256,128]{1,0:T(8,128)}, s32[1,64]{1,0:T(1,128)}) custom-call(s32[1,64]{1,0:T(1,128)} %bitcast.12, s32[1,64]{1,0:T(1,128)} %bitcast.13, s32[1,64]{1,0:T(1,128)} %bitcast.14), custom_call_target="tpu_custom_call" | custom-call | tf_op jit(solution)/shard_map/route/pallas_call | solution.py:138
  3.2 1.0 %copy-done.4 = bf16[64,4,2048]{2,1,0:T(4,128)(2,1)} copy-done((bf16[64,4,2048]{2,1,0:T(4,128)(2,1)}, bf16[64,4,2048]{2,1,0:T(4,128)(2,1)S(1)}, u32[]{:S(2)}) %copy-start.4) | copy-done | bytes 1048600
  4.1 3.1 %pack.1 = (bf16[1040,128]{1,0:T(8,128)(2,1)}, bf16[1040,128]{1,0:T(8,128)(2,1)}, bf16[1040,128]{1,0:T(8,128)(2,1)}, bf16[1040,128]{1,0:T(8,128)(2,1)}) custom-call(bf16[128,256]{1,0:T(8,128)(2,1)} %get-tuple-element.45.send_ref, bf16[64,128]{1,0:T(8,128)(2,1)} %get-tuple-element.46.slot_ref, bf16[64,4,2048]{2,1,0:T(4,128)(2,1)} %refs_0_.1, ...), custom_call_target="tpu_custom_call" | custom-call | tf_op jit(solution)/shard_map/pack/pallas_call | solution.py:166
  7.7 3.1 %collective-permute-start.6 = (bf16[1040,128]{1,0:T(8,128)(2,1)}, bf16[1040,128]{1,0:T(8,128)(2,1)S(1)}, u32[]{:S(2)}, u32[]{:S(2)}) collective-permute-start(bf16[1040,128]{1,0:T(8,128)(2,1)} %get-tuple-element.47), channel_id=1, source_target_pairs={{0,0},{1,5},{2,2},{3,7},{4,4},{5,1},{6,6},{7,3},{8,8},{9,13},{10,1... | collective-permute-start | bytes 798728 | tf_op jit(solution)/shard_map/ppermute | solution.py:552
  11.1 2.3 %collective-permute-start.3 = (bf16[1040,128]{1,0:T(8,128)(2,1)}, bf16[1040,128]{1,0:T(8,128)(2,1)S(1)}, u32[]{:S(2)}, u32[]{:S(2)}) collective-permute-start(bf16[1040,128]{1,0:T(8,128)(2,1)} %get-tuple-element.50), channel_id=1, source_target_pairs={{0,16},{1,21},{2,18},{3,23},{4,20},{5,17},{6,22},{7,19},{8,24},{9,... | collective-permute-start | bytes 798728 | tf_op jit(solution)/shard_map/ppermute | solution.py:552
  13.4 2.0 %collective-permute-done.6.refs_3_ = bf16[1040,128]{1,0:T(8,128)(2,1)S(1)} collective-permute-done((bf16[1040,128]{1,0:T(8,128)(2,1)}, bf16[1040,128]{1,0:T(8,128)(2,1)S(1)}, u32[]{:S(2)}, u32[]{:S(2)}) %collective-permute-start.6) | collective-permute-done | bytes 266272 | tf_op jit(solution)/shard_map/ppermute | solution.py:552
  15.4 1.3 %collective-permute-start.5 = (bf16[1040,128]{1,0:T(8,128)(2,1)}, bf16[1040,128]{1,0:T(8,128)(2,1)S(1)}, u32[]{:S(2)}, u32[]{:S(2)}) collective-permute-start(bf16[1040,128]{1,0:T(8,128)(2,1)} %get-tuple-element.52), channel_id=1, source_target_pairs={{0,8},{1,13},{2,10},{3,15},{4,12},{5,9},{6,14},{7,11},{8,0},{9,5},... | collective-permute-start | bytes 798728 | tf_op jit(solution)/shard_map/ppermute | solution.py:552
  17.3 0.8 pad_maximum_fusion.refs_5_
  18.1 1.4 %copy-done.2 = bf16[512,2048]{1,0:T(8,128)(2,1)} copy-done((bf16[512,2048]{1,0:T(8,128)(2,1)}, bf16[512,2048]{1,0:T(8,128)(2,1)S(1)}, u32[]{:S(2)}) %copy-start.2) | copy-done | bytes 2097176
  19.5 1.2 %collective-permute-start.9 = (bf16[64,4,2048]{2,1,0:T(4,128)(2,1)}, bf16[64,4,2048]{2,1,0:T(4,128)(2,1)}, u32[]{:S(2)}, u32[]{:S(2)}) collective-permute-start(bf16[64,4,2048]{2,1,0:T(4,128)(2,1)} %refs_0_.1), channel_id=1, source_target_pairs={{0,2},{1,3},{2,0},{3,1},{4,6},{5,7},{6,4},{7,5},{8,10},{9,11},{10,... | collective-permute-start | bytes 3145736 | tf_op jit(solution)/shard_map/ppermute | solution.py:515
  20.7 13.1 %qkv.2 = (f32[256,2048]{1,0:T(8,128)}, f32[256,256]{1,0:T(8,128)}, f32[256,256]{1,0:T(8,128)}) custom-call(bf16[256,256]{1,0:T(8,128)(2,1)} %get-tuple-element.64.perm_ref, bf16[64,4,2048]{2,1,0:T(4,128)(2,1)} %refs_0_.1, bf16[64,4,2048]{2,1,0:T(4,128)(2,1)} %copy-done.4, bf16[8192,2048]{1,0:T(8,128)(2,1)} %refs_2_.3, bf16[8192,256]{1,0:T(8,128)(2,1)} %refs_3_.3, ...), custom_call_target="tpu_custom_call" | custom-call | flops 99999997952 | bytes 300000000 | tf_op jit(solution)/shard_map/qkv/pallas_call | solution.py:240
  33.9 2.9 %collective-permute-done.4.refs_1_ = bf16[1040,128]{1,0:T(8,128)(2,1)S(1)} collective-permute-done((bf16[1040,128]{1,0:T(8,128)(2,1)}, bf16[1040,128]{1,0:T(8,128)(2,1)S(1)}, u32[]{:S(2)}, u32[]{:S(2)}) %collective-permute-start.4) | collective-permute-done | bytes 266272 | tf_op jit(solution)/shard_map/ppermute | solution.py:552
  36.8 3.3 %mid.1.a_ref = f32[128,128]{1,0:T(8,128)S(1)} custom-call(bf16[512,2048]{1,0:T(8,128)(2,1)S(1)} %bitcast.9, bf16[512,2048]{1,0:T(8,128)(2,1)} %collective-permute-done.2.oth_ref, bf16[1040,128]{1,0:T(8,128)(2,1)S(1)} %collective-permute-done.3.refs_0_, bf16[1040,128]{1,0:T(8,128)(2,1)S(1)} %collective-permute-done.4.refs_1_, ...), custom_call_target="tpu_custom_call" | custom-call | flops 10000000000 | bytes 30000000 | tf_op jit(solution)/shard_map/mid/pallas_call | solution.py:301
  40.1 1.3 %collective-permute-start.7 = (f32[128,128]{1,0:T(8,128)S(1)}, f32[128,128]{1,0:T(8,128)S(1)}, u32[]{:S(2)}, u32[]{:S(2)}) collective-permute-start(f32[128,128]{1,0:T(8,128)S(1)} %mid.1.a_ref), channel_id=1, source_target_pairs={{0,2},{1,3},{2,0},{3,1},{4,6},{5,7},{6,4},{7,5},{8,10},{9,11},{10,... | collective-permute-start | bytes 196616 | tf_op jit(solution)/shard_map/ppermute | solution.py:515
  41.3 2.7 %collective-permute-done.7.b_ref = f32[128,128]{1,0:T(8,128)S(1)} collective-permute-done((f32[128,128]{1,0:T(8,128)S(1)}, f32[128,128]{1,0:T(8,128)S(1)}, u32[]{:S(2)}, u32[]{:S(2)}) %collective-permute-start.7) | collective-permute-done | bytes 65568 | tf_op jit(solution)/shard_map/ppermute | solution.py:515
  44.1 1.3 %up.1 = (bf16[64,2048]{1,0:T(8,128)(2,1)S(1)}, bf16[64,2048]{1,0:T(8,128)(2,1)S(1)}, bf16[64,2048]{1,0:T(8,128)(2,1)S(1)}, bf16[64,2048]{1,0:T(8,128)(2,1)S(1)}) custom-call(bf16[512,2048]{1,0:T(8,128)(2,1)S(1)} %bitcast.11, bf16[512,2048]{1,0:T(8,128)(2,1)S(1)} %copy-done.3, f32[128,128]{1,0:T(8,128)S(1)} %mid.1.a_ref, ...), custom_call_target="tpu_custom_call" | custom-call | flops 10000000000 | bytes 30000000 | tf_op jit(solution)/shard_map/up/pallas_call | solution.py:347
  45.4 0.8 collective-permute-start.10
  46.1 3.3 %collective-permute-start.8 = (bf16[64,2048]{1,0:T(8,128)(2,1)S(1)}, bf16[64,2048]{1,0:T(8,128)(2,1)S(1)}, u32[]{:S(2)}, u32[]{:S(2)}) collective-permute-start(bf16[64,2048]{1,0:T(8,128)(2,1)S(1)} %get-tuple-element.63), channel_id=1, source_target_pairs={{0,0},{1,5},{2,2},{3,7},{4,4},{5,1},{6,6},{7,3},{8,8},{9,13},{10,1... | collective-permute-start | bytes 786440 | tf_op jit(solution)/shard_map/ppermute | solution.py:552
  50.2 1.5 %collective-permute-start.13 = (bf16[64,2048]{1,0:T(8,128)(2,1)S(1)}, bf16[64,2048]{1,0:T(8,128)(2,1)S(1)}, u32[]{:S(2)}, u32[]{:S(2)}) collective-permute-start(bf16[64,2048]{1,0:T(8,128)(2,1)S(1)} %get-tuple-element.76), channel_id=1, source_target_pairs={{0,24},{1,29},{2,26},{3,31},{4,28},{5,25},{6,30},{7,27},{8,16},{9,... | collective-permute-start | bytes 786440 | tf_op jit(solution)/shard_map/ppermute | solution.py:552
  51.7 2.2 %collective-permute-start.15 = (bf16[64,2048]{1,0:T(8,128)(2,1)S(1)}, bf16[64,2048]{1,0:T(8,128)(2,1)S(1)}, u32[]{:S(2)}, u32[]{:S(2)}) collective-permute-start(bf16[64,2048]{1,0:T(8,128)(2,1)S(1)} %get-tuple-element.78), channel_id=1, source_target_pairs={{0,8},{1,13},{2,10},{3,15},{4,12},{5,9},{6,14},{7,11},{8,0},{9,5},... | collective-permute-start | bytes 786440 | tf_op jit(solution)/shard_map/ppermute | solution.py:552
  53.9 14.0 %qkv.3 = (f32[256,2048]{1,0:T(8,128)}, f32[256,256]{1,0:T(8,128)}, f32[256,256]{1,0:T(8,128)}) custom-call(bf16[256,256]{1,0:T(8,128)(2,1)} %get-tuple-element.64.perm_ref, bf16[64,4,2048]{2,1,0:T(4,128)(2,1)} %collective-permute-done.9.refs_0_, bf16[64,4,2048]{2,1,0:T(4,128)(2,1)} %collective-permute-done.10.refs_1_, bf16[8192,2048]{1,0:T(8,128)(2,1)} %refs_2_.3, ...), custom_call_target="tpu_custom_call" | custom-call | flops 99999997952 | bytes 300000000 | tf_op jit(solution)/shard_map/qkv/pallas_call | solution.py:240
  68.0 5.3 %collective-permute-done.13.refs_10_ = bf16[64,2048]{1,0:T(8,128)(2,1)S(1)} collective-permute-done((bf16[64,2048]{1,0:T(8,128)(2,1)S(1)}, bf16[64,2048]{1,0:T(8,128)(2,1)S(1)}, u32[]{:S(2)}, u32[]{:S(2)}) %collective-permute-start.13) | collective-permute-done | bytes 262176 | tf_op jit(solution)/shard_map/ppermute | solution.py:552
  73.9 0.9 %collective-permute-done.14.refs_11_ = bf16[64,2048]{1,0:T(8,128)(2,1)S(1)} collective-permute-done((bf16[64,2048]{1,0:T(8,128)(2,1)S(1)}, bf16[64,2048]{1,0:T(8,128)(2,1)S(1)}, u32[]{:S(2)}, u32[]{:S(2)}) %collective-permute-start.14) | collective-permute-done | bytes 262176 | tf_op jit(solution)/shard_map/ppermute | solution.py:515
  76.4 8.3 %attn.1 = bf16[64,4,2048]{2,1,0:T(4,128)(2,1)} custom-call(s32[1]{0:T(128)} %bitcast.refs_0_, s32[1,64]{1,0:T(1,128)} %get-tuple-element.43.refs_1_, f32[256,2048]{1,0:T(8,128)} %get-tuple-element.71.refs_2_, f32[256,256]{1,0:T(8,128)} %get-tuple-element.72.refs_3_, f32[256,256]{1,0:T(8,128)} %get-tuple-element.73.refs_4_, ...), custom_call_target="tpu_custom_call" | custom-call | flops 1 | bytes 1 | tf_op jit(solution)/shard_map/attn/pallas_call | solution.py:490
  (55 shorter events, 5.5 us)
Async XLA Ops:
  0.0 3.2 %collective-permute-start = (bf16[64,4,2048]{2,1,0:T(4,128)(2,1)}, bf16[64,4,2048]{2,1,0:T(4,128)(2,1)S(1)}, u32[]{:S(2)}, u32[]{:S(2)}) collective-permute-start(bf16[64,4,2048]{2,1,0:T(4,128)(2,1)} %refs_0_.1), channel_id=1, source_target_pairs={{0,1},{1,0},{2,3},{3,2},{4,5},{5,4},{6,7},{7,6},{8,9},{9,8},{10,11... | collective-permute-start | bytes 3145736 | tf_op jit(solution)/shard_map/ppermute | solution.py:515
  2.6 14.1 %copy-start.5 = (f32[256,128]{1,0:T(8,128)S(1)}, f32[256,128]{1,0:T(8,128)}, u32[]{:S(2)}) copy-start(f32[256,128]{1,0:T(8,128)} %get-tuple-element.58) | copy-start | bytes 393220
  7.2 10.9 %collective-permute-start.1 = (bf16[512,2048]{1,0:T(8,128)(2,1)}, bf16[512,2048]{1,0:T(8,128)(2,1)S(1)}, u32[]{:S(2)}, u32[]{:S(2)}) collective-permute-start(bf16[512,2048]{1,0:T(8,128)(2,1)} %bitcast.10), channel_id=1, source_target_pairs={{0,1},{1,0},{2,3},{3,2},{4,5},{5,4},{6,7},{7,6},{8,9},{9,8},{10,11... | collective-permute-start | bytes 6291464 | tf_op jit(solution)/shard_map/ppermute | solution.py:515
  7.6 13.1 %collective-permute-start.2 = (bf16[512,2048]{1,0:T(8,128)(2,1)}, bf16[512,2048]{1,0:T(8,128)(2,1)}, u32[]{:S(2)}, u32[]{:S(2)}) collective-permute-start(bf16[512,2048]{1,0:T(8,128)(2,1)} %bitcast.8), channel_id=1, source_target_pairs={{0,1},{1,0},{2,3},{3,2},{4,5},{5,4},{6,7},{7,6},{8,9},{9,8},{10,11... | collective-permute-start | bytes 6291464 | tf_op jit(solution)/shard_map/ppermute | solution.py:515
  7.7 7.7 %collective-permute-start.6 = (bf16[1040,128]{1,0:T(8,128)(2,1)}, bf16[1040,128]{1,0:T(8,128)(2,1)S(1)}, u32[]{:S(2)}, u32[]{:S(2)}) collective-permute-start(bf16[1040,128]{1,0:T(8,128)(2,1)} %get-tuple-element.47), channel_id=1, source_target_pairs={{0,0},{1,5},{2,2},{3,7},{4,4},{5,1},{6,6},{7,3},{8,8},{9,13},{10,1... | collective-permute-start | bytes 798728 | tf_op jit(solution)/shard_map/ppermute | solution.py:552
  11.1 22.7 %collective-permute-start.3 = (bf16[1040,128]{1,0:T(8,128)(2,1)}, bf16[1040,128]{1,0:T(8,128)(2,1)S(1)}, u32[]{:S(2)}, u32[]{:S(2)}) collective-permute-start(bf16[1040,128]{1,0:T(8,128)(2,1)} %get-tuple-element.50), channel_id=1, source_target_pairs={{0,16},{1,21},{2,18},{3,23},{4,20},{5,17},{6,22},{7,19},{8,24},{9,... | collective-permute-start | bytes 798728 | tf_op jit(solution)/shard_map/ppermute | solution.py:552
  13.4 23.4 %collective-permute-start.4 = (bf16[1040,128]{1,0:T(8,128)(2,1)}, bf16[1040,128]{1,0:T(8,128)(2,1)S(1)}, u32[]{:S(2)}, u32[]{:S(2)}) collective-permute-start(bf16[1040,128]{1,0:T(8,128)(2,1)} %get-tuple-element.51), channel_id=1, source_target_pairs={{0,24},{1,29},{2,26},{3,31},{4,28},{5,25},{6,30},{7,27},{8,16},{9,... | collective-permute-start | bytes 798728 | tf_op jit(solution)/shard_map/ppermute | solution.py:552
  15.4 21.4 %collective-permute-start.5 = (bf16[1040,128]{1,0:T(8,128)(2,1)}, bf16[1040,128]{1,0:T(8,128)(2,1)S(1)}, u32[]{:S(2)}, u32[]{:S(2)}) collective-permute-start(bf16[1040,128]{1,0:T(8,128)(2,1)} %get-tuple-element.52), channel_id=1, source_target_pairs={{0,8},{1,13},{2,10},{3,15},{4,12},{5,9},{6,14},{7,11},{8,0},{9,5},... | collective-permute-start | bytes 798728 | tf_op jit(solution)/shard_map/ppermute | solution.py:552
  19.5 25.9 %collective-permute-start.9 = (bf16[64,4,2048]{2,1,0:T(4,128)(2,1)}, bf16[64,4,2048]{2,1,0:T(4,128)(2,1)}, u32[]{:S(2)}, u32[]{:S(2)}) collective-permute-start(bf16[64,4,2048]{2,1,0:T(4,128)(2,1)} %refs_0_.1), channel_id=1, source_target_pairs={{0,2},{1,3},{2,0},{3,1},{4,6},{5,7},{6,4},{7,5},{8,10},{9,11},{10,... | collective-permute-start | bytes 3145736 | tf_op jit(solution)/shard_map/ppermute | solution.py:515
  20.7 16.1 %copy-start = (bf16[8,2048,64]{1,2,0:T(8,128)(2,1)S(1)}, bf16[8,2048,64]{1,2,0:T(8,128)(2,1)}, u32[]{:S(2)}) copy-start(bf16[8,2048,64]{1,2,0:T(8,128)(2,1)} %param.18) | copy-start | bytes 6291460
  36.8 7.3 %copy-start.1 = (bf16[8,64,2048]{2,1,0:T(8,128)(2,1)S(1)}, bf16[8,64,2048]{2,1,0:T(8,128)(2,1)}, u32[]{:S(2)}) copy-start(bf16[8,64,2048]{2,1,0:T(8,128)(2,1)} %param.19) | copy-start | bytes 6291460
  36.8 7.3 %copy-start.3 = (bf16[512,2048]{1,0:T(8,128)(2,1)S(1)}, bf16[512,2048]{1,0:T(8,128)(2,1)}, u32[]{:S(2)}) copy-start(bf16[512,2048]{1,0:T(8,128)(2,1)} %copy-done.2) | copy-start | bytes 6291460
  40.1 4.0 %collective-permute-start.7 = (f32[128,128]{1,0:T(8,128)S(1)}, f32[128,128]{1,0:T(8,128)S(1)}, u32[]{:S(2)}, u32[]{:S(2)}) collective-permute-start(f32[128,128]{1,0:T(8,128)S(1)} %mid.1.a_ref), channel_id=1, source_target_pairs={{0,2},{1,3},{2,0},{3,1},{4,6},{5,7},{6,4},{7,5},{8,10},{9,11},{10,... | collective-permute-start | bytes 196616 | tf_op jit(solution)/shard_map/ppermute | solution.py:515
  45.4 8.6 %collective-permute-start.10 = (bf16[64,4,2048]{2,1,0:T(4,128)(2,1)}, bf16[64,4,2048]{2,1,0:T(4,128)(2,1)}, u32[]{:S(2)}, u32[]{:S(2)}) collective-permute-start(bf16[64,4,2048]{2,1,0:T(4,128)(2,1)} %collective-permute-done.9.refs_0_), channel_id=1, source_target_pairs={{0,1},{1,0},{2,3},{3,2},{4,5},{5,4},{6,7},{7,6},{8,9},{9,8},{10,11... | collective-permute-start | bytes 3145736 | tf_op jit(solution)/shard_map/ppermute | solution.py:515
  46.1 7.8 %collective-permute-start.8 = (bf16[64,2048]{1,0:T(8,128)(2,1)S(1)}, bf16[64,2048]{1,0:T(8,128)(2,1)S(1)}, u32[]{:S(2)}, u32[]{:S(2)}) collective-permute-start(bf16[64,2048]{1,0:T(8,128)(2,1)S(1)} %get-tuple-element.63), channel_id=1, source_target_pairs={{0,0},{1,5},{2,2},{3,7},{4,4},{5,1},{6,6},{7,3},{8,8},{9,13},{10,1... | collective-permute-start | bytes 786440 | tf_op jit(solution)/shard_map/ppermute | solution.py:552
  49.4 18.4 %collective-permute-start.11 = (bf16[64,2048]{1,0:T(8,128)(2,1)S(1)}, bf16[64,2048]{1,0:T(8,128)(2,1)S(1)}, u32[]{:S(2)}, u32[]{:S(2)}) collective-permute-start(bf16[64,2048]{1,0:T(8,128)(2,1)S(1)} %get-tuple-element.66), channel_id=1, source_target_pairs={{0,16},{1,21},{2,18},{3,23},{4,20},{5,17},{6,22},{7,19},{8,24},{9,... | collective-permute-start | bytes 786440 | tf_op jit(solution)/shard_map/ppermute | solution.py:552
  50.2 23.1 %collective-permute-start.13 = (bf16[64,2048]{1,0:T(8,128)(2,1)S(1)}, bf16[64,2048]{1,0:T(8,128)(2,1)S(1)}, u32[]{:S(2)}, u32[]{:S(2)}) collective-permute-start(bf16[64,2048]{1,0:T(8,128)(2,1)S(1)} %get-tuple-element.76), channel_id=1, source_target_pairs={{0,24},{1,29},{2,26},{3,31},{4,28},{5,25},{6,30},{7,27},{8,16},{9,... | collective-permute-start | bytes 786440 | tf_op jit(solution)/shard_map/ppermute | solution.py:552
  51.7 21.6 %collective-permute-start.15 = (bf16[64,2048]{1,0:T(8,128)(2,1)S(1)}, bf16[64,2048]{1,0:T(8,128)(2,1)S(1)}, u32[]{:S(2)}, u32[]{:S(2)}) collective-permute-start(bf16[64,2048]{1,0:T(8,128)(2,1)S(1)} %get-tuple-element.78), channel_id=1, source_target_pairs={{0,8},{1,13},{2,10},{3,15},{4,12},{5,9},{6,14},{7,11},{8,0},{9,5},... | collective-permute-start | bytes 786440 | tf_op jit(solution)/shard_map/ppermute | solution.py:552
  53.9 19.9 %copy-start.6 = (bf16[64,2048]{1,0:T(8,128)(2,1)}, bf16[64,2048]{1,0:T(8,128)(2,1)S(1)}, u32[]{:S(2)}) copy-start(bf16[64,2048]{1,0:T(8,128)(2,1)S(1)} %collective-permute-done.8.refs_14_) | copy-start | bytes 786436
  67.9 8.4 %copy-start.7 = (bf16[64,2048]{1,0:T(8,128)(2,1)}, bf16[64,2048]{1,0:T(8,128)(2,1)S(1)}, u32[]{:S(2)}) copy-start(bf16[64,2048]{1,0:T(8,128)(2,1)S(1)} %collective-permute-done.11.refs_8_) | copy-start | bytes 786436
  67.9 6.0 %collective-permute-start.12 = (bf16[64,2048]{1,0:T(8,128)(2,1)S(1)}, bf16[64,2048]{1,0:T(8,128)(2,1)S(1)}, u32[]{:S(2)}, u32[]{:S(2)}) collective-permute-start(bf16[64,2048]{1,0:T(8,128)(2,1)S(1)} %collective-permute-done.11.refs_8_), channel_id=1, source_target_pairs={{0,1},{1,0},{2,3},{3,2},{4,5},{5,4},{6,7},{7,6},{8,9},{9,8},{10,11... | collective-permute-start | bytes 786440 | tf_op jit(solution)/shard_map/ppermute | solution.py:515
  73.3 1.5 %collective-permute-start.14 = (bf16[64,2048]{1,0:T(8,128)(2,1)S(1)}, bf16[64,2048]{1,0:T(8,128)(2,1)S(1)}, u32[]{:S(2)}, u32[]{:S(2)}) collective-permute-start(bf16[64,2048]{1,0:T(8,128)(2,1)S(1)} %collective-permute-done.13.refs_10_), channel_id=1, source_target_pairs={{0,1},{1,0},{2,3},{3,2},{4,5},{5,4},{6,7},{7,6},{8,9},{9,8},{10,11... | collective-permute-start | bytes 786440 | tf_op jit(solution)/shard_map/ppermute | solution.py:515
  73.3 1.9 %collective-permute-start.16 = (bf16[64,2048]{1,0:T(8,128)(2,1)S(1)}, bf16[64,2048]{1,0:T(8,128)(2,1)S(1)}, u32[]{:S(2)}, u32[]{:S(2)}) collective-permute-start(bf16[64,2048]{1,0:T(8,128)(2,1)S(1)} %collective-permute-done.15.refs_12_), channel_id=1, source_target_pairs={{0,1},{1,0},{2,3},{3,2},{4,5},{5,4},{6,7},{7,6},{8,9},{9,8},{10,11... | collective-permute-start | bytes 786440 | tf_op jit(solution)/shard_map/ppermute | solution.py:515
  73.8 1.8 %collective-permute-start.17 = (bf16[64,2048]{1,0:T(8,128)(2,1)S(1)}, bf16[64,2048]{1,0:T(8,128)(2,1)S(1)}, u32[]{:S(2)}, u32[]{:S(2)}) collective-permute-start(bf16[64,2048]{1,0:T(8,128)(2,1)S(1)} %collective-permute-done.8.refs_14_), channel_id=1, source_target_pairs={{0,1},{1,0},{2,3},{3,2},{4,5},{5,4},{6,7},{7,6},{8,9},{9,8},{10,11... | collective-permute-start | bytes 786440 | tf_op jit(solution)/shard_map/ppermute | solution.py:515
  (8 other events, 14.1 us)

commit v7 on v6

--- a/solution.py
+++ b/solution.py
@@ -20,7 +20,7 @@
 FIRST_STEPS = (256, 256)
 STEP = 512
 PARTS = 4
-AHEAD = 4
+AHEAD = 6
 TOGETHER = 2
 
 TINY = pl.CostEstimate(flops=1, bytes_accessed=1, transcendentals=0)

time: 85.2 us -> 85.2 us (level)
  no operation moved by 1% of the time
where the time goes in v7:
time: 85.2 us; the launch traced here: 84.8 us
  Pallas kernels  45 us (53%)
  starting transfers between devices  19.6 us (23%)
  waiting for transfers between devices  15.2 us (18%)
  local copies, waits for them, and re-layouts  3.29 us (4%)
  other arithmetic  1.43 us (2%)
    pallas_call x2, Pallas kernels, qkv(): pl.pallas_call(functools.partial(qkv_kernel, tuple(offsets), has_acc, pla...  27.1 us
    ppermute x8, starting transfers between devices, cross(): return lax.ppermute(x, ('grp', 'tp'), perm)  14.5 us
    ppermute x8, waiting for transfers between devices, cross(): return lax.ppermute(x, ('grp', 'tp'), perm)  10.2 us
    pallas_call x1, Pallas kernels, attention(): pl.pallas_call(make_attn_kernel(plan, steps, group, bool(extra)), out_sha...  8.32 us
    ppermute x10, starting transfers between devices, swap(): return lax.ppermute(x, 'tp', [(i, i ^ bit) for i in range(n)])  5.11 us
    ppermute x10, waiting for transfers between devices, swap(): return lax.ppermute(x, 'tp', [(i, i ^ bit) for i in range(n)])  4.95 us
    pallas_call x1, Pallas kernels, mid(): pl.pallas_call(functools.partial(mid_kernel, n_tok, rank), out_shape=jax....  3.26 us
    unnamed x28, local copies, waits for them, and re-layouts  3.11 us
  transfers between devices with their start and end apart: 18, of which 8 were waited for; matrix products, arithmetic and copies ran while one was open for 2% of the time, Pallas kernels for 40%

profile of v7, /device:TPU:9, one launch (start us, length us, event | category | flops | bytes accessed | tf_op | source)
XLA Modules:
  0.0 84.8 jit_solution(2105784249300209181)
XLA Ops:
  0.7 1.9 %route.1 = (bf16[256,256]{1,0:T(8,128)(2,1)}, bf16[128,256]{1,0:T(8,128)(2,1)}, bf16[64,128]{1,0:T(8,128)(2,1)}, f32[256,128]{1,0:T(8,128)}, s32[1,64]{1,0:T(1,128)}) custom-call(s32[1,64]{1,0:T(1,128)} %bitcast.12, s32[1,64]{1,0:T(1,128)} %bitcast.13, s32[1,64]{1,0:T(1,128)} %bitcast.14), custom_call_target="tpu_custom_call" | custom-call | tf_op jit(solution)/shard_map/route/pallas_call | solution.py:138
  3.2 1.0 %copy-done.4 = bf16[64,4,2048]{2,1,0:T(4,128)(2,1)} copy-done((bf16[64,4,2048]{2,1,0:T(4,128)(2,1)}, bf16[64,4,2048]{2,1,0:T(4,128)(2,1)S(1)}, u32[]{:S(2)}) %copy-start.4) | copy-done | bytes 1048600
  4.1 3.1 %pack.1 = (bf16[1040,128]{1,0:T(8,128)(2,1)}, bf16[1040,128]{1,0:T(8,128)(2,1)}, bf16[1040,128]{1,0:T(8,128)(2,1)}, bf16[1040,128]{1,0:T(8,128)(2,1)}) custom-call(bf16[128,256]{1,0:T(8,128)(2,1)} %get-tuple-element.45.send_ref, bf16[64,128]{1,0:T(8,128)(2,1)} %get-tuple-element.46.slot_ref, bf16[64,4,2048]{2,1,0:T(4,128)(2,1)} %refs_0_.1, ...), custom_call_target="tpu_custom_call" | custom-call | tf_op jit(solution)/shard_map/pack/pallas_call | solution.py:166
  7.7 3.1 %collective-permute-start.6 = (bf16[1040,128]{1,0:T(8,128)(2,1)}, bf16[1040,128]{1,0:T(8,128)(2,1)S(1)}, u32[]{:S(2)}, u32[]{:S(2)}) collective-permute-start(bf16[1040,128]{1,0:T(8,128)(2,1)} %get-tuple-element.47), channel_id=1, source_target_pairs={{0,0},{1,5},{2,2},{3,7},{4,4},{5,1},{6,6},{7,3},{8,8},{9,13},{10,1... | collective-permute-start | bytes 798728 | tf_op jit(solution)/shard_map/ppermute | solution.py:552
  11.1 2.3 %collective-permute-start.3 = (bf16[1040,128]{1,0:T(8,128)(2,1)}, bf16[1040,128]{1,0:T(8,128)(2,1)S(1)}, u32[]{:S(2)}, u32[]{:S(2)}) collective-permute-start(bf16[1040,128]{1,0:T(8,128)(2,1)} %get-tuple-element.50), channel_id=1, source_target_pairs={{0,16},{1,21},{2,18},{3,23},{4,20},{5,17},{6,22},{7,19},{8,24},{9,... | collective-permute-start | bytes 798728 | tf_op jit(solution)/shard_map/ppermute | solution.py:552
  13.4 2.0 %collective-permute-done.6.refs_3_ = bf16[1040,128]{1,0:T(8,128)(2,1)S(1)} collective-permute-done((bf16[1040,128]{1,0:T(8,128)(2,1)}, bf16[1040,128]{1,0:T(8,128)(2,1)S(1)}, u32[]{:S(2)}, u32[]{:S(2)}) %collective-permute-start.6) | collective-permute-done | bytes 266272 | tf_op jit(solution)/shard_map/ppermute | solution.py:552
  15.4 1.3 %collective-permute-start.5 = (bf16[1040,128]{1,0:T(8,128)(2,1)}, bf16[1040,128]{1,0:T(8,128)(2,1)S(1)}, u32[]{:S(2)}, u32[]{:S(2)}) collective-permute-start(bf16[1040,128]{1,0:T(8,128)(2,1)} %get-tuple-element.52), channel_id=1, source_target_pairs={{0,8},{1,13},{2,10},{3,15},{4,12},{5,9},{6,14},{7,11},{8,0},{9,5},... | collective-permute-start | bytes 798728 | tf_op jit(solution)/shard_map/ppermute | solution.py:552
  17.3 0.8 pad_maximum_fusion.refs_5_
  18.1 1.4 %copy-done.2 = bf16[512,2048]{1,0:T(8,128)(2,1)} copy-done((bf16[512,2048]{1,0:T(8,128)(2,1)}, bf16[512,2048]{1,0:T(8,128)(2,1)S(1)}, u32[]{:S(2)}) %copy-start.2) | copy-done | bytes 2097176
  19.5 1.2 %collective-permute-start.9 = (bf16[64,4,2048]{2,1,0:T(4,128)(2,1)}, bf16[64,4,2048]{2,1,0:T(4,128)(2,1)}, u32[]{:S(2)}, u32[]{:S(2)}) collective-permute-start(bf16[64,4,2048]{2,1,0:T(4,128)(2,1)} %refs_0_.1), channel_id=1, source_target_pairs={{0,2},{1,3},{2,0},{3,1},{4,6},{5,7},{6,4},{7,5},{8,10},{9,11},{10,... | collective-permute-start | bytes 3145736 | tf_op jit(solution)/shard_map/ppermute | solution.py:515
  20.7 13.1 %qkv.2 = (f32[256,2048]{1,0:T(8,128)}, f32[256,256]{1,0:T(8,128)}, f32[256,256]{1,0:T(8,128)}) custom-call(bf16[256,256]{1,0:T(8,128)(2,1)} %get-tuple-element.64.perm_ref, bf16[64,4,2048]{2,1,0:T(4,128)(2,1)} %refs_0_.1, bf16[64,4,2048]{2,1,0:T(4,128)(2,1)} %copy-done.4, bf16[8192,2048]{1,0:T(8,128)(2,1)} %refs_2_.3, bf16[8192,256]{1,0:T(8,128)(2,1)} %refs_3_.3, ...), custom_call_target="tpu_custom_call" | custom-call | flops 99999997952 | bytes 300000000 | tf_op jit(solution)/shard_map/qkv/pallas_call | solution.py:240
  33.9 2.9 %collective-permute-done.4.refs_1_ = bf16[1040,128]{1,0:T(8,128)(2,1)S(1)} collective-permute-done((bf16[1040,128]{1,0:T(8,128)(2,1)}, bf16[1040,128]{1,0:T(8,128)(2,1)S(1)}, u32[]{:S(2)}, u32[]{:S(2)}) %collective-permute-start.4) | collective-permute-done | bytes 266272 | tf_op jit(solution)/shard_map/ppermute | solution.py:552
  36.8 3.3 %mid.1.a_ref = f32[128,128]{1,0:T(8,128)S(1)} custom-call(bf16[512,2048]{1,0:T(8,128)(2,1)S(1)} %bitcast.9, bf16[512,2048]{1,0:T(8,128)(2,1)} %collective-permute-done.2.oth_ref, bf16[1040,128]{1,0:T(8,128)(2,1)S(1)} %collective-permute-done.3.refs_0_, bf16[1040,128]{1,0:T(8,128)(2,1)S(1)} %collective-permute-done.4.refs_1_, ...), custom_call_target="tpu_custom_call" | custom-call | flops 10000000000 | bytes 30000000 | tf_op jit(solution)/shard_map/mid/pallas_call | solution.py:301
  40.1 1.3 %collective-permute-start.7 = (f32[128,128]{1,0:T(8,128)S(1)}, f32[128,128]{1,0:T(8,128)S(1)}, u32[]{:S(2)}, u32[]{:S(2)}) collective-permute-start(f32[128,128]{1,0:T(8,128)S(1)} %mid.1.a_ref), channel_id=1, source_target_pairs={{0,2},{1,3},{2,0},{3,1},{4,6},{5,7},{6,4},{7,5},{8,10},{9,11},{10,... | collective-permute-start | bytes 196616 | tf_op jit(solution)/shard_map/ppermute | solution.py:515
  41.3 2.7 %collective-permute-done.7.b_ref = f32[128,128]{1,0:T(8,128)S(1)} collective-permute-done((f32[128,128]{1,0:T(8,128)S(1)}, f32[128,128]{1,0:T(8,128)S(1)}, u32[]{:S(2)}, u32[]{:S(2)}) %collective-permute-start.7) | collective-permute-done | bytes 65568 | tf_op jit(solution)/shard_map/ppermute | solution.py:515
  44.1 1.3 %up.1 = (bf16[64,2048]{1,0:T(8,128)(2,1)S(1)}, bf16[64,2048]{1,0:T(8,128)(2,1)S(1)}, bf16[64,2048]{1,0:T(8,128)(2,1)S(1)}, bf16[64,2048]{1,0:T(8,128)(2,1)S(1)}) custom-call(bf16[512,2048]{1,0:T(8,128)(2,1)S(1)} %bitcast.11, bf16[512,2048]{1,0:T(8,128)(2,1)S(1)} %copy-done.3, f32[128,128]{1,0:T(8,128)S(1)} %mid.1.a_ref, ...), custom_call_target="tpu_custom_call" | custom-call | flops 10000000000 | bytes 30000000 | tf_op jit(solution)/shard_map/up/pallas_call | solution.py:347
  45.4 0.8 collective-permute-start.10
  46.1 3.3 %collective-permute-start.8 = (bf16[64,2048]{1,0:T(8,128)(2,1)S(1)}, bf16[64,2048]{1,0:T(8,128)(2,1)S(1)}, u32[]{:S(2)}, u32[]{:S(2)}) collective-permute-start(bf16[64,2048]{1,0:T(8,128)(2,1)S(1)} %get-tuple-element.63), channel_id=1, source_target_pairs={{0,0},{1,5},{2,2},{3,7},{4,4},{5,1},{6,6},{7,3},{8,8},{9,13},{10,1... | collective-permute-start | bytes 786440 | tf_op jit(solution)/shard_map/ppermute | solution.py:552
  50.2 1.5 %collective-permute-start.13 = (bf16[64,2048]{1,0:T(8,128)(2,1)S(1)}, bf16[64,2048]{1,0:T(8,128)(2,1)S(1)}, u32[]{:S(2)}, u32[]{:S(2)}) collective-permute-start(bf16[64,2048]{1,0:T(8,128)(2,1)S(1)} %get-tuple-element.76), channel_id=1, source_target_pairs={{0,24},{1,29},{2,26},{3,31},{4,28},{5,25},{6,30},{7,27},{8,16},{9,... | collective-permute-start | bytes 786440 | tf_op jit(solution)/shard_map/ppermute | solution.py:552
  51.7 2.2 %collective-permute-start.15 = (bf16[64,2048]{1,0:T(8,128)(2,1)S(1)}, bf16[64,2048]{1,0:T(8,128)(2,1)S(1)}, u32[]{:S(2)}, u32[]{:S(2)}) collective-permute-start(bf16[64,2048]{1,0:T(8,128)(2,1)S(1)} %get-tuple-element.78), channel_id=1, source_target_pairs={{0,8},{1,13},{2,10},{3,15},{4,12},{5,9},{6,14},{7,11},{8,0},{9,5},... | collective-permute-start | bytes 786440 | tf_op jit(solution)/shard_map/ppermute | solution.py:552
  53.9 14.0 %qkv.3 = (f32[256,2048]{1,0:T(8,128)}, f32[256,256]{1,0:T(8,128)}, f32[256,256]{1,0:T(8,128)}) custom-call(bf16[256,256]{1,0:T(8,128)(2,1)} %get-tuple-element.64.perm_ref, bf16[64,4,2048]{2,1,0:T(4,128)(2,1)} %collective-permute-done.9.refs_0_, bf16[64,4,2048]{2,1,0:T(4,128)(2,1)} %collective-permute-done.10.refs_1_, bf16[8192,2048]{1,0:T(8,128)(2,1)} %refs_2_.3, ...), custom_call_target="tpu_custom_call" | custom-call | flops 99999997952 | bytes 300000000 | tf_op jit(solution)/shard_map/qkv/pallas_call | solution.py:240
  68.0 5.3 %collective-permute-done.13.refs_10_ = bf16[64,2048]{1,0:T(8,128)(2,1)S(1)} collective-permute-done((bf16[64,2048]{1,0:T(8,128)(2,1)S(1)}, bf16[64,2048]{1,0:T(8,128)(2,1)S(1)}, u32[]{:S(2)}, u32[]{:S(2)}) %collective-permute-start.13) | collective-permute-done | bytes 262176 | tf_op jit(solution)/shard_map/ppermute | solution.py:552
  73.9 0.9 %collective-permute-done.14.refs_11_ = bf16[64,2048]{1,0:T(8,128)(2,1)S(1)} collective-permute-done((bf16[64,2048]{1,0:T(8,128)(2,1)S(1)}, bf16[64,2048]{1,0:T(8,128)(2,1)S(1)}, u32[]{:S(2)}, u32[]{:S(2)}) %collective-permute-start.14) | collective-permute-done | bytes 262176 | tf_op jit(solution)/shard_map/ppermute | solution.py:515
  76.4 8.3 %attn.1 = bf16[64,4,2048]{2,1,0:T(4,128)(2,1)} custom-call(s32[1]{0:T(128)} %bitcast.refs_0_, s32[1,64]{1,0:T(1,128)} %get-tuple-element.43.refs_1_, f32[256,2048]{1,0:T(8,128)} %get-tuple-element.71.refs_2_, f32[256,256]{1,0:T(8,128)} %get-tuple-element.72.refs_3_, f32[256,256]{1,0:T(8,128)} %get-tuple-element.73.refs_4_, ...), custom_call_target="tpu_custom_call" | custom-call | flops 1 | bytes 1 | tf_op jit(solution)/shard_map/attn/pallas_call | solution.py:490
  (55 shorter events, 5.5 us)
Async XLA Ops:
  0.0 3.2 %collective-permute-start = (bf16[64,4,2048]{2,1,0:T(4,128)(2,1)}, bf16[64,4,2048]{2,1,0:T(4,128)(2,1)S(1)}, u32[]{:S(2)}, u32[]{:S(2)}) collective-permute-start(bf16[64,4,2048]{2,1,0:T(4,128)(2,1)} %refs_0_.1), channel_id=1, source_target_pairs={{0,1},{1,0},{2,3},{3,2},{4,5},{5,4},{6,7},{7,6},{8,9},{9,8},{10,11... | collective-permute-start | bytes 3145736 | tf_op jit(solution)/shard_map/ppermute | solution.py:515
  2.6 14.1 %copy-start.5 = (f32[256,128]{1,0:T(8,128)S(1)}, f32[256,128]{1,0:T(8,128)}, u32[]{:S(2)}) copy-start(f32[256,128]{1,0:T(8,128)} %get-tuple-element.58) | copy-start | bytes 393220
  7.2 10.9 %collective-permute-start.1 = (bf16[512,2048]{1,0:T(8,128)(2,1)}, bf16[512,2048]{1,0:T(8,128)(2,1)S(1)}, u32[]{:S(2)}, u32[]{:S(2)}) collective-permute-start(bf16[512,2048]{1,0:T(8,128)(2,1)} %bitcast.10), channel_id=1, source_target_pairs={{0,1},{1,0},{2,3},{3,2},{4,5},{5,4},{6,7},{7,6},{8,9},{9,8},{10,11... | collective-permute-start | bytes 6291464 | tf_op jit(solution)/shard_map/ppermute | solution.py:515
  7.6 13.1 %collective-permute-start.2 = (bf16[512,2048]{1,0:T(8,128)(2,1)}, bf16[512,2048]{1,0:T(8,128)(2,1)}, u32[]{:S(2)}, u32[]{:S(2)}) collective-permute-start(bf16[512,2048]{1,0:T(8,128)(2,1)} %bitcast.8), channel_id=1, source_target_pairs={{0,1},{1,0},{2,3},{3,2},{4,5},{5,4},{6,7},{7,6},{8,9},{9,8},{10,11... | collective-permute-start | bytes 6291464 | tf_op jit(solution)/shard_map/ppermute | solution.py:515
  7.7 7.7 %collective-permute-start.6 = (bf16[1040,128]{1,0:T(8,128)(2,1)}, bf16[1040,128]{1,0:T(8,128)(2,1)S(1)}, u32[]{:S(2)}, u32[]{:S(2)}) collective-permute-start(bf16[1040,128]{1,0:T(8,128)(2,1)} %get-tuple-element.47), channel_id=1, source_target_pairs={{0,0},{1,5},{2,2},{3,7},{4,4},{5,1},{6,6},{7,3},{8,8},{9,13},{10,1... | collective-permute-start | bytes 798728 | tf_op jit(solution)/shard_map/ppermute | solution.py:552
  11.1 22.7 %collective-permute-start.3 = (bf16[1040,128]{1,0:T(8,128)(2,1)}, bf16[1040,128]{1,0:T(8,128)(2,1)S(1)}, u32[]{:S(2)}, u32[]{:S(2)}) collective-permute-start(bf16[1040,128]{1,0:T(8,128)(2,1)} %get-tuple-element.50), channel_id=1, source_target_pairs={{0,16},{1,21},{2,18},{3,23},{4,20},{5,17},{6,22},{7,19},{8,24},{9,... | collective-permute-start | bytes 798728 | tf_op jit(solution)/shard_map/ppermute | solution.py:552
  13.4 23.4 %collective-permute-start.4 = (bf16[1040,128]{1,0:T(8,128)(2,1)}, bf16[1040,128]{1,0:T(8,128)(2,1)S(1)}, u32[]{:S(2)}, u32[]{:S(2)}) collective-permute-start(bf16[1040,128]{1,0:T(8,128)(2,1)} %get-tuple-element.51), channel_id=1, source_target_pairs={{0,24},{1,29},{2,26},{3,31},{4,28},{5,25},{6,30},{7,27},{8,16},{9,... | collective-permute-start | bytes 798728 | tf_op jit(solution)/shard_map/ppermute | solution.py:552
  15.4 21.4 %collective-permute-start.5 = (bf16[1040,128]{1,0:T(8,128)(2,1)}, bf16[1040,128]{1,0:T(8,128)(2,1)S(1)}, u32[]{:S(2)}, u32[]{:S(2)}) collective-permute-start(bf16[1040,128]{1,0:T(8,128)(2,1)} %get-tuple-element.52), channel_id=1, source_target_pairs={{0,8},{1,13},{2,10},{3,15},{4,12},{5,9},{6,14},{7,11},{8,0},{9,5},... | collective-permute-start | bytes 798728 | tf_op jit(solution)/shard_map/ppermute | solution.py:552
  19.5 25.9 %collective-permute-start.9 = (bf16[64,4,2048]{2,1,0:T(4,128)(2,1)}, bf16[64,4,2048]{2,1,0:T(4,128)(2,1)}, u32[]{:S(2)}, u32[]{:S(2)}) collective-permute-start(bf16[64,4,2048]{2,1,0:T(4,128)(2,1)} %refs_0_.1), channel_id=1, source_target_pairs={{0,2},{1,3},{2,0},{3,1},{4,6},{5,7},{6,4},{7,5},{8,10},{9,11},{10,... | collective-permute-start | bytes 3145736 | tf_op jit(solution)/shard_map/ppermute | solution.py:515
  20.7 16.1 %copy-start = (bf16[8,2048,64]{1,2,0:T(8,128)(2,1)S(1)}, bf16[8,2048,64]{1,2,0:T(8,128)(2,1)}, u32[]{:S(2)}) copy-start(bf16[8,2048,64]{1,2,0:T(8,128)(2,1)} %param.18) | copy-start | bytes 6291460
  36.8 7.3 %copy-start.1 = (bf16[8,64,2048]{2,1,0:T(8,128)(2,1)S(1)}, bf16[8,64,2048]{2,1,0:T(8,128)(2,1)}, u32[]{:S(2)}) copy-start(bf16[8,64,2048]{2,1,0:T(8,128)(2,1)} %param.19) | copy-start | bytes 6291460
  36.8 7.3 %copy-start.3 = (bf16[512,2048]{1,0:T(8,128)(2,1)S(1)}, bf16[512,2048]{1,0:T(8,128)(2,1)}, u32[]{:S(2)}) copy-start(bf16[512,2048]{1,0:T(8,128)(2,1)} %copy-done.2) | copy-start | bytes 6291460
  40.1 4.0 %collective-permute-start.7 = (f32[128,128]{1,0:T(8,128)S(1)}, f32[128,128]{1,0:T(8,128)S(1)}, u32[]{:S(2)}, u32[]{:S(2)}) collective-permute-start(f32[128,128]{1,0:T(8,128)S(1)} %mid.1.a_ref), channel_id=1, source_target_pairs={{0,2},{1,3},{2,0},{3,1},{4,6},{5,7},{6,4},{7,5},{8,10},{9,11},{10,... | collective-permute-start | bytes 196616 | tf_op jit(solution)/shard_map/ppermute | solution.py:515
  45.4 8.6 %collective-permute-start.10 = (bf16[64,4,2048]{2,1,0:T(4,128)(2,1)}, bf16[64,4,2048]{2,1,0:T(4,128)(2,1)}, u32[]{:S(2)}, u32[]{:S(2)}) collective-permute-start(bf16[64,4,2048]{2,1,0:T(4,128)(2,1)} %collective-permute-done.9.refs_0_), channel_id=1, source_target_pairs={{0,1},{1,0},{2,3},{3,2},{4,5},{5,4},{6,7},{7,6},{8,9},{9,8},{10,11... | collective-permute-start | bytes 3145736 | tf_op jit(solution)/shard_map/ppermute | solution.py:515
  46.1 7.8 %collective-permute-start.8 = (bf16[64,2048]{1,0:T(8,128)(2,1)S(1)}, bf16[64,2048]{1,0:T(8,128)(2,1)S(1)}, u32[]{:S(2)}, u32[]{:S(2)}) collective-permute-start(bf16[64,2048]{1,0:T(8,128)(2,1)S(1)} %get-tuple-element.63), channel_id=1, source_target_pairs={{0,0},{1,5},{2,2},{3,7},{4,4},{5,1},{6,6},{7,3},{8,8},{9,13},{10,1... | collective-permute-start | bytes 786440 | tf_op jit(solution)/shard_map/ppermute | solution.py:552
  49.4 18.4 %collective-permute-start.11 = (bf16[64,2048]{1,0:T(8,128)(2,1)S(1)}, bf16[64,2048]{1,0:T(8,128)(2,1)S(1)}, u32[]{:S(2)}, u32[]{:S(2)}) collective-permute-start(bf16[64,2048]{1,0:T(8,128)(2,1)S(1)} %get-tuple-element.66), channel_id=1, source_target_pairs={{0,16},{1,21},{2,18},{3,23},{4,20},{5,17},{6,22},{7,19},{8,24},{9,... | collective-permute-start | bytes 786440 | tf_op jit(solution)/shard_map/ppermute | solution.py:552
  50.2 23.1 %collective-permute-start.13 = (bf16[64,2048]{1,0:T(8,128)(2,1)S(1)}, bf16[64,2048]{1,0:T(8,128)(2,1)S(1)}, u32[]{:S(2)}, u32[]{:S(2)}) collective-permute-start(bf16[64,2048]{1,0:T(8,128)(2,1)S(1)} %get-tuple-element.76), channel_id=1, source_target_pairs={{0,24},{1,29},{2,26},{3,31},{4,28},{5,25},{6,30},{7,27},{8,16},{9,... | collective-permute-start | bytes 786440 | tf_op jit(solution)/shard_map/ppermute | solution.py:552
  51.7 21.6 %collective-permute-start.15 = (bf16[64,2048]{1,0:T(8,128)(2,1)S(1)}, bf16[64,2048]{1,0:T(8,128)(2,1)S(1)}, u32[]{:S(2)}, u32[]{:S(2)}) collective-permute-start(bf16[64,2048]{1,0:T(8,128)(2,1)S(1)} %get-tuple-element.78), channel_id=1, source_target_pairs={{0,8},{1,13},{2,10},{3,15},{4,12},{5,9},{6,14},{7,11},{8,0},{9,5},... | collective-permute-start | bytes 786440 | tf_op jit(solution)/shard_map/ppermute | solution.py:552
  53.9 19.9 %copy-start.6 = (bf16[64,2048]{1,0:T(8,128)(2,1)}, bf16[64,2048]{1,0:T(8,128)(2,1)S(1)}, u32[]{:S(2)}) copy-start(bf16[64,2048]{1,0:T(8,128)(2,1)S(1)} %collective-permute-done.8.refs_14_) | copy-start | bytes 786436
  67.9 8.4 %copy-start.7 = (bf16[64,2048]{1,0:T(8,128)(2,1)}, bf16[64,2048]{1,0:T(8,128)(2,1)S(1)}, u32[]{:S(2)}) copy-start(bf16[64,2048]{1,0:T(8,128)(2,1)S(1)} %collective-permute-done.11.refs_8_) | copy-start | bytes 786436
  67.9 6.0 %collective-permute-start.12 = (bf16[64,2048]{1,0:T(8,128)(2,1)S(1)}, bf16[64,2048]{1,0:T(8,128)(2,1)S(1)}, u32[]{:S(2)}, u32[]{:S(2)}) collective-permute-start(bf16[64,2048]{1,0:T(8,128)(2,1)S(1)} %collective-permute-done.11.refs_8_), channel_id=1, source_target_pairs={{0,1},{1,0},{2,3},{3,2},{4,5},{5,4},{6,7},{7,6},{8,9},{9,8},{10,11... | collective-permute-start | bytes 786440 | tf_op jit(solution)/shard_map/ppermute | solution.py:515
  73.3 1.5 %collective-permute-start.14 = (bf16[64,2048]{1,0:T(8,128)(2,1)S(1)}, bf16[64,2048]{1,0:T(8,128)(2,1)S(1)}, u32[]{:S(2)}, u32[]{:S(2)}) collective-permute-start(bf16[64,2048]{1,0:T(8,128)(2,1)S(1)} %collective-permute-done.13.refs_10_), channel_id=1, source_target_pairs={{0,1},{1,0},{2,3},{3,2},{4,5},{5,4},{6,7},{7,6},{8,9},{9,8},{10,11... | collective-permute-start | bytes 786440 | tf_op jit(solution)/shard_map/ppermute | solution.py:515
  73.3 1.9 %collective-permute-start.16 = (bf16[64,2048]{1,0:T(8,128)(2,1)S(1)}, bf16[64,2048]{1,0:T(8,128)(2,1)S(1)}, u32[]{:S(2)}, u32[]{:S(2)}) collective-permute-start(bf16[64,2048]{1,0:T(8,128)(2,1)S(1)} %collective-permute-done.15.refs_12_), channel_id=1, source_target_pairs={{0,1},{1,0},{2,3},{3,2},{4,5},{5,4},{6,7},{7,6},{8,9},{9,8},{10,11... | collective-permute-start | bytes 786440 | tf_op jit(solution)/shard_map/ppermute | solution.py:515
  73.8 1.8 %collective-permute-start.17 = (bf16[64,2048]{1,0:T(8,128)(2,1)S(1)}, bf16[64,2048]{1,0:T(8,128)(2,1)S(1)}, u32[]{:S(2)}, u32[]{:S(2)}) collective-permute-start(bf16[64,2048]{1,0:T(8,128)(2,1)S(1)} %collective-permute-done.8.refs_14_), channel_id=1, source_target_pairs={{0,1},{1,0},{2,3},{3,2},{4,5},{5,4},{6,7},{7,6},{8,9},{9,8},{10,11... | collective-permute-start | bytes 786440 | tf_op jit(solution)/shard_map/ppermute | solution.py:515
  (8 other events, 14.1 us)
